TPU v7x, 128 devices: a whole 4x4x4 slice. The times are simulated.
128 devices in a mesh: rows: 32 (over x, y, z_hi), cols: 4 (over z_lo, core).
Axes of the slice: x: 4, y: 4, z: 4 (z_hi: 2, z_lo: 2; z = z_hi * 2 + z_lo), core: 2. Of those that a mesh axis runs over, the one named last changes fastest.
Arguments:
- counts: int32 [8192, 65536], P('rows', 'cols'), may hold values from 0 to 11
- row_marg: int32 [8192], P('rows'), may hold values from 16384 to 131071
- ctx_marg: int32 [65536], P('cols'), may hold values from 1 to 113554
- discount: int32 [65536], P('cols'), may hold values from 1 to 5
- probes: bfloat16 [65536, 256], P('cols'), may hold values from -0.0234375 to 0.0234375
Outputs:
- y_proj: bfloat16 [8192, 256], P('rows')
- z_proj: float32 [4, 16384, 256], P('cols', 'rows')
All inputs are finite; a program needn't handle non-finite values.
Results may differ from a plain program's by a relative error of at most 0.005.
Values may be sent and summed in bfloat16 or wider, within the bound.
No kernel may reach another device: no remote copies, remote signals or barrier semaphores. Data moves between devices by JAX's collectives and lax.ppermute only.
A program may use at most 128 MiB of HBM per device.

v0:
```python
import jax
import jax.numpy as jnp
from jax import lax
from jax.sharding import PartitionSpec as P


def build_tile(counts, log_row, ctx_term, log_total, shrink):
    excess = counts.astype(jnp.float32) - shrink[None, :]
    raw_pmi = jnp.log(jnp.maximum(excess, 0.25)) + log_total - log_row[:, None] - ctx_term[None, :]
    return jnp.where(excess > 0.0, jnp.maximum(raw_pmi, 0.0), 0.0).astype(jnp.bfloat16)


def local(counts, row_marg, ctx_marg, discount, probes):
    shrink = discount.astype(jnp.float32) * 0.25
    log_ctx = jnp.log(ctx_marg.astype(jnp.float32))
    ctx_term = 0.75 * log_ctx
    ctx_total = lax.psum(jnp.sum(jnp.exp(ctx_term)), "cols")
    log_total = jnp.log(ctx_total)
    log_row = jnp.log(row_marg.astype(jnp.float32))
    a_tile = build_tile(counts, log_row, ctx_term, log_total, shrink)
    y_local = jnp.dot(a_tile, probes, preferred_element_type=jnp.float32)
    y_proj = lax.psum(y_local, "cols").astype(jnp.bfloat16)
    row_devices = lax.axis_size("rows")
    block_len = a_tile.shape[0]
    factor = (block_len * row_devices) ** (-0.5)
    z_local = lax.psum_scatter(
        lax.dot_general(
            a_tile, y_proj, (((0,), (0,)), ((), ())), preferred_element_type=jnp.float32
        ),
        "rows",
        scatter_dimension=0,
        tiled=True,
    )
    return (y_proj, (z_local * factor)[None])


def solution(mesh):
    in_specs = (P("rows", "cols"), P("rows"), P("cols"), P("cols"), P("cols", None))
    out_specs = (P("rows", None), P("cols", "rows", None))
    return jax.shard_map(local, mesh=mesh, in_specs=in_specs, out_specs=out_specs, check_vma=False)
```

profile of v0, /device:TPU:24, one launch (start us, length us, event | category | flops | bytes accessed | tf_op | source)
XLA Modules:
  0.0 432.7 jit_solution(2429820084834865784)
XLA Ops:
  7.2 0.0 reduce-scatter.2.cloned.1.call-start
  7.2 0.7 convert_log_fusion
  7.9 0.9 convert_multiply_fusion
  8.7 1.5 exponential_reduce_fusion
  10.2 7.9 %psum.14 = f32[]{:T(128)} all-reduce(f32[]{:T(128)} %get-tuple-element.2), channel_id=1, replica_groups=mesh['rows'=32,'cols'=4] {'cols'}, use_global_device_ids=true, to_apply=%region_1.0 | all-reduce | flops 1 | bytes 8 | tf_op jit(solution)/shard_map/psum | solution.py:17
  18.8 0.0 slice-start
  18.8 0.0 slice-start.1
  18.9 10.2 %select_convert_fusion = bf16[256,16384]{1,0:T(8,128)(2,1)S(1)} fusion(s32[256,16384]{1,0:T(8,128)} %param.5, f32[16384]{0:T(1024)S(1)} %get-tuple-element.3, f32[256]{0:T(256)S(1)} %convert_log_fusion, f32[]{:T(128)S(6)} %log.14, f32[16384]{0:T(1024)S(1)} %convert_multiply_fusion), kind=kLoop, calls=%fused_computation | loop fusion | flops 41943040 | bytes 25297924 | tf_op jit(solution)/shard_map/convert_element_type | solution.py:10
  29.0 0.0 copy-start
  29.0 3.2 copy-done
  32.2 0.0 slice-done
  32.2 0.0 slice-done.1
  32.3 2.3 fusion
  34.6 13.5 %all-reduce.1 = bf16[256,256]{1,0:T(8,128)(2,1)S(1)} all-reduce(f32[256,256]{1,0:T(8,128)S(1)} %fusion), channel_id=1, replica_groups=mesh['rows'=32,'cols'=4] {'cols'}, use_global_device_ids=true, to_apply=%region_2.3 | all-reduce | flops 65536 | bytes 393216 | tf_op jit(solution)/shard_map/psum | solution.py:22
  48.1 0.0 copy-start.1
  48.1 11.6 %fusion.1 = f32[16384,256]{1,0:T(8,128)} fusion(bf16[256,16384]{1,0:T(8,128)(2,1)} %copy-done, bf16[256,256]{1,0:T(8,128)(2,1)S(1)} %all-reduce.1), kind=kOutput, calls=%fused_computation.8 | convolution fusion | flops 2147483648 | bytes 25296896 | tf_op jit(solution)/shard_map/dot_general | solution.py:27
  59.7 0.0 reduce-scatter.2.cloned.1.call-update
  59.7 0.0 copy-done.1
  59.7 364.3 %reduce-scatter.2.cloned.1.call-done = f32[512,256]{1,0:T(8,128)} async-done(((f32[16384,256]{1,0:T(8,128)}), f32[512,256]{1,0:T(8,128)}) %reduce-scatter.2.cloned.1.call-update) | async-done | bytes 524304 | tf_op jit(solution)/shard_map/reduce_scatter | solution.py:26
  424.0 1.9 multiply_bitcast_fusion
  (1 shorter events, 0.0 us)
Async XLA Ops:
  7.2 416.8 %reduce-scatter.2.cloned.1.call-start = ((), (), s32[]{:S(2)}) async-start(), calls=%async_computation.1 | async-start | bytes 17301504 | tf_op jit(solution)/shard_map/reduce_scatter | solution.py:26
  18.8 13.4 %slice-start = ((s8[8388608]{0:T(1024)(128)(4,1)}), s8[4194304]{0:T(1024)(128)(4,1)S(1)}, s32[]{:S(2)}) async-start(s8[8388608]{0:T(1024)(128)(4,1)} %bitcast.6), calls=%async_computation.2 | async-start | bytes 8388608
  18.8 13.4 %slice-start.1 = ((s8[8388608]{0:T(1024)(128)(4,1)}), s8[4194304]{0:T(1024)(128)(4,1)S(1)}, s32[]{:S(2)}) async-start(s8[8388608]{0:T(1024)(128)(4,1)} %bitcast.6), calls=%async_computation.3 | async-start | bytes 8388608
  29.0 3.2 copy-start
  48.1 11.6 %copy-start.1 = (bf16[256,256]{1,0:T(8,128)(2,1)}, bf16[256,256]{1,0:T(8,128)(2,1)S(1)}, u32[]{:S(2)}) copy-start(bf16[256,256]{1,0:T(8,128)(2,1)S(1)} %all-reduce.1) | copy-start | bytes 393220
Sparse Core Ops, SparseCore 0:
  59.8 364.1 reduce-scatter.1
where the time goes:
time: 434 us; the launch traced here: 433 us
  waiting for transfers between devices  364 us (84%)
  blocking collectives  21.4 us (5%)
  other arithmetic  15 us (3%)
  between operations  14.8 us (3%)
  matrix products  13.9 us (3%)
    reduce_scatter x1, waiting for transfers between devices, local(): lax.psum_scatter(lax.dot_general(a_tile, y_proj, (((0,), (0,)), ((), ()))...  364 us
    psum x1, blocking collectives, local(): y_proj = lax.psum(y_local, 'cols').astype(jnp.bfloat16)  13.5 us
    dot_general x1, matrix products, local(): lax.dot_general(a_tile, y_proj, (((0,), (0,)), ((), ())), preferred_eleme...  11.6 us
    convert_element_type x1, other arithmetic, build_tile(): jnp.where(excess > 0.0, jnp.maximum(raw_pmi, 0.0), 0.0).astype(jnp.bfloat16)  10.2 us
  transfers between devices with their start and end apart: 1, of which 1 were waited for; matrix products, arithmetic and copies ran while one was open for 0% of the time, Pallas kernels for 0%

commit v1 on v0

v1 whole, which is shorter than its diff:
```python
import functools

import jax
import jax.numpy as jnp
import numpy as np
from jax import lax
from jax.experimental import pallas as pl
from jax.experimental.pallas import tpu as pltpu

from jax.sharding import PartitionSpec as P

AXES = ("rows", "cols")
W = 256
PACK = 8
F32, BF16 = jnp.float32, jnp.bfloat16


def device_id(x, y, zh, zl, core):
    return (x * 8 + y * 2 + zh) * 4 + zl * 2 + core


def flip(kind, a):
    return a ^ 1 if kind == 0 else 3 - a


def all_devices():
    for x in range(4):
        for y in range(4):
            for zh in range(2):
                for zl in range(2):
                    for core in range(2):
                        yield x, y, zh, zl, core


def ring_perm(kind, second_axis):
    pairs = []
    for x, y, zh, zl, core in all_devices():
        if (core == 0) != second_axis:
            to = device_id(flip(kind, x), y, zh, zl, core)
        else:
            to = device_id(x, flip(kind, y), zh, zl, core)
        pairs.append((device_id(x, y, zh, zl, core), to))
    return pairs


ZH_PERM = [(device_id(*d), device_id(d[0], d[1], 1 - d[2], d[3], d[4])) for d in all_devices()]
ZL_PERM = [(device_id(*d), device_id(d[0], d[1], d[2], 1 - d[3], d[4])) for d in all_devices()]
CORE_PERM = [(device_id(*d), device_id(d[0], d[1], d[2], d[3], 1 - d[4])) for d in all_devices()]


def block_order():
    table = np.zeros((128, 4, 16), np.int32)
    for d in all_devices():
        x, y, zh, zl, core = d
        u, v = (x, y) if core == 0 else (y, x)
        for g in range(2):
            near, far = g, 1 - g
            vs = [v, flip(far, v), flip(near, v), flip(far, flip(near, v))]
            for part, start in enumerate((u, flip(near, u))):
                us = [start, flip(far, start)]
                blocks = []
                for i in us:
                    for j in vs:
                        for k in (zh, 1 - zh):
                            own = (i * 8 + j * 2 + k) if core == 0 else (j * 8 + i * 2 + k)
                            blocks.append(own * 2 + g)
                table[device_id(*d), 2 * g + part] = blocks
    return table.reshape(128, 64)


ORDER = block_order()


def permute(a, perm):
    return lax.ppermute(a, AXES, perm)


def params(mib):
    return pltpu.CompilerParams(vmem_limit_bytes=mib << 20)


def context_kernel(marg_ref, disc_ref, power_ref, shrink_ref, total_ref):
    power = jnp.exp(0.75 * jnp.log(marg_ref[...].astype(F32)))
    power_ref[...] = 1.0 / power
    shrink_ref[...] = disc_ref[...].astype(F32) * 0.25
    total_ref[...] = jnp.full((8, 128), jnp.sum(power), F32)


def context(ctx_marg, discount):
    shape = jax.ShapeDtypeStruct((64, W), F32)
    return pl.pallas_call(
        context_kernel,
        out_shape=(shape, shape, jax.ShapeDtypeStruct((8, 128), F32)),
        cost_estimate=pl.CostEstimate(flops=1 << 16, bytes_accessed=1 << 18, transcendentals=1 << 15),
    )(ctx_marg.reshape(64, W), discount.reshape(64, W))


def send_kernel(order_ref, *refs):
    for k in range(PACK):
        refs[PACK][k] = refs[k][...].astype(F32).astype(BF16)


def counts_to_send(order, counts, first):
    rows = counts.shape[0]
    specs = [
        pl.BlockSpec((rows, W), functools.partial(lambda k, i, o: (0, o[first + i * PACK + k]), k))
        for k in range(PACK)
    ]
    return pl.pallas_call(
        send_kernel,
        grid_spec=pltpu.PrefetchScalarGridSpec(
            num_scalar_prefetch=1,
            grid=(16 // PACK,),
            in_specs=specs,
            out_specs=pl.BlockSpec((PACK, rows, W), lambda i, o: (i, 0, 0)),
        ),
        out_shape=jax.ShapeDtypeStruct((16, rows, W), BF16),
        compiler_params=params(40),
        cost_estimate=pl.CostEstimate(flops=1 << 20, bytes_accessed=6 << 20, transcendentals=0),
    )(order, *([counts] * PACK))


def tile_rows(counts, shrink, scale, inv_row):
    excess = counts.astype(F32) - shrink
    return jnp.log(jnp.maximum(excess * scale * inv_row, 1.0)).astype(BF16)


def forward_kernel(order_ref, total_ref, row_ref, power_ref, shrink_ref, *refs):
    counts, probes = refs[:PACK], refs[PACK:2 * PACK]
    tile_ref, y_ref, acc_ref, work_ref = refs[2 * PACK:]
    step = pl.program_id(0)

    @pl.when(step == 0)
    def _():
        acc_ref[...] = jnp.zeros_like(acc_ref)

    total = total_ref[0, 0]
    rows = row_ref.shape[0]
    part = None
    for k in range(PACK):
        block = order_ref[step * PACK + k]
        shrink = shrink_ref[pl.ds(block, 1), :]
        scale = power_ref[pl.ds(block, 1), :] * total
        for r in range(0, rows, 32):
            inv_row = row_ref[r:r + 32, :]
            work_ref[k, r:r + 32, :] = tile_rows(counts[k][r:r + 32, :], shrink, scale, inv_row)
        term = jnp.dot(work_ref[k], probes[k][...], preferred_element_type=F32)
        part = term if part is None else part + term
    acc_ref[...] += part

    @pl.when((step & 3) < 2)
    def _():
        tile_ref[...] = work_ref[...]

    @pl.when(step == pl.num_programs(0) - 1)
    def _():
        y_ref[...] = jnp.transpose(acc_ref[...])


def forward(order, total, inv_row, power, shrink, counts, probes):
    rows, width = counts.shape[0], probes.shape[1]
    steps = 64 // PACK
    count_specs = [
        pl.BlockSpec((rows, W), functools.partial(lambda k, i, o: (0, o[i * PACK + k]), k)) for k in range(PACK)
    ]
    probe_specs = [
        pl.BlockSpec((W, width), functools.partial(lambda k, i, o: (o[i * PACK + k], 0), k)) for k in range(PACK)
    ]
    whole = lambda shape: pl.BlockSpec(shape, lambda i, o: (0, 0))
    return pl.pallas_call(
        forward_kernel,
        grid_spec=pltpu.PrefetchScalarGridSpec(
            num_scalar_prefetch=1,
            grid=(steps,),
            in_specs=[
                pl.BlockSpec(memory_space=pltpu.SMEM),
                whole((rows, 1)),
                whole((64, W)),
                whole((64, W)),
                *count_specs,
                *probe_specs,
            ],
            out_specs=[
                pl.BlockSpec((PACK, rows, W), lambda i, o: (2 * (i // 4) + jnp.minimum(i % 4, 1), 0, 0)),
                whole((width, rows)),
            ],
            scratch_shapes=[pltpu.VMEM((rows, width), F32), pltpu.VMEM((PACK, rows, W), BF16)],
        ),
        out_shape=(
            jax.ShapeDtypeStruct((32, rows, W), BF16),
            jax.ShapeDtypeStruct((width, rows), F32),
        ),
        compiler_params=params(48),
        cost_estimate=pl.CostEstimate(flops=1 << 31, bytes_accessed=28 << 20, transcendentals=1 << 22),
    )(order, total, inv_row, power, shrink, *([counts] * PACK), *([probes] * PACK))


def back_kernel(base, order_ref, total_ref, row_ref, power_ref, shrink_ref, y_own_ref, y_other_ref, tile_ref, count_ref, z_ref, work_ref):
    step = pl.program_id(0)
    total = total_ref[0, 0]
    n, rows, _ = tile_ref.shape
    for k in range(n):
        block = order_ref[base + step * n + k]
        shrink = shrink_ref[pl.ds(block, 1), :]
        scale = power_ref[pl.ds(block, 1), :] * total
        for r in range(0, rows, 32):
            inv_row = row_ref[r:r + 32, :]
            work_ref[k, r:r + 32, :] = tile_rows(count_ref[k, r:r + 32, :], shrink, scale, inv_row)
        out = jnp.dot(y_own_ref[...], tile_ref[k], preferred_element_type=F32)
        out = out + jnp.dot(y_other_ref[...], work_ref[k], preferred_element_type=F32)
        z_ref[k] = out.astype(z_ref.dtype)


def back(order, total, inv_row, power, shrink, y_own, y_other, tile, received, group, half, dtype):
    n = 4
    rows, width = tile.shape[1], y_own.shape[0]
    tile_at = (group * 16 + half * 8) // n
    count_at = half * 8 // n
    whole = lambda shape: pl.BlockSpec(shape, lambda i, o: (0, 0))
    return pl.pallas_call(
        functools.partial(back_kernel, group * 32 + half * 8),
        grid_spec=pltpu.PrefetchScalarGridSpec(
            num_scalar_prefetch=1,
            grid=(8 // n,),
            in_specs=[
                pl.BlockSpec(memory_space=pltpu.SMEM),
                whole((rows, 1)),
                whole((64, W)),
                whole((64, W)),
                whole((width, rows)),
                whole((width, rows)),
                pl.BlockSpec((n, rows, W), lambda i, o: (tile_at + i, 0, 0)),
                pl.BlockSpec((n, rows, W), lambda i, o: (count_at + i, 0, 0)),
            ],
            out_specs=pl.BlockSpec((n, width, W), lambda i, o: (i, 0, 0)),
            scratch_shapes=[pltpu.VMEM((n, rows, W), BF16)],
        ),
        out_shape=jax.ShapeDtypeStruct((8, width, W), dtype),
        compiler_params=params(32),
        cost_estimate=pl.CostEstimate(flops=1 << 29, bytes_accessed=4 << 20, transcendentals=1 << 19),
    )(order, total, inv_row, power, shrink, y_own, y_other, tile, received)


def local(counts, row_marg, ctx_marg, discount, probes):
    me = lax.axis_index("rows") * 4 + lax.axis_index("cols")
    order = lax.dynamic_index_in_dim(jnp.asarray(ORDER), me, 0, keepdims=False)
    first = [ring_perm(g, False) for g in range(2)]
    second = [ring_perm(1 - g, False) for g in range(2)]
    third = [ring_perm(g, True) for g in range(2)]
    fourth = [ring_perm(1 - g, True) for g in range(2)]

    power, shrink, total = context(ctx_marg, discount)
    total = total + permute(total, CORE_PERM)
    total = total + permute(total, ZL_PERM)
    inv_row = (1.0 / row_marg.astype(F32))[:, None]

    received = [permute(counts_to_send(order, counts, 32 * g + 16), first[g]) for g in range(2)]
    inv_other = [permute(inv_row, first[g]) for g in range(2)]

    tile, y_part = forward(order, total, inv_row, power, shrink, counts, probes)
    y_part = y_part + permute(y_part, CORE_PERM)
    y_part = y_part + permute(y_part, ZL_PERM)
    y_own = y_part.astype(BF16)
    y_other = [permute(y_own, first[g]) for g in range(2)]

    def run(g, half, dtype):
        return back(order, total, inv_other[g], power, shrink, y_own, y_other[g], tile, received[g], g, half, dtype)

    out = []
    sends = [run(g, 1, BF16) for g in range(2)]
    for g in range(2):
        r2 = permute(sends[g], second[g]).astype(F32)
        z = run(g, 0, F32)
        r3 = permute((z[4:8] + r2[4:8]).astype(BF16), third[g]).astype(F32)
        r4 = permute((z[2:4] + r2[2:4] + r3[2:4]).astype(BF16), fourth[g]).astype(F32)
        r5 = permute((z[1] + r2[1] + r3[1] + r4[1]).astype(BF16), ZH_PERM).astype(F32)
        out.append(jnp.transpose(z[0] + r2[0] + r3[0] + r4[0] + r5))
    row_devices = lax.axis_size("rows")
    factor = (counts.shape[0] * row_devices) ** (-0.5)
    z_proj = jnp.concatenate(out, axis=0) * factor
    return (jnp.transpose(y_own), z_proj[None])


def solution(mesh):
    in_specs = (P("rows", "cols"), P("rows"), P("cols"), P("cols"), P("cols", None))
    out_specs = (P("rows", None), P("cols", "rows", None))
    return jax.shard_map(local, mesh=mesh, in_specs=in_specs, out_specs=out_specs, check_vma=False)
```

time: 434 us -> 128 us (0.29)
  waiting for transfers between devices: 364 us -> 52.7 us
  Pallas kernels: 0 us -> 33.5 us
  starting transfers between devices: 0.04 us -> 26.1 us
  blocking collectives: 21.4 us -> 0 us
  between operations: 14.8 us -> 0.89 us
  matrix products: 13.9 us -> 0 us
  other arithmetic: 15 us -> 8.71 us
    reduce_scatter x1 -> x0, waiting for transfers between devices: 364 us -> none  [local(): lax.psum_scatter(lax.dot_general(a_tile, y_proj, (((0,), (0,)), ((), ()))...]
    ppermute x0 -> x18, waiting for transfers between devices: none -> 52.7 us  [permute(): return lax.ppermute(a, AXES, perm)]
    pallas_call x0 -> x8, Pallas kernels: none -> 33.5 us  [the longest x1 13.6 us: forward(): pl.pallas_call(forward_kernel, grid_spec=pltpu.PrefetchScalarGridSpec(num...]
    ppermute x0 -> x18, starting transfers between devices: none -> 26.1 us  [permute(): return lax.ppermute(a, AXES, perm)]
    psum x2 -> x0, blocking collectives: 21.4 us -> none  [the longest x1 13.5 us: local(): y_proj = lax.psum(y_local, 'cols').astype(jnp.bfloat16)]
    dot_general x2 -> x0, matrix products: 13.9 us -> none  [the longest x1 11.6 us: local(): lax.dot_general(a_tile, y_proj, (((0,), (0,)), ((), ())), preferred_eleme...]
    convert_element_type x1 -> x13, other arithmetic: 10.2 us -> 5.79 us  [the longest x2 2.13 us: local(): (z[1] + r2[1] + r3[1] + r4[1]).astype(BF16)]
  transfers between devices with their start and end apart: 1 -> 18, of which waited for: 1 -> 11; matrix products, arithmetic and copies ran while one was open for 0% -> 8% of each run, Pallas kernels for 0% -> 23%
where the time goes in v1:
time: 128 us
  waiting for transfers between devices  52.7 us (41%)
  Pallas kernels  33.5 us (26%)
  starting transfers between devices  26.1 us (20%)
  other arithmetic  8.71 us (7%)
  local copies, waits for them, and re-layouts  5.78 us (5%)
    ppermute x18, waiting for transfers between devices, permute(): return lax.ppermute(a, AXES, perm)  52.7 us
    ppermute x18, starting transfers between devices, permute(): return lax.ppermute(a, AXES, perm)  26.1 us
    pallas_call x1, Pallas kernels, forward(): pl.pallas_call(forward_kernel, grid_spec=pltpu.PrefetchScalarGridSpec(num...  13.6 us
    pallas_call x4, Pallas kernels, back(): pl.pallas_call(functools.partial(back_kernel, group * 32 + half * 8), gri...  10.5 us
    pallas_call x2, Pallas kernels, counts_to_send(): pl.pallas_call(send_kernel, grid_spec=pltpu.PrefetchScalarGridSpec(num_sc...  7.72 us
    unnamed x26, local copies, waits for them, and re-layouts  3.64 us
  transfers between devices with their start and end apart: 18, of which 11 were waited for; matrix products, arithmetic and copies ran while one was open for 8% of the time, Pallas kernels for 23%

profile of v1, /device:TPU:24, one launch (start us, length us, event | category | flops | bytes accessed | tf_op | source)
XLA Modules:
  0.0 127.6 jit_solution(7424563933322035438)
XLA Ops:
  1.3 3.9 %shard_map.79 = bf16[16,256,256]{2,1,0:T(8,128)(2,1)} custom-call(s32[64]{0:T(128)S(1)} %dynamic-slice_bitcast_fusion.order_ref, s32[256,16384]{1,0:T(8,128)} %refs_7_.5, s32[256,16384]{1,0:T(8,128)} %refs_7_.5, s32[256,16384]{1,0:T(8,128)} %refs_7_.5, s32[256,16384]{1,0:T(8,128)} %refs_7_.5, s32[256,16384]{1,0:T(8,128)} %refs_7_.5, s32[256,16384]{1,0:T(8,128)} %refs_7_.5, ...), custom_call_target="tpu_custom_call" | custom-call | flops 1048576 | bytes 6291456 | tf_op jit(solution)/shard_map/pallas_call | solution.py:109
  5.2 1.6 %collective-permute-start.6 = (bf16[16,256,256]{2,1,0:T(8,128)(2,1)}, bf16[16,256,256]{2,1,0:T(8,128)(2,1)S(1)}, u32[]{:S(2)}, u32[]{:S(2)}) collective-permute-start(bf16[16,256,256]{2,1,0:T(8,128)(2,1)} %shard_map.79), channel_id=1, source_target_pairs={{0,32},{1,9},{2,34},{3,11},{4,36},{5,13},{6,38},{7,15},{8,40},{9,1... | collective-permute-start | bytes 6291464 | tf_op jit(solution)/shard_map/ppermute | solution.py:75
  6.8 3.8 %shard_map.82 = bf16[16,256,256]{2,1,0:T(8,128)(2,1)} custom-call(s32[64]{0:T(128)S(1)} %dynamic-slice_bitcast_fusion.order_ref, s32[256,16384]{1,0:T(8,128)} %refs_7_.5, s32[256,16384]{1,0:T(8,128)} %refs_7_.5, s32[256,16384]{1,0:T(8,128)} %refs_7_.5, s32[256,16384]{1,0:T(8,128)} %refs_7_.5, s32[256,16384]{1,0:T(8,128)} %refs_7_.5, s32[256,16384]{1,0:T(8,128)} %refs_7_.5, ...), custom_call_target="tpu_custom_call" | custom-call | flops 1048576 | bytes 6291456 | tf_op jit(solution)/shard_map/pallas_call | solution.py:109
  10.6 2.1 %collective-permute-start.13 = (bf16[16,256,256]{2,1,0:T(8,128)(2,1)}, bf16[16,256,256]{2,1,0:T(8,128)(2,1)}, u32[]{:S(2)}, u32[]{:S(2)}) collective-permute-start(bf16[16,256,256]{2,1,0:T(8,128)(2,1)} %shard_map.82), channel_id=1, source_target_pairs={{0,96},{1,25},{2,98},{3,27},{4,100},{5,29},{6,102},{7,31},{8,104},... | collective-permute-start | bytes 6291464 | tf_op jit(solution)/shard_map/ppermute | solution.py:75
  14.0 1.6 %shard_map.77 = (f32[64,256]{1,0:T(8,128)}, f32[64,256]{1,0:T(8,128)}, f32[8,128]{1,0:T(8,128)}) custom-call(s32[64,256]{1,0:T(8,128)} %reshape.53.marg_ref, s32[64,256]{1,0:T(8,128)} %reshape.54.disc_ref), custom_call_target="tpu_custom_call" | custom-call | flops 65536 | bytes 262144 | tf_op jit(solution)/shard_map/pallas_call | solution.py:91
  17.7 1.9 %collective-permute-start.1 = (f32[8,128]{1,0:T(8,128)S(1)}, f32[8,128]{1,0:T(8,128)S(1)}, u32[]{:S(2)}, u32[]{:S(2)}) collective-permute-start(f32[8,128]{1,0:T(8,128)S(1)} %add.97), channel_id=1, source_target_pairs={{0,2},{1,3},{2,0},{3,1},{4,6},{5,7},{6,4},{7,5},{8,10},{9,11},{10,... | collective-permute-start | bytes 12296 | tf_op jit(solution)/shard_map/ppermute | solution.py:75
  19.8 1.5 %collective-permute-done.1 = f32[8,128]{1,0:T(8,128)S(1)} collective-permute-done((f32[8,128]{1,0:T(8,128)S(1)}, f32[8,128]{1,0:T(8,128)S(1)}, u32[]{:S(2)}, u32[]{:S(2)}) %collective-permute-start.1) | collective-permute-done | bytes 4128 | tf_op jit(solution)/shard_map/ppermute | solution.py:75
  23.0 13.6 %shard_map.78 = (bf16[32,256,256]{2,1,0:T(8,128)(2,1)S(1)}, f32[256,256]{1,0:T(8,128)S(1)}) custom-call(s32[64]{0:T(128)S(1)} %dynamic-slice_bitcast_fusion.order_ref, f32[8,128]{1,0:T(8,128)S(1)} %add.98.total_ref, f32[256,1]{1,0:T(8,128)S(1)} %copy.10.row_ref, f32[64,256]{1,0:T(8,128)S(1)} %copy-done.1, f32[64,256]{1,0:T(8,128)S(1)} %copy-done.3, ...), custom_call_target="tpu_custom_call" | custom-call | flops 2147483648 | bytes 29360128 | tf_op jit(solution)/shard_map/pallas_call | solution.py:170
  36.7 1.5 %collective-permute-done.2 = f32[256,256]{1,0:T(8,128)S(1)} collective-permute-done((f32[256,256]{1,0:T(8,128)S(1)}, f32[256,256]{1,0:T(8,128)S(1)}, u32[]{:S(2)}, u32[]{:S(2)}) %collective-permute-start.2) | collective-permute-done | bytes 262176 | tf_op jit(solution)/shard_map/ppermute | solution.py:75
  38.3 2.0 %collective-permute-start.3 = (f32[256,256]{1,0:T(8,128)S(1)}, f32[256,256]{1,0:T(8,128)S(1)}, u32[]{:S(2)}, u32[]{:S(2)}) collective-permute-start(f32[256,256]{1,0:T(8,128)S(1)} %add.99), channel_id=1, source_target_pairs={{0,2},{1,3},{2,0},{3,1},{4,6},{5,7},{6,4},{7,5},{8,10},{9,11},{10,... | collective-permute-start | bytes 786440 | tf_op jit(solution)/shard_map/ppermute | solution.py:75
  40.3 6.6 %collective-permute-done.3 = f32[256,256]{1,0:T(8,128)S(1)} collective-permute-done((f32[256,256]{1,0:T(8,128)S(1)}, f32[256,256]{1,0:T(8,128)S(1)}, u32[]{:S(2)}, u32[]{:S(2)}) %collective-permute-start.3) | collective-permute-done | bytes 262176 | tf_op jit(solution)/shard_map/ppermute | solution.py:75
  49.0 4.3 %collective-permute-done.4.row_ref = f32[256,1]{1,0:T(8,128)S(1)} collective-permute-done((f32[256,1]{1,0:T(8,128)S(1)}, f32[256,1]{1,0:T(8,128)S(1)}, u32[]{:S(2)}, u32[]{:S(2)}) %collective-permute-start.4) | collective-permute-done | bytes 1056 | tf_op jit(solution)/shard_map/ppermute | solution.py:75
  53.4 2.4 %shard_map.81 = bf16[8,256,256]{2,1,0:T(8,128)(2,1)S(1)} custom-call(s32[64]{0:T(128)S(1)} %dynamic-slice_bitcast_fusion.order_ref, f32[8,128]{1,0:T(8,128)S(1)} %add.98.total_ref, f32[256,1]{1,0:T(8,128)S(1)} %collective-permute-done.4.row_ref, f32[64,256]{1,0:T(8,128)S(1)} %copy-done.2, f32[64,256]{1,0:T(8,128)S(1)} %copy-done.4, ...), custom_call_target="tpu_custom_call" | custom-call | flops 536870912 | bytes 4194304 | tf_op jit(solution)/shard_map/pallas_call | solution.py:220
  57.0 2.1 %collective-permute-start.12 = (bf16[256,256]{1,0:T(8,128)(2,1)S(1)}, bf16[256,256]{1,0:T(8,128)(2,1)S(1)}, u32[]{:S(2)}, u32[]{:S(2)}) collective-permute-start(bf16[256,256]{1,0:T(8,128)(2,1)S(1)} %add_convert_fusion.y_own_ref), channel_id=1, source_target_pairs={{0,96},{1,25},{2,98},{3,27},{4,100},{5,29},{6,102},{7,31},{8,104},... | collective-permute-start | bytes 393224 | tf_op jit(solution)/shard_map/ppermute | solution.py:75
  60.2 14.4 %collective-permute-done.11.row_ref = f32[256,1]{1,0:T(8,128)S(1)} collective-permute-done((f32[256,1]{1,0:T(8,128)S(1)}, f32[256,1]{1,0:T(8,128)S(1)}, u32[]{:S(2)}, u32[]{:S(2)}) %collective-permute-start.11) | collective-permute-done | bytes 1056 | tf_op jit(solution)/shard_map/ppermute | solution.py:75
  74.7 2.8 %shard_map.84 = bf16[8,256,256]{2,1,0:T(8,128)(2,1)S(1)} custom-call(s32[64]{0:T(128)S(1)} %dynamic-slice_bitcast_fusion.order_ref, f32[8,128]{1,0:T(8,128)S(1)} %add.98.total_ref, f32[256,1]{1,0:T(8,128)S(1)} %collective-permute-done.11.row_ref, f32[64,256]{1,0:T(8,128)S(1)} %copy-done.2, f32[64,256]{1,0:T(8,128)S(1)} %copy-done.4, ...), custom_call_target="tpu_custom_call" | custom-call | flops 536870912 | bytes 4194304 | tf_op jit(solution)/shard_map/pallas_call | solution.py:220
  77.6 2.4 %shard_map.80 = f32[8,256,256]{2,1,0:T(8,128)S(1)} custom-call(s32[64]{0:T(128)S(1)} %dynamic-slice_bitcast_fusion.order_ref, f32[8,128]{1,0:T(8,128)S(1)} %add.98.total_ref, f32[256,1]{1,0:T(8,128)S(1)} %collective-permute-done.4.row_ref, f32[64,256]{1,0:T(8,128)S(1)} %copy-done.2, f32[64,256]{1,0:T(8,128)S(1)} %copy-done.4, ...), custom_call_target="tpu_custom_call" | custom-call | flops 536870912 | bytes 4194304 | tf_op jit(solution)/shard_map/pallas_call | solution.py:220
  80.0 3.0 %shard_map.83 = f32[8,256,256]{2,1,0:T(8,128)S(1)} custom-call(s32[64]{0:T(128)S(1)} %dynamic-slice_bitcast_fusion.order_ref, f32[8,128]{1,0:T(8,128)S(1)} %add.98.total_ref, f32[256,1]{1,0:T(8,128)S(1)} %collective-permute-done.11.row_ref, f32[64,256]{1,0:T(8,128)S(1)} %copy-done.2, f32[64,256]{1,0:T(8,128)S(1)} %copy-done.4, ...), custom_call_target="tpu_custom_call" | custom-call | flops 536870912 | bytes 4194304 | tf_op jit(solution)/shard_map/pallas_call | solution.py:220
  84.2 13.8 %collective-permute-done.14 = bf16[8,256,256]{2,1,0:T(8,128)(2,1)S(1)} collective-permute-done((bf16[8,256,256]{2,1,0:T(8,128)(2,1)S(1)}, bf16[8,256,256]{2,1,0:T(8,128)(2,1)S(1)}, u32[]{:S(2)}, u32[]{:S(2)}) %collective-permute-start.14) | collective-permute-done | bytes 1048608 | tf_op jit(solution)/shard_map/ppermute | solution.py:75
  99.6 3.0 %collective-permute-start.9 = (bf16[2,256,256]{2,1,0:T(8,128)(2,1)}, bf16[2,256,256]{2,1,0:T(8,128)(2,1)S(1)}, u32[]{:S(2)}, u32[]{:S(2)}) collective-permute-start(bf16[2,256,256]{2,1,0:T(8,128)(2,1)} %fusion.3), channel_id=1, source_target_pairs={{0,24},{1,97},{2,26},{3,99},{4,28},{5,101},{6,30},{7,103},{8,16},{... | collective-permute-start | bytes 786440 | tf_op jit(solution)/shard_map/ppermute | solution.py:75
  102.6 6.3 %collective-permute-done.15 = bf16[4,256,256]{2,1,0:T(8,128)(2,1)S(1)} collective-permute-done((bf16[4,256,256]{2,1,0:T(8,128)(2,1)S(1)}, bf16[4,256,256]{2,1,0:T(8,128)(2,1)S(1)}, u32[]{:S(2)}, u32[]{:S(2)}) %collective-permute-start.15) | collective-permute-done | bytes 524320 | tf_op jit(solution)/shard_map/ppermute | solution.py:75
  112.8 3.8 %collective-permute-start.10 = (bf16[256,256]{1,0:T(8,128)(2,1)S(1)}, bf16[256,256]{1,0:T(8,128)(2,1)S(1)}, u32[]{:S(2)}, u32[]{:S(2)}) collective-permute-start(bf16[256,256]{1,0:T(8,128)(2,1)S(1)} %fusion.12), channel_id=1, source_target_pairs={{0,4},{1,5},{2,6},{3,7},{4,0},{5,1},{6,2},{7,3},{8,12},{9,13},{10,... | collective-permute-start | bytes 393224 | tf_op jit(solution)/shard_map/ppermute | solution.py:75
  118.7 3.8 %collective-permute-start.17 = (bf16[256,256]{1,0:T(8,128)(2,1)S(1)}, bf16[256,256]{1,0:T(8,128)(2,1)S(1)}, u32[]{:S(2)}, u32[]{:S(2)}) collective-permute-start(bf16[256,256]{1,0:T(8,128)(2,1)S(1)} %fusion.13), channel_id=1, source_target_pairs={{0,4},{1,5},{2,6},{3,7},{4,0},{5,1},{6,2},{7,3},{8,12},{9,13},{10,... | collective-permute-start | bytes 393224 | tf_op jit(solution)/shard_map/ppermute | solution.py:75
  123.7 1.8 %collective-permute-done.17 = bf16[256,256]{1,0:T(8,128)(2,1)S(1)} collective-permute-done((bf16[256,256]{1,0:T(8,128)(2,1)S(1)}, bf16[256,256]{1,0:T(8,128)(2,1)S(1)}, u32[]{:S(2)}, u32[]{:S(2)}) %collective-permute-start.17) | collective-permute-done | bytes 131104 | tf_op jit(solution)/shard_map/ppermute | solution.py:75
  (70 shorter events, 22.7 us)
Async XLA Ops:
  5.2 14.4 %copy-start.11 = (s32[256]{0:T(256)S(1)}, s32[256]{0:T(256)}, u32[]{:S(2)}) copy-start(s32[256]{0:T(256)} %param.7) | copy-start | bytes 3076
  5.2 48.1 %collective-permute-start.6 = (bf16[16,256,256]{2,1,0:T(8,128)(2,1)}, bf16[16,256,256]{2,1,0:T(8,128)(2,1)S(1)}, u32[]{:S(2)}, u32[]{:S(2)}) collective-permute-start(bf16[16,256,256]{2,1,0:T(8,128)(2,1)} %shard_map.79), channel_id=1, source_target_pairs={{0,32},{1,9},{2,34},{3,11},{4,36},{5,13},{6,38},{7,15},{8,40},{9,1... | collective-permute-start | bytes 6291464 | tf_op jit(solution)/shard_map/ppermute | solution.py:75
  10.6 64.0 %collective-permute-start.13 = (bf16[16,256,256]{2,1,0:T(8,128)(2,1)}, bf16[16,256,256]{2,1,0:T(8,128)(2,1)}, u32[]{:S(2)}, u32[]{:S(2)}) collective-permute-start(bf16[16,256,256]{2,1,0:T(8,128)(2,1)} %shard_map.82), channel_id=1, source_target_pairs={{0,96},{1,25},{2,98},{3,27},{4,100},{5,29},{6,102},{7,31},{8,104},... | collective-permute-start | bytes 6291464 | tf_op jit(solution)/shard_map/ppermute | solution.py:75
  15.7 1.4 %collective-permute-start = (f32[8,128]{1,0:T(8,128)}, f32[8,128]{1,0:T(8,128)S(1)}, u32[]{:S(2)}, u32[]{:S(2)}) collective-permute-start(f32[8,128]{1,0:T(8,128)} %get-tuple-element.7), channel_id=1, source_target_pairs={{0,1},{1,0},{2,3},{3,2},{4,5},{5,4},{6,7},{7,6},{8,9},{9,8},{10,11... | collective-permute-start | bytes 12296 | tf_op jit(solution)/shard_map/ppermute | solution.py:75
  17.7 3.6 %collective-permute-start.1 = (f32[8,128]{1,0:T(8,128)S(1)}, f32[8,128]{1,0:T(8,128)S(1)}, u32[]{:S(2)}, u32[]{:S(2)}) collective-permute-start(f32[8,128]{1,0:T(8,128)S(1)} %add.97), channel_id=1, source_target_pairs={{0,2},{1,3},{2,0},{3,1},{4,6},{5,7},{6,4},{7,5},{8,10},{9,11},{10,... | collective-permute-start | bytes 12296 | tf_op jit(solution)/shard_map/ppermute | solution.py:75
  23.0 30.4 %copy-start.2 = (f32[64,256]{1,0:T(8,128)S(1)}, f32[64,256]{1,0:T(8,128)}, u32[]{:S(2)}) copy-start(f32[64,256]{1,0:T(8,128)} %get-tuple-element.8.power_ref) | copy-start | bytes 196612
  23.0 30.4 %copy-start.4 = (f32[64,256]{1,0:T(8,128)S(1)}, f32[64,256]{1,0:T(8,128)}, u32[]{:S(2)}) copy-start(f32[64,256]{1,0:T(8,128)} %get-tuple-element.9.shrink_ref) | copy-start | bytes 196612
  36.6 1.6 %collective-permute-start.2 = (f32[256,256]{1,0:T(8,128)S(1)}, f32[256,256]{1,0:T(8,128)S(1)}, u32[]{:S(2)}, u32[]{:S(2)}) collective-permute-start(f32[256,256]{1,0:T(8,128)S(1)} %get-tuple-element.10), channel_id=1, source_target_pairs={{0,1},{1,0},{2,3},{3,2},{4,5},{5,4},{6,7},{7,6},{8,9},{9,8},{10,11... | collective-permute-start | bytes 786440 | tf_op jit(solution)/shard_map/ppermute | solution.py:75
  38.3 8.6 %collective-permute-start.3 = (f32[256,256]{1,0:T(8,128)S(1)}, f32[256,256]{1,0:T(8,128)S(1)}, u32[]{:S(2)}, u32[]{:S(2)}) collective-permute-start(f32[256,256]{1,0:T(8,128)S(1)} %add.99), channel_id=1, source_target_pairs={{0,2},{1,3},{2,0},{3,1},{4,6},{5,7},{6,4},{7,5},{8,10},{9,11},{10,... | collective-permute-start | bytes 786440 | tf_op jit(solution)/shard_map/ppermute | solution.py:75
  46.9 6.5 %collective-permute-start.5 = (bf16[256,256]{1,0:T(8,128)(2,1)S(1)}, bf16[256,256]{1,0:T(8,128)(2,1)S(1)}, u32[]{:S(2)}, u32[]{:S(2)}) collective-permute-start(bf16[256,256]{1,0:T(8,128)(2,1)S(1)} %add_convert_fusion.y_own_ref), channel_id=1, source_target_pairs={{0,32},{1,9},{2,34},{3,11},{4,36},{5,13},{6,38},{7,15},{8,40},{9,1... | collective-permute-start | bytes 393224 | tf_op jit(solution)/shard_map/ppermute | solution.py:75
  47.6 5.8 %collective-permute-start.4 = (f32[256,1]{1,0:T(8,128)S(1)}, f32[256,1]{1,0:T(8,128)S(1)}, u32[]{:S(2)}, u32[]{:S(2)}) collective-permute-start(f32[256,1]{1,0:T(8,128)S(1)} %copy.10.row_ref), channel_id=1, source_target_pairs={{0,32},{1,9},{2,34},{3,11},{4,36},{5,13},{6,38},{7,15},{8,40},{9,1... | collective-permute-start | bytes 3080 | tf_op jit(solution)/shard_map/ppermute | solution.py:75
  55.8 27.2 %collective-permute-start.7 = (bf16[8,256,256]{2,1,0:T(8,128)(2,1)S(1)}, bf16[8,256,256]{2,1,0:T(8,128)(2,1)S(1)}, u32[]{:S(2)}, u32[]{:S(2)}) collective-permute-start(bf16[8,256,256]{2,1,0:T(8,128)(2,1)S(1)} %shard_map.81), channel_id=1, source_target_pairs={{0,96},{1,25},{2,98},{3,27},{4,100},{5,29},{6,102},{7,31},{8,104},... | collective-permute-start | bytes 3145736 | tf_op jit(solution)/shard_map/ppermute | solution.py:75
  57.0 17.7 %collective-permute-start.12 = (bf16[256,256]{1,0:T(8,128)(2,1)S(1)}, bf16[256,256]{1,0:T(8,128)(2,1)S(1)}, u32[]{:S(2)}, u32[]{:S(2)}) collective-permute-start(bf16[256,256]{1,0:T(8,128)(2,1)S(1)} %add_convert_fusion.y_own_ref), channel_id=1, source_target_pairs={{0,96},{1,25},{2,98},{3,27},{4,100},{5,29},{6,102},{7,31},{8,104},... | collective-permute-start | bytes 393224 | tf_op jit(solution)/shard_map/ppermute | solution.py:75
  59.1 15.6 %collective-permute-start.11 = (f32[256,1]{1,0:T(8,128)S(1)}, f32[256,1]{1,0:T(8,128)S(1)}, u32[]{:S(2)}, u32[]{:S(2)}) collective-permute-start(f32[256,1]{1,0:T(8,128)S(1)} %copy.10.row_ref), channel_id=1, source_target_pairs={{0,96},{1,25},{2,98},{3,27},{4,100},{5,29},{6,102},{7,31},{8,104},... | collective-permute-start | bytes 3080 | tf_op jit(solution)/shard_map/ppermute | solution.py:75
  77.5 20.5 %collective-permute-start.14 = (bf16[8,256,256]{2,1,0:T(8,128)(2,1)S(1)}, bf16[8,256,256]{2,1,0:T(8,128)(2,1)S(1)}, u32[]{:S(2)}, u32[]{:S(2)}) collective-permute-start(bf16[8,256,256]{2,1,0:T(8,128)(2,1)S(1)} %shard_map.84), channel_id=1, source_target_pairs={{0,32},{1,9},{2,34},{3,11},{4,36},{5,13},{6,38},{7,15},{8,40},{9,1... | collective-permute-start | bytes 3145736 | tf_op jit(solution)/shard_map/ppermute | solution.py:75
  80.0 18.8 %copy-start = (f32[8,256,256]{2,1,0:T(8,128)}, f32[8,256,256]{2,1,0:T(8,128)S(1)}, u32[]{:S(2)}) copy-start(f32[8,256,256]{2,1,0:T(8,128)S(1)} %shard_map.80) | copy-start | bytes 6291460
  83.2 15.7 %copy-start.5 = (f32[8,256,256]{2,1,0:T(8,128)}, f32[8,256,256]{2,1,0:T(8,128)S(1)}, u32[]{:S(2)}) copy-start(f32[8,256,256]{2,1,0:T(8,128)S(1)} %convert_element_type.56) | copy-start | bytes 6291460
  83.4 15.3 %collective-permute-start.8 = (bf16[4,256,256]{2,1,0:T(8,128)(2,1)S(1)}, bf16[4,256,256]{2,1,0:T(8,128)(2,1)S(1)}, u32[]{:S(2)}, u32[]{:S(2)}) collective-permute-start(bf16[4,256,256]{2,1,0:T(8,128)(2,1)S(1)} %fusion.1), channel_id=1, source_target_pairs={{0,8},{1,33},{2,10},{3,35},{4,12},{5,37},{6,14},{7,39},{8,0},{9,41... | collective-permute-start | bytes 1572872 | tf_op jit(solution)/shard_map/ppermute | solution.py:75
  98.2 10.8 %copy-start.6 = (f32[8,256,256]{2,1,0:T(8,128)}, f32[8,256,256]{2,1,0:T(8,128)S(1)}, u32[]{:S(2)}) copy-start(f32[8,256,256]{2,1,0:T(8,128)S(1)} %convert_element_type.64) | copy-start | bytes 6291460
  98.4 10.5 %collective-permute-start.15 = (bf16[4,256,256]{2,1,0:T(8,128)(2,1)S(1)}, bf16[4,256,256]{2,1,0:T(8,128)(2,1)S(1)}, u32[]{:S(2)}, u32[]{:S(2)}) collective-permute-start(bf16[4,256,256]{2,1,0:T(8,128)(2,1)S(1)} %fusion), channel_id=1, source_target_pairs={{0,24},{1,97},{2,26},{3,99},{4,28},{5,101},{6,30},{7,103},{8,16},{... | collective-permute-start | bytes 1572872 | tf_op jit(solution)/shard_map/ppermute | solution.py:75
  99.6 12.0 %collective-permute-start.9 = (bf16[2,256,256]{2,1,0:T(8,128)(2,1)}, bf16[2,256,256]{2,1,0:T(8,128)(2,1)S(1)}, u32[]{:S(2)}, u32[]{:S(2)}) collective-permute-start(bf16[2,256,256]{2,1,0:T(8,128)(2,1)} %fusion.3), channel_id=1, source_target_pairs={{0,24},{1,97},{2,26},{3,99},{4,28},{5,101},{6,30},{7,103},{8,16},{... | collective-permute-start | bytes 786440 | tf_op jit(solution)/shard_map/ppermute | solution.py:75
  110.0 6.7 %collective-permute-start.16 = (bf16[2,256,256]{2,1,0:T(8,128)(2,1)}, bf16[2,256,256]{2,1,0:T(8,128)(2,1)}, u32[]{:S(2)}, u32[]{:S(2)}) collective-permute-start(bf16[2,256,256]{2,1,0:T(8,128)(2,1)} %fusion.2), channel_id=1, source_target_pairs={{0,8},{1,33},{2,10},{3,35},{4,12},{5,37},{6,14},{7,39},{8,0},{9,41... | collective-permute-start | bytes 786440 | tf_op jit(solution)/shard_map/ppermute | solution.py:75
  112.8 9.7 %collective-permute-start.10 = (bf16[256,256]{1,0:T(8,128)(2,1)S(1)}, bf16[256,256]{1,0:T(8,128)(2,1)S(1)}, u32[]{:S(2)}, u32[]{:S(2)}) collective-permute-start(bf16[256,256]{1,0:T(8,128)(2,1)S(1)} %fusion.12), channel_id=1, source_target_pairs={{0,4},{1,5},{2,6},{3,7},{4,0},{5,1},{6,2},{7,3},{8,12},{9,13},{10,... | collective-permute-start | bytes 393224 | tf_op jit(solution)/shard_map/ppermute | solution.py:75
  118.7 6.7 %collective-permute-start.17 = (bf16[256,256]{1,0:T(8,128)(2,1)S(1)}, bf16[256,256]{1,0:T(8,128)(2,1)S(1)}, u32[]{:S(2)}, u32[]{:S(2)}) collective-permute-start(bf16[256,256]{1,0:T(8,128)(2,1)S(1)} %fusion.13), channel_id=1, source_target_pairs={{0,4},{1,5},{2,6},{3,7},{4,0},{5,1},{6,2},{7,3},{8,12},{9,13},{10,... | collective-permute-start | bytes 393224 | tf_op jit(solution)/shard_map/ppermute | solution.py:75
  (6 other events, 25.4 us)

commit v2 on v0

v2 whole, which is shorter than its diff:
```python
import functools

import jax
import jax.numpy as jnp
from jax import lax
from jax.experimental import pallas as pl
from jax.experimental.pallas import tpu as pltpu
from jax.sharding import PartitionSpec as P

AXES = ("rows", "cols")
W = 256
STEP = 8
F32, BF16 = jnp.float32, jnp.bfloat16

NEAR, FAR = (1, 3), (3, 1)


def xor_perm(mask):
    pairs = []
    for d in range(128):
        r, zl, core = d >> 2, (d >> 1) & 1, d & 1
        dr, dzl, dcore = mask(core)
        pairs.append((d, ((r ^ dr) << 2) | ((zl ^ dzl) << 1) | (core ^ dcore)))
    return pairs


def u_perm(d):
    return xor_perm(lambda core: (d * (2 if core else 8), 0, 0))


def v_perm(d):
    return xor_perm(lambda core: (d * (8 if core else 2), 0, 0))


ZH_PERM = xor_perm(lambda core: (1, 0, 0))
ZL_PERM = xor_perm(lambda core: (0, 1, 0))
CORE_PERM = xor_perm(lambda core: (0, 0, 1))


def permute(a, perm):
    return lax.ppermute(a, AXES, perm)


def place():
    core = lax.rem(lax.axis_index("cols"), 2)
    return lax.axis_index("rows"), core


def block_of(r, core, g, d, e, k):
    return (r ^ (d * (8 - 6 * core) + e * (2 + 6 * core) + k)) * 2 + g


def slots(g, part):
    out = []
    for i in range(2):
        for j in range(4):
            for k in range(2):
                out.append(((NEAR[g] if part else 0) ^ (FAR[g] * i), (FAR[g] * (j & 1)) ^ (NEAR[g] * (j >> 1)), k))
    return out


def params(mib):
    return pltpu.CompilerParams(vmem_limit_bytes=mib << 20)


def spec(space):
    return pl.BlockSpec(memory_space=space)


def context_kernel(all_ref, power_ref, shrink_ref, total_ref, inv_ref, tail_ref):
    power = jnp.exp(0.75 * jnp.log(all_ref[0:128, :].astype(F32)))
    power_ref[...] = 1.0 / power
    shrink_ref[...] = all_ref[128:256, :].astype(F32) * 0.25
    total_ref[...] = jnp.full((8, 128), jnp.sum(power), F32)
    wide = jnp.concatenate([all_ref[256:257, :], all_ref[257:258, :]], axis=1)
    inv_ref[...] = 1.0 / jnp.transpose(jnp.broadcast_to(wide.astype(F32), (128, W)))
    at = lax.broadcasted_iota(jnp.int32, (16, W), 0)
    low, mid, high = wide & 63, (wide >> 6) & 63, wide >> 12
    tail_ref[...] = jnp.where(at == 0, low, jnp.where(at == 1, mid, high)).astype(F32).astype(BF16)


def context(ctx_marg, discount, row_marg):
    square = jax.ShapeDtypeStruct((128, 128), F32)
    return pl.pallas_call(
        context_kernel,
        in_specs=[spec(pltpu.VMEM)],
        out_specs=[spec(pltpu.VMEM)] * 5,
        out_shape=(square, square, jax.ShapeDtypeStruct((8, 128), F32), jax.ShapeDtypeStruct((W, 128), F32),
                   jax.ShapeDtypeStruct((16, W), BF16)),
        compiler_params=params(2),
        cost_estimate=pl.CostEstimate(flops=1 << 18, bytes_accessed=1 << 18, transcendentals=1 << 15),
    )(jnp.concatenate([ctx_marg, discount, row_marg]).reshape(258, 128))


def prepare_kernel(part, *refs):
    if part == 1:
        tail_ref, counts_ref, *outs, in_ref, sem = refs
        for out_ref in outs:
            out_ref[16 * W:16 * W + 16, :] = tail_ref[...]
    else:
        counts_ref, kept_ref, in_ref, sem = refs
    r, core = place()

    def fetch(s):
        d, e, k = slots(s // 16, part)[s % 16]
        at = pl.multiple_of(block_of(r, core, s // 16, d, e, k) * W, W)
        return pltpu.make_async_copy(counts_ref.at[:, pl.ds(at, W)], in_ref.at[s], sem.at[s])

    for s in range(32):
        fetch(s).start()
    for s in range(32):
        fetch(s).wait()
        block = in_ref[s].astype(F32).astype(BF16)
        if part == 1:
            outs[s // 16][s % 16 * W:(s % 16 + 1) * W, :] = block
        else:
            kept_ref[s * W:(s + 1) * W, :] = block


def prepare(part, counts, *tail):
    rows = counts.shape[0]
    lengths = [16 * W + 16] * 2 if part else [32 * W]
    return pl.pallas_call(
        functools.partial(prepare_kernel, part),
        in_specs=[spec(pltpu.VMEM)] * part + [spec(pl.ANY)],
        out_specs=[spec(pltpu.VMEM)] * len(lengths),
        out_shape=[jax.ShapeDtypeStruct((n, W), BF16) for n in lengths],
        scratch_shapes=[pltpu.VMEM((32, rows, W), jnp.int32), pltpu.SemaphoreType.DMA((32,))],
        compiler_params=params(42),
        cost_estimate=pl.CostEstimate(flops=1 << 22, bytes_accessed=12 << 20, transcendentals=0),
    )(*tail, counts)


def tile_rows(counts, shrink, scale, inv_row):
    inv_row = jnp.concatenate([inv_row, inv_row], axis=1)
    excess = counts.astype(F32) - shrink
    return jnp.log(jnp.maximum(excess * scale * inv_row, 1.0)).astype(BF16)


def column_terms(ref, block):
    return jnp.concatenate([ref[pl.ds(2 * block, 1), :], ref[pl.ds(2 * block + 1, 1), :]], axis=1)


def forward_kernel(total_ref, other_ref, inv_ref, power_ref, shrink_ref, kept_ref, sent_a, sent_b, probes_ref,
                   tile_ref, y_ref, acc_ref, work_ref):
    r, core = place()
    total = total_ref[0, 0] + other_ref[0, 0]
    rows = inv_ref.shape[0]
    acc_ref[...] = jnp.zeros_like(acc_ref)
    for g, sent_ref in enumerate((sent_a, sent_b)):
        for part in range(2):
            @pl.loop(0, 2)
            def _(i):
                sums = None
                for n, (d, e, k) in enumerate(slots(g, part)[:8]):
                    block = block_of(r, core, g, d ^ (FAR[g] * i), e, k)
                    at = pl.multiple_of(block * W, W)
                    shrink = column_terms(shrink_ref, block)
                    scale = column_terms(power_ref, block) * total
                    if part == 0:
                        source, base, out = kept_ref, (16 * g + 8 * i + n) * rows, tile_ref.at[16 * g + 8 * i + n]
                    else:
                        source, base, out = sent_ref, (8 * i + n) * rows, work_ref.at[n]
                    base = pl.multiple_of(base, rows)
                    for q in range(0, rows, 32):
                        out[q:q + 32, :] = tile_rows(source[pl.ds(base + q, 32), :], shrink, scale, inv_ref[q:q + 32, :])
                    term = jnp.dot(out[...], probes_ref[pl.ds(at, W), :], preferred_element_type=F32)
                    sums = term if sums is None else sums + term
                acc_ref[...] += sums
    y_ref[...] = jnp.transpose(acc_ref[...])


def forward(total, other, inv_row, power, shrink, kept, sent, probes):
    rows, width = inv_row.shape[0], probes.shape[1]
    vmem, smem = spec(pltpu.VMEM), spec(pltpu.SMEM)
    return pl.pallas_call(
        forward_kernel,
        in_specs=[smem, smem] + [vmem] * 7,
        out_specs=[vmem, vmem],
        scratch_shapes=[pltpu.VMEM((rows, width), F32), pltpu.VMEM((STEP, rows, W), BF16)],
        out_shape=(jax.ShapeDtypeStruct((32, rows, W), BF16), jax.ShapeDtypeStruct((width, rows), F32)),
        compiler_params=params(4),
        cost_estimate=pl.CostEstimate(flops=1 << 31, bytes_accessed=28 << 20, transcendentals=1 << 22),
    )(total, other, inv_row, power, shrink, kept, *sent, probes)


def back_kernel(group, half, total_ref, other_ref, power_ref, shrink_ref, y_own_ref, y_other_ref, tile_ref, count_ref,
                z_ref, work_ref, inv_ref):
    r, core = place()
    total = total_ref[0, 0] + other_ref[0, 0]
    rows = tile_ref.shape[1]
    tail = count_ref[16 * W:16 * W + 16, :].astype(F32)
    marg = tail[0:1, :] + tail[1:2, :] * 64.0 + tail[2:3, :] * 4096.0
    inv_ref[...] = 1.0 / jnp.transpose(jnp.broadcast_to(marg, (128, rows)))
    for n in range(8):
        s = half * 8 + n
        d, e, k = slots(group, 0)[s]
        block = block_of(r, core, group, d, e, k)
        shrink = column_terms(shrink_ref, block)
        scale = column_terms(power_ref, block) * total
        for i in range(0, rows, 32):
            work_ref[n, i:i + 32, :] = tile_rows(
                count_ref[s * W + i:s * W + i + 32, :], shrink, scale, inv_ref[i:i + 32, :])
        out = jnp.dot(y_own_ref[...], tile_ref[group * 16 + s], preferred_element_type=F32)
        out = out + jnp.dot(y_other_ref[...], work_ref[n], preferred_element_type=F32)
        z_ref[n] = out.astype(z_ref.dtype)


def back(total, other, power, shrink, y_own, y_other, tile, received, group, half, dtype):
    rows, width = tile.shape[1], y_own.shape[0]
    vmem, smem = spec(pltpu.VMEM), spec(pltpu.SMEM)
    return pl.pallas_call(
        functools.partial(back_kernel, group, half),
        in_specs=[smem, smem] + [vmem] * 6,
        out_specs=vmem,
        scratch_shapes=[pltpu.VMEM((8, rows, W), BF16), pltpu.VMEM((rows, 128), F32)],
        out_shape=jax.ShapeDtypeStruct((8, width, W), dtype),
        compiler_params=params(4),
        cost_estimate=pl.CostEstimate(flops=1 << 29, bytes_accessed=4 << 20, transcendentals=1 << 19),
    )(total, other, power, shrink, y_own, y_other, tile, received)


def pair_kernel(a_ref, b_ref, out_ref):
    out_ref[0] = a_ref[...]
    out_ref[1] = b_ref[...]


def pair(a, b):
    vmem = spec(pltpu.VMEM)
    return pl.pallas_call(
        pair_kernel,
        in_specs=[vmem, vmem],
        out_specs=vmem,
        out_shape=jax.ShapeDtypeStruct((2,) + a.shape, a.dtype),
        compiler_params=params(1),
        cost_estimate=pl.CostEstimate(flops=0, bytes_accessed=1 << 19, transcendentals=0),
    )(a, b)


def last_kernel(factor, a_ref, b_ref, got_ref, z_ref):
    for g, ref in enumerate((a_ref, b_ref)):
        z_ref[g * W:(g + 1) * W, :] = jnp.transpose(ref[...] + got_ref[g].astype(F32)) * factor


def last(a, b, got, factor):
    width = a.shape[0]
    vmem = spec(pltpu.VMEM)
    return pl.pallas_call(
        functools.partial(last_kernel, factor),
        in_specs=[vmem] * 3,
        out_specs=vmem,
        out_shape=jax.ShapeDtypeStruct((2 * W, width), F32),
        compiler_params=params(2),
        cost_estimate=pl.CostEstimate(flops=1 << 20, bytes_accessed=2 << 20, transcendentals=0),
    )(a, b, got)


def local(counts, row_marg, ctx_marg, discount, probes):
    power, shrink, total, inv_row, tail = context(ctx_marg, discount, row_marg)
    sent = prepare(1, counts, tail)
    received = [permute(sent[g], u_perm(NEAR[g])) for g in range(2)]
    total = total + permute(total, CORE_PERM)
    other = permute(total, ZL_PERM)
    kept, = prepare(0, counts)
    tile, y_part = forward(total, other, inv_row, power, shrink, kept, sent, probes)
    y_chip = (y_part + permute(y_part, CORE_PERM)).astype(BF16)
    y_own = (y_chip.astype(F32) + permute(y_chip, ZL_PERM).astype(F32)).astype(BF16)
    y_other = lax.optimization_barrier([permute(y_own, u_perm(NEAR[g])) for g in range(2)])

    def run(g, half, dtype):
        return back(total, other, power, shrink, y_own, y_other[g], tile, received[g], g, half, dtype)

    own, ends = [], []
    sends = [run(g, 1, BF16) for g in range(2)]
    for g in range(2):
        r2 = permute(sends[g], u_perm(FAR[g]))
        z = run(g, 0, F32)
        r3 = permute((z[4:8] + r2[4:8].astype(F32)).astype(BF16), v_perm(NEAR[g]))
        r4 = permute((z[2:4] + r2[2:4].astype(F32) + r3[2:4].astype(F32)).astype(BF16), v_perm(FAR[g]))
        kept = [z[k] + r2[k].astype(F32) + r3[k].astype(F32) + r4[k].astype(F32) for k in range(2)]
        own.append(kept[0])
        ends.append(kept[1].astype(BF16))
    r5 = permute(pair(*ends), ZH_PERM)
    factor = (counts.shape[0] * lax.axis_size("rows")) ** (-0.5)
    z_proj = last(*own, r5, factor)
    return (jnp.transpose(y_own), z_proj[None])


def solution(mesh):
    in_specs = (P("rows", "cols"), P("rows"), P("cols"), P("cols"), P("cols", None))
    out_specs = (P("rows", None), P("cols", "rows", None))
    return jax.shard_map(local, mesh=mesh, in_specs=in_specs, out_specs=out_specs, check_vma=False)
```

time: 434 us -> 86.3 us (0.20)
  waiting for transfers between devices: 364 us -> 42 us
  Pallas kernels: 0 us -> 21.6 us
  blocking collectives: 21.4 us -> 0 us
  starting transfers between devices: 0.04 us -> 18.6 us
  between operations: 14.8 us -> 0.8 us
  matrix products: 13.9 us -> 0 us
  other arithmetic: 15 us -> 1.6 us
    reduce_scatter x1 -> x0, waiting for transfers between devices: 364 us -> none  [local(): lax.psum_scatter(lax.dot_general(a_tile, y_proj, (((0,), (0,)), ((), ()))...]
    ppermute x0 -> x15, waiting for transfers between devices: none -> 42 us  [permute(): return lax.ppermute(a, AXES, perm)]
    pallas_call x0 -> x10, Pallas kernels: none -> 21.6 us  [the longest x2 7.9 us: prepare(): pl.pallas_call(functools.partial(prepare_kernel, part), in_specs=[spec(pl...]
    psum x2 -> x0, blocking collectives: 21.4 us -> none  [the longest x1 13.5 us: local(): y_proj = lax.psum(y_local, 'cols').astype(jnp.bfloat16)]
    ppermute x0 -> x15, starting transfers between devices: none -> 18.6 us  [permute(): return lax.ppermute(a, AXES, perm)]
    dot_general x2 -> x0, matrix products: 13.9 us -> none  [the longest x1 11.6 us: local(): lax.dot_general(a_tile, y_proj, (((0,), (0,)), ((), ())), preferred_eleme...]
    convert_element_type x1 -> x6, other arithmetic: 10.2 us -> 0.48 us  [the longest x2 0.24 us: local(): r3 = permute((z[4:8] + r2[4:8].astype(F32)).astype(BF16), v_perm(NEAR[g]))]
  transfers between devices with their start and end apart: 1 -> 15, of which waited for: 1 -> 11; matrix products, arithmetic and copies ran while one was open for 0% -> 2% of each run, Pallas kernels for 0% -> 20%
where the time goes in v2:
time: 86.3 us; the launch traced here: 85.3 us
  waiting for transfers between devices  42 us (49%)
  Pallas kernels  21.6 us (25%)
  starting transfers between devices  18.6 us (22%)
  other arithmetic  1.6 us (2%)
    ppermute x15, waiting for transfers between devices, permute(): return lax.ppermute(a, AXES, perm)  42 us
    ppermute x15, starting transfers between devices, permute(): return lax.ppermute(a, AXES, perm)  18.6 us
    pallas_call x2, Pallas kernels, prepare(): pl.pallas_call(functools.partial(prepare_kernel, part), in_specs=[spec(pl...  7.9 us
    pallas_call x1, Pallas kernels, forward(): pl.pallas_call(forward_kernel, in_specs=[smem, smem] + [vmem] * 7, out_sp...  6.31 us
    pallas_call x4, Pallas kernels, back(): pl.pallas_call(functools.partial(back_kernel, group, half), in_specs=[sme...  6.2 us
  transfers between devices with their start and end apart: 15, of which 11 were waited for; matrix products, arithmetic and copies ran while one was open for 2% of the time, Pallas kernels for 20%

profile of v2, /device:TPU:24, one launch (start us, length us, event | category | flops | bytes accessed | tf_op | source)
XLA Modules:
  0.0 85.3 jit_solution(16988137000601386881)
XLA Ops:
  1.7 3.7 %shard_map.70 = (bf16[4112,256]{1,0:T(8,128)(2,1)S(1)}, bf16[4112,256]{1,0:T(8,128)(2,1)S(1)}) custom-call(bf16[16,256]{1,0:T(8,128)(2,1)S(1)} %get-tuple-element.17.refs_0_, s32[256,16384]{1,0:T(8,128)} %refs_1_.1), custom_call_target="tpu_custom_call" | custom-call | flops 4194304 | bytes 12582912 | tf_op jit(solution)/shard_map/pallas_call | solution.py:123
  5.5 1.6 %collective-permute-start.6 = (bf16[4112,256]{1,0:T(8,128)(2,1)S(1)}, bf16[4112,256]{1,0:T(8,128)(2,1)S(1)}, u32[]{:S(2)}, u32[]{:S(2)}) collective-permute-start(bf16[4112,256]{1,0:T(8,128)(2,1)S(1)} %get-tuple-element.18.sent_a), channel_id=1, source_target_pairs={{0,32},{1,9},{2,34},{3,11},{4,36},{5,13},{6,38},{7,15},{8,40},{9,1... | collective-permute-start | bytes 6316040 | tf_op jit(solution)/shard_map/ppermute | solution.py:41
  7.0 2.1 %collective-permute-start.10 = (bf16[4112,256]{1,0:T(8,128)(2,1)S(1)}, bf16[4112,256]{1,0:T(8,128)(2,1)S(1)}, u32[]{:S(2)}, u32[]{:S(2)}) collective-permute-start(bf16[4112,256]{1,0:T(8,128)(2,1)S(1)} %get-tuple-element.19.sent_b), channel_id=1, source_target_pairs={{0,96},{1,25},{2,98},{3,27},{4,100},{5,29},{6,102},{7,31},{8,104},... | collective-permute-start | bytes 6316040 | tf_op jit(solution)/shard_map/ppermute | solution.py:41
  10.3 2.0 %collective-permute-start.1 = (f32[8,128]{1,0:T(8,128)S(1)}, f32[8,128]{1,0:T(8,128)S(1)}, u32[]{:S(2)}, u32[]{:S(2)}) collective-permute-start(f32[8,128]{1,0:T(8,128)S(1)} %add.81.total_ref), channel_id=1, source_target_pairs={{0,2},{1,3},{2,0},{3,1},{4,6},{5,7},{6,4},{7,5},{8,10},{9,11},{10,... | collective-permute-start | bytes 12296 | tf_op jit(solution)/shard_map/ppermute | solution.py:41
  12.3 4.2 %shard_map.69.kept_ref = bf16[8192,256]{1,0:T(8,128)(2,1)S(1)} custom-call(s32[256,16384]{1,0:T(8,128)} %refs_1_.1), custom_call_target="tpu_custom_call" | custom-call | flops 4194304 | bytes 12582912 | tf_op jit(solution)/shard_map/pallas_call | solution.py:123
  16.5 6.3 %shard_map.71 = (bf16[32,256,256]{2,1,0:T(8,128)(2,1)S(1)}, f32[256,256]{1,0:T(8,128)S(1)}) custom-call(f32[8,128]{1,0:T(8,128)S(1)} %add.81.total_ref, f32[8,128]{1,0:T(8,128)S(1)} %collective-permute-done.1.other_ref, f32[256,128]{1,0:T(8,128)S(1)} %get-tuple-element.14.inv_ref, f32[128,128]{1,0:T(8,128)S(1)} %get-tuple-element.15.power_ref, ...), custom_call_target="tpu_custom_call" | custom-call | flops 2147483648 | bytes 29360128 | tf_op jit(solution)/shard_map/pallas_call | solution.py:176
  23.0 1.4 %collective-permute-done.2 = f32[256,256]{1,0:T(8,128)S(1)} collective-permute-done((f32[256,256]{1,0:T(8,128)S(1)}, f32[256,256]{1,0:T(8,128)S(1)}, u32[]{:S(2)}, u32[]{:S(2)}) %collective-permute-start.2) | collective-permute-done | bytes 262176 | tf_op jit(solution)/shard_map/ppermute | solution.py:41
  24.5 1.8 %collective-permute-start.3 = (bf16[256,256]{1,0:T(8,128)(2,1)S(1)}, bf16[256,256]{1,0:T(8,128)(2,1)S(1)}, u32[]{:S(2)}, u32[]{:S(2)}) collective-permute-start(bf16[256,256]{1,0:T(8,128)(2,1)S(1)} %add_convert_fusion.1), channel_id=1, source_target_pairs={{0,2},{1,3},{2,0},{3,1},{4,6},{5,7},{6,4},{7,5},{8,10},{9,11},{10,... | collective-permute-start | bytes 393224 | tf_op jit(solution)/shard_map/ppermute | solution.py:41
  26.3 3.8 %collective-permute-done.3 = bf16[256,256]{1,0:T(8,128)(2,1)S(1)} collective-permute-done((bf16[256,256]{1,0:T(8,128)(2,1)S(1)}, bf16[256,256]{1,0:T(8,128)(2,1)S(1)}, u32[]{:S(2)}, u32[]{:S(2)}) %collective-permute-start.3) | collective-permute-done | bytes 131104 | tf_op jit(solution)/shard_map/ppermute | solution.py:41
  30.1 1.2 %collective-permute-start.5 = (bf16[256,256]{1,0:T(8,128)(2,1)S(1)}, bf16[256,256]{1,0:T(8,128)(2,1)S(1)}, u32[]{:S(2)}, u32[]{:S(2)}) collective-permute-start(bf16[256,256]{1,0:T(8,128)(2,1)S(1)} %add_convert_fusion.y_own_ref), channel_id=1, source_target_pairs={{0,96},{1,25},{2,98},{3,27},{4,100},{5,29},{6,102},{7,31},{8,104},... | collective-permute-start | bytes 393224 | tf_op jit(solution)/shard_map/ppermute | solution.py:41
  31.3 5.0 %collective-permute-done.5.y_other_ref = bf16[256,256]{1,0:T(8,128)(2,1)S(1)} collective-permute-done((bf16[256,256]{1,0:T(8,128)(2,1)S(1)}, bf16[256,256]{1,0:T(8,128)(2,1)S(1)}, u32[]{:S(2)}, u32[]{:S(2)}) %collective-permute-start.5) | collective-permute-done | bytes 131104 | tf_op jit(solution)/shard_map/ppermute | solution.py:41
  36.4 1.5 %shard_map.73 = bf16[8,256,256]{2,1,0:T(8,128)(2,1)S(1)} custom-call(f32[8,128]{1,0:T(8,128)S(1)} %add.81.total_ref, f32[8,128]{1,0:T(8,128)S(1)} %collective-permute-done.1.other_ref, f32[128,128]{1,0:T(8,128)S(1)} %get-tuple-element.15.power_ref, f32[128,128]{1,0:T(8,128)S(1)} %get-tuple-element.16.shrink_ref, ...), custom_call_target="tpu_custom_call" | custom-call | flops 536870912 | bytes 4194304 | tf_op jit(solution)/shard_map/pallas_call | solution.py:212
  37.9 2.1 %collective-permute-start.7 = (bf16[8,256,256]{2,1,0:T(8,128)(2,1)S(1)}, bf16[8,256,256]{2,1,0:T(8,128)(2,1)S(1)}, u32[]{:S(2)}, u32[]{:S(2)}) collective-permute-start(bf16[8,256,256]{2,1,0:T(8,128)(2,1)S(1)} %shard_map.73), channel_id=1, source_target_pairs={{0,96},{1,25},{2,98},{3,27},{4,100},{5,29},{6,102},{7,31},{8,104},... | collective-permute-start | bytes 3145736 | tf_op jit(solution)/shard_map/ppermute | solution.py:41
  40.1 1.6 %shard_map.75 = bf16[8,256,256]{2,1,0:T(8,128)(2,1)S(1)} custom-call(f32[8,128]{1,0:T(8,128)S(1)} %add.81.total_ref, f32[8,128]{1,0:T(8,128)S(1)} %collective-permute-done.1.other_ref, f32[128,128]{1,0:T(8,128)S(1)} %get-tuple-element.15.power_ref, f32[128,128]{1,0:T(8,128)S(1)} %get-tuple-element.16.shrink_ref, ...), custom_call_target="tpu_custom_call" | custom-call | flops 536870912 | bytes 4194304 | tf_op jit(solution)/shard_map/pallas_call | solution.py:212
  41.7 1.5 %shard_map.72 = f32[8,256,256]{2,1,0:T(8,128)S(1)} custom-call(f32[8,128]{1,0:T(8,128)S(1)} %add.81.total_ref, f32[8,128]{1,0:T(8,128)S(1)} %collective-permute-done.1.other_ref, f32[128,128]{1,0:T(8,128)S(1)} %get-tuple-element.15.power_ref, f32[128,128]{1,0:T(8,128)S(1)} %get-tuple-element.16.shrink_ref, bf16[256,256]{1,0:T(8,128)(2,1)S(1)} %add_convert_fusion.y_own_ref, ...), custom_call_target="tpu_custom_call" | custom-call | flops 536870912 | bytes 4194304 | tf_op jit(solution)/shard_map/pallas_call | solution.py:212
  43.3 1.6 %shard_map.74 = f32[8,256,256]{2,1,0:T(8,128)S(1)} custom-call(f32[8,128]{1,0:T(8,128)S(1)} %add.81.total_ref, f32[8,128]{1,0:T(8,128)S(1)} %collective-permute-done.1.other_ref, f32[128,128]{1,0:T(8,128)S(1)} %get-tuple-element.15.power_ref, f32[128,128]{1,0:T(8,128)S(1)} %get-tuple-element.16.shrink_ref, bf16[256,256]{1,0:T(8,128)(2,1)S(1)} %add_convert_fusion.y_own_ref, ...), custom_call_target="tpu_custom_call" | custom-call | flops 536870912 | bytes 4194304 | tf_op jit(solution)/shard_map/pallas_call | solution.py:212
  44.8 9.2 %collective-permute-done.7 = bf16[8,256,256]{2,1,0:T(8,128)(2,1)S(1)} collective-permute-done((bf16[8,256,256]{2,1,0:T(8,128)(2,1)S(1)}, bf16[8,256,256]{2,1,0:T(8,128)(2,1)S(1)}, u32[]{:S(2)}, u32[]{:S(2)}) %collective-permute-start.7) | collective-permute-done | bytes 1048608 | tf_op jit(solution)/shard_map/ppermute | solution.py:41
  55.0 3.8 %collective-permute-done.11 = bf16[8,256,256]{2,1,0:T(8,128)(2,1)S(1)} collective-permute-done((bf16[8,256,256]{2,1,0:T(8,128)(2,1)S(1)}, bf16[8,256,256]{2,1,0:T(8,128)(2,1)S(1)}, u32[]{:S(2)}, u32[]{:S(2)}) %collective-permute-start.11) | collective-permute-done | bytes 1048608 | tf_op jit(solution)/shard_map/ppermute | solution.py:41
  59.0 4.4 %collective-permute-done.8 = bf16[4,256,256]{2,1,0:T(8,128)(2,1)S(1)} collective-permute-done((bf16[4,256,256]{2,1,0:T(8,128)(2,1)S(1)}, bf16[4,256,256]{2,1,0:T(8,128)(2,1)S(1)}, u32[]{:S(2)}, u32[]{:S(2)}) %collective-permute-start.8) | collective-permute-done | bytes 524320 | tf_op jit(solution)/shard_map/ppermute | solution.py:41
  64.7 4.7 %collective-permute-done.12 = bf16[4,256,256]{2,1,0:T(8,128)(2,1)S(1)} collective-permute-done((bf16[4,256,256]{2,1,0:T(8,128)(2,1)S(1)}, bf16[4,256,256]{2,1,0:T(8,128)(2,1)S(1)}, u32[]{:S(2)}, u32[]{:S(2)}) %collective-permute-start.12) | collective-permute-done | bytes 524320 | tf_op jit(solution)/shard_map/ppermute | solution.py:41
  69.5 1.6 %collective-permute-start.13 = (bf16[2,256,256]{2,1,0:T(8,128)(2,1)S(1)}, bf16[2,256,256]{2,1,0:T(8,128)(2,1)S(1)}, u32[]{:S(2)}, u32[]{:S(2)}) collective-permute-start(bf16[2,256,256]{2,1,0:T(8,128)(2,1)S(1)} %fusion.3), channel_id=1, source_target_pairs={{0,8},{1,33},{2,10},{3,35},{4,12},{5,37},{6,14},{7,39},{8,0},{9,41... | collective-permute-start | bytes 786440 | tf_op jit(solution)/shard_map/ppermute | solution.py:41
  72.3 3.6 %collective-permute-done.13 = bf16[2,256,256]{2,1,0:T(8,128)(2,1)S(1)} collective-permute-done((bf16[2,256,256]{2,1,0:T(8,128)(2,1)S(1)}, bf16[2,256,256]{2,1,0:T(8,128)(2,1)S(1)}, u32[]{:S(2)}, u32[]{:S(2)}) %collective-permute-start.13) | collective-permute-done | bytes 262176 | tf_op jit(solution)/shard_map/ppermute | solution.py:41
  76.1 3.9 %collective-permute-start.14 = (bf16[2,256,256]{2,1,0:T(8,128)(2,1)S(1)}, bf16[2,256,256]{2,1,0:T(8,128)(2,1)S(1)}, u32[]{:S(2)}, u32[]{:S(2)}) collective-permute-start(bf16[2,256,256]{2,1,0:T(8,128)(2,1)S(1)} %shard_map.76), channel_id=1, source_target_pairs={{0,4},{1,5},{2,6},{3,7},{4,0},{5,1},{6,2},{7,3},{8,12},{9,13},{10,... | collective-permute-start | bytes 786440 | tf_op jit(solution)/shard_map/ppermute | solution.py:41
  80.7 3.6 %collective-permute-done.14.got_ref = bf16[2,256,256]{2,1,0:T(8,128)(2,1)S(1)} collective-permute-done((bf16[2,256,256]{2,1,0:T(8,128)(2,1)S(1)}, bf16[2,256,256]{2,1,0:T(8,128)(2,1)S(1)}, u32[]{:S(2)}, u32[]{:S(2)}) %collective-permute-start.14) | collective-permute-done | bytes 262176 | tf_op jit(solution)/shard_map/ppermute | solution.py:41
  (32 shorter events, 8.2 us)
Async XLA Ops:
  5.5 30.9 %collective-permute-start.6 = (bf16[4112,256]{1,0:T(8,128)(2,1)S(1)}, bf16[4112,256]{1,0:T(8,128)(2,1)S(1)}, u32[]{:S(2)}, u32[]{:S(2)}) collective-permute-start(bf16[4112,256]{1,0:T(8,128)(2,1)S(1)} %get-tuple-element.18.sent_a), channel_id=1, source_target_pairs={{0,32},{1,9},{2,34},{3,11},{4,36},{5,13},{6,38},{7,15},{8,40},{9,1... | collective-permute-start | bytes 6316040 | tf_op jit(solution)/shard_map/ppermute | solution.py:41
  7.0 33.0 %collective-permute-start.10 = (bf16[4112,256]{1,0:T(8,128)(2,1)S(1)}, bf16[4112,256]{1,0:T(8,128)(2,1)S(1)}, u32[]{:S(2)}, u32[]{:S(2)}) collective-permute-start(bf16[4112,256]{1,0:T(8,128)(2,1)S(1)} %get-tuple-element.19.sent_b), channel_id=1, source_target_pairs={{0,96},{1,25},{2,98},{3,27},{4,100},{5,29},{6,102},{7,31},{8,104},... | collective-permute-start | bytes 6316040 | tf_op jit(solution)/shard_map/ppermute | solution.py:41
  9.1 1.2 %collective-permute-start = (f32[8,128]{1,0:T(8,128)S(1)}, f32[8,128]{1,0:T(8,128)S(1)}, u32[]{:S(2)}, u32[]{:S(2)}) collective-permute-start(f32[8,128]{1,0:T(8,128)S(1)} %get-tuple-element.13), channel_id=1, source_target_pairs={{0,1},{1,0},{2,3},{3,2},{4,5},{5,4},{6,7},{7,6},{8,9},{9,8},{10,11... | collective-permute-start | bytes 12296 | tf_op jit(solution)/shard_map/ppermute | solution.py:41
  10.3 6.2 %slice-start = ((s8[8388608]{0:T(1024)(128)(4,1)}), s8[4194304]{0:T(1024)(128)(4,1)S(1)}, s32[]{:S(2)}) async-start(s8[8388608]{0:T(1024)(128)(4,1)} %bitcast.12), calls=%async_computation | async-start | bytes 8388608
  10.3 6.2 %slice-start.1 = ((s8[8388608]{0:T(1024)(128)(4,1)}), s8[4194304]{0:T(1024)(128)(4,1)S(1)}, s32[]{:S(2)}) async-start(s8[8388608]{0:T(1024)(128)(4,1)} %bitcast.12), calls=%async_computation.1 | async-start | bytes 8388608
  10.3 6.2 %collective-permute-start.1 = (f32[8,128]{1,0:T(8,128)S(1)}, f32[8,128]{1,0:T(8,128)S(1)}, u32[]{:S(2)}, u32[]{:S(2)}) collective-permute-start(f32[8,128]{1,0:T(8,128)S(1)} %add.81.total_ref), channel_id=1, source_target_pairs={{0,2},{1,3},{2,0},{3,1},{4,6},{5,7},{6,4},{7,5},{8,10},{9,11},{10,... | collective-permute-start | bytes 12296 | tf_op jit(solution)/shard_map/ppermute | solution.py:41
  22.8 1.6 %collective-permute-start.2 = (f32[256,256]{1,0:T(8,128)S(1)}, f32[256,256]{1,0:T(8,128)S(1)}, u32[]{:S(2)}, u32[]{:S(2)}) collective-permute-start(f32[256,256]{1,0:T(8,128)S(1)} %get-tuple-element.20), channel_id=1, source_target_pairs={{0,1},{1,0},{2,3},{3,2},{4,5},{5,4},{6,7},{7,6},{8,9},{9,8},{10,11... | collective-permute-start | bytes 786440 | tf_op jit(solution)/shard_map/ppermute | solution.py:41
  24.5 5.6 %collective-permute-start.3 = (bf16[256,256]{1,0:T(8,128)(2,1)S(1)}, bf16[256,256]{1,0:T(8,128)(2,1)S(1)}, u32[]{:S(2)}, u32[]{:S(2)}) collective-permute-start(bf16[256,256]{1,0:T(8,128)(2,1)S(1)} %add_convert_fusion.1), channel_id=1, source_target_pairs={{0,2},{1,3},{2,0},{3,1},{4,6},{5,7},{6,4},{7,5},{8,10},{9,11},{10,... | collective-permute-start | bytes 393224 | tf_op jit(solution)/shard_map/ppermute | solution.py:41
  30.1 6.3 %collective-permute-start.5 = (bf16[256,256]{1,0:T(8,128)(2,1)S(1)}, bf16[256,256]{1,0:T(8,128)(2,1)S(1)}, u32[]{:S(2)}, u32[]{:S(2)}) collective-permute-start(bf16[256,256]{1,0:T(8,128)(2,1)S(1)} %add_convert_fusion.y_own_ref), channel_id=1, source_target_pairs={{0,96},{1,25},{2,98},{3,27},{4,100},{5,29},{6,102},{7,31},{8,104},... | collective-permute-start | bytes 393224 | tf_op jit(solution)/shard_map/ppermute | solution.py:41
  31.3 5.0 %collective-permute-start.4 = (bf16[256,256]{1,0:T(8,128)(2,1)S(1)}, bf16[256,256]{1,0:T(8,128)(2,1)S(1)}, u32[]{:S(2)}, u32[]{:S(2)}) collective-permute-start(bf16[256,256]{1,0:T(8,128)(2,1)S(1)} %add_convert_fusion.y_own_ref), channel_id=1, source_target_pairs={{0,32},{1,9},{2,34},{3,11},{4,36},{5,13},{6,38},{7,15},{8,40},{9,1... | collective-permute-start | bytes 393224 | tf_op jit(solution)/shard_map/ppermute | solution.py:41
  37.9 16.1 %collective-permute-start.7 = (bf16[8,256,256]{2,1,0:T(8,128)(2,1)S(1)}, bf16[8,256,256]{2,1,0:T(8,128)(2,1)S(1)}, u32[]{:S(2)}, u32[]{:S(2)}) collective-permute-start(bf16[8,256,256]{2,1,0:T(8,128)(2,1)S(1)} %shard_map.73), channel_id=1, source_target_pairs={{0,96},{1,25},{2,98},{3,27},{4,100},{5,29},{6,102},{7,31},{8,104},... | collective-permute-start | bytes 3145736 | tf_op jit(solution)/shard_map/ppermute | solution.py:41
  41.6 17.2 %collective-permute-start.11 = (bf16[8,256,256]{2,1,0:T(8,128)(2,1)S(1)}, bf16[8,256,256]{2,1,0:T(8,128)(2,1)S(1)}, u32[]{:S(2)}, u32[]{:S(2)}) collective-permute-start(bf16[8,256,256]{2,1,0:T(8,128)(2,1)S(1)} %shard_map.75), channel_id=1, source_target_pairs={{0,32},{1,9},{2,34},{3,11},{4,36},{5,13},{6,38},{7,15},{8,40},{9,1... | collective-permute-start | bytes 3145736 | tf_op jit(solution)/shard_map/ppermute | solution.py:41
  54.2 9.3 %collective-permute-start.8 = (bf16[4,256,256]{2,1,0:T(8,128)(2,1)S(1)}, bf16[4,256,256]{2,1,0:T(8,128)(2,1)S(1)}, u32[]{:S(2)}, u32[]{:S(2)}) collective-permute-start(bf16[4,256,256]{2,1,0:T(8,128)(2,1)S(1)} %fusion.1), channel_id=1, source_target_pairs={{0,8},{1,33},{2,10},{3,35},{4,12},{5,37},{6,14},{7,39},{8,0},{9,41... | collective-permute-start | bytes 1572872 | tf_op jit(solution)/shard_map/ppermute | solution.py:41
  58.9 10.5 %collective-permute-start.12 = (bf16[4,256,256]{2,1,0:T(8,128)(2,1)S(1)}, bf16[4,256,256]{2,1,0:T(8,128)(2,1)S(1)}, u32[]{:S(2)}, u32[]{:S(2)}) collective-permute-start(bf16[4,256,256]{2,1,0:T(8,128)(2,1)S(1)} %fusion), channel_id=1, source_target_pairs={{0,24},{1,97},{2,26},{3,99},{4,28},{5,101},{6,30},{7,103},{8,16},{... | collective-permute-start | bytes 1572872 | tf_op jit(solution)/shard_map/ppermute | solution.py:41
  63.5 8.7 %collective-permute-start.9 = (bf16[2,256,256]{2,1,0:T(8,128)(2,1)S(1)}, bf16[2,256,256]{2,1,0:T(8,128)(2,1)S(1)}, u32[]{:S(2)}, u32[]{:S(2)}) collective-permute-start(bf16[2,256,256]{2,1,0:T(8,128)(2,1)S(1)} %fusion.5), channel_id=1, source_target_pairs={{0,24},{1,97},{2,26},{3,99},{4,28},{5,101},{6,30},{7,103},{8,16},{... | collective-permute-start | bytes 786440 | tf_op jit(solution)/shard_map/ppermute | solution.py:41
  69.5 6.5 %collective-permute-start.13 = (bf16[2,256,256]{2,1,0:T(8,128)(2,1)S(1)}, bf16[2,256,256]{2,1,0:T(8,128)(2,1)S(1)}, u32[]{:S(2)}, u32[]{:S(2)}) collective-permute-start(bf16[2,256,256]{2,1,0:T(8,128)(2,1)S(1)} %fusion.3), channel_id=1, source_target_pairs={{0,8},{1,33},{2,10},{3,35},{4,12},{5,37},{6,14},{7,39},{8,0},{9,41... | collective-permute-start | bytes 786440 | tf_op jit(solution)/shard_map/ppermute | solution.py:41
  76.1 8.3 %collective-permute-start.14 = (bf16[2,256,256]{2,1,0:T(8,128)(2,1)S(1)}, bf16[2,256,256]{2,1,0:T(8,128)(2,1)S(1)}, u32[]{:S(2)}, u32[]{:S(2)}) collective-permute-start(bf16[2,256,256]{2,1,0:T(8,128)(2,1)S(1)} %shard_map.76), channel_id=1, source_target_pairs={{0,4},{1,5},{2,6},{3,7},{4,0},{5,1},{6,2},{7,3},{8,12},{9,13},{10,... | collective-permute-start | bytes 786440 | tf_op jit(solution)/shard_map/ppermute | solution.py:41

commit v3 on v2

--- a/solution.py
+++ b/solution.py
@@ -51,12 +51,7 @@
 
 
 def slots(g, part):
-    out = []
-    for i in range(2):
-        for j in range(4):
-            for k in range(2):
-                out.append(((NEAR[g] if part else 0) ^ (FAR[g] * i), (FAR[g] * (j & 1)) ^ (NEAR[g] * (j >> 1)), k))
-    return out
+    return [((NEAR[g] if part else 0) ^ (FAR[g] * i), e, k) for i in range(2) for k in (1, 0) for e in range(4)]
 
 
 def params(mib):
@@ -141,10 +136,15 @@
     return jnp.concatenate([ref[pl.ds(2 * block, 1), :], ref[pl.ds(2 * block + 1, 1), :]], axis=1)
 
 
+def whole_total(a_ref, b_ref):
+    both = a_ref[0:1, :] + b_ref[0:1, :]
+    return jnp.concatenate([both, both], axis=1)
+
+
 def forward_kernel(total_ref, other_ref, inv_ref, power_ref, shrink_ref, kept_ref, sent_a, sent_b, probes_ref,
                    tile_ref, y_ref, acc_ref, work_ref):
     r, core = place()
-    total = total_ref[0, 0] + other_ref[0, 0]
+    total = whole_total(total_ref, other_ref)
     rows = inv_ref.shape[0]
     acc_ref[...] = jnp.zeros_like(acc_ref)
     for g, sent_ref in enumerate((sent_a, sent_b)):
@@ -172,87 +172,127 @@
 
 def forward(total, other, inv_row, power, shrink, kept, sent, probes):
     rows, width = inv_row.shape[0], probes.shape[1]
-    vmem, smem = spec(pltpu.VMEM), spec(pltpu.SMEM)
+    vmem = spec(pltpu.VMEM)
     return pl.pallas_call(
         forward_kernel,
-        in_specs=[smem, smem] + [vmem] * 7,
+        in_specs=[vmem] * 9,
         out_specs=[vmem, vmem],
         scratch_shapes=[pltpu.VMEM((rows, width), F32), pltpu.VMEM((STEP, rows, W), BF16)],
         out_shape=(jax.ShapeDtypeStruct((32, rows, W), BF16), jax.ShapeDtypeStruct((width, rows), F32)),
-        compiler_params=params(4),
+        compiler_params=params(6),
         cost_estimate=pl.CostEstimate(flops=1 << 31, bytes_accessed=28 << 20, transcendentals=1 << 22),
     )(total, other, inv_row, power, shrink, kept, *sent, probes)
 
 
-def back_kernel(group, half, total_ref, other_ref, power_ref, shrink_ref, y_own_ref, y_other_ref, tile_ref, count_ref,
-                z_ref, work_ref, inv_ref):
+def other_kernel(group, total_ref, other_ref, power_ref, shrink_ref, count_ref, tile_ref, inv_ref):
     r, core = place()
-    total = total_ref[0, 0] + other_ref[0, 0]
+    total = whole_total(total_ref, other_ref)
     rows = tile_ref.shape[1]
     tail = count_ref[16 * W:16 * W + 16, :].astype(F32)
     marg = tail[0:1, :] + tail[1:2, :] * 64.0 + tail[2:3, :] * 4096.0
     inv_ref[...] = 1.0 / jnp.transpose(jnp.broadcast_to(marg, (128, rows)))
+
+    @pl.loop(0, 2)
+    def _(i):
+        for n, (d, e, k) in enumerate(slots(group, 0)[:8]):
+            block = block_of(r, core, group, d ^ (FAR[group] * i), e, k)
+            shrink = column_terms(shrink_ref, block)
+            scale = column_terms(power_ref, block) * total
+            s = 8 * i + n
+            base = pl.multiple_of(s * rows, rows)
+            for q in range(0, rows, 32):
+                tile_ref[s, q:q + 32, :] = tile_rows(count_ref[pl.ds(base + q, 32), :], shrink, scale, inv_ref[q:q + 32, :])
+
+
+def other_tile(group, total, other, power, shrink, received):
+    vmem = spec(pltpu.VMEM)
+    return pl.pallas_call(
+        functools.partial(other_kernel, group),
+        in_specs=[vmem] * 5,
+        out_specs=vmem,
+        scratch_shapes=[pltpu.VMEM((W, 128), F32)],
+        out_shape=jax.ShapeDtypeStruct((16, W, W), BF16),
+        compiler_params=params(4),
+        cost_estimate=pl.CostEstimate(flops=1 << 24, bytes_accessed=4 << 20, transcendentals=1 << 20),
+    )(total, other, power, shrink, received)
+
+
+def back_kernel(base, half, y_own_ref, y_other_ref, own_ref, other_ref, *outs):
     for n in range(8):
-        s = half * 8 + n
-        d, e, k = slots(group, 0)[s]
-        block = block_of(r, core, group, d, e, k)
-        shrink = column_terms(shrink_ref, block)
-        scale = column_terms(power_ref, block) * total
-        for i in range(0, rows, 32):
-            work_ref[n, i:i + 32, :] = tile_rows(
-                count_ref[s * W + i:s * W + i + 32, :], shrink, scale, inv_ref[i:i + 32, :])
-        out = jnp.dot(y_own_ref[...], tile_ref[group * 16 + s], preferred_element_type=F32)
-        out = out + jnp.dot(y_other_ref[...], work_ref[n], preferred_element_type=F32)
-        z_ref[n] = out.astype(z_ref.dtype)
-
-
-def back(total, other, power, shrink, y_own, y_other, tile, received, group, half, dtype):
-    rows, width = tile.shape[1], y_own.shape[0]
-    vmem, smem = spec(pltpu.VMEM), spec(pltpu.SMEM)
-    return pl.pallas_call(
-        functools.partial(back_kernel, group, half),
-        in_specs=[smem, smem] + [vmem] * 6,
+        out = jnp.dot(y_own_ref[...], own_ref[base + half * 8 + n], preferred_element_type=F32)
+        out = out + jnp.dot(y_other_ref[...], other_ref[half * 8 + n], preferred_element_type=F32)
+        outs[n // 4][n % 4] = out.astype(outs[0].dtype)
+
+
+def back(group, half, y_own, y_other, own, other, dtype):
+    vmem = spec(pltpu.VMEM)
+    return pl.pallas_call(
+        functools.partial(back_kernel, group * 16, half),
+        in_specs=[vmem] * 4,
+        out_specs=[vmem] * 2,
+        out_shape=[jax.ShapeDtypeStruct((4, y_own.shape[0], W), dtype)] * 2,
+        compiler_params=params(4),
+        cost_estimate=pl.CostEstimate(flops=1 << 29, bytes_accessed=4 << 20, transcendentals=0),
+    )(y_own, y_other, own, other)
+
+
+def pack_kernel(z_a, r_a, z_b, r_b, own_ref, *outs):
+    for g, (z_ref, r_ref) in enumerate(((z_a, r_a), (z_b, r_b))):
+        for e in range(4):
+            total = z_ref[e] + r_ref[e].astype(F32)
+            if e == 0:
+                own_ref[g] = total
+            else:
+                outs[e - 1][g] = total.astype(BF16)
+
+
+def pack(z, r):
+    vmem = spec(pltpu.VMEM)
+    width = z[0].shape[1]
+    return pl.pallas_call(
+        pack_kernel,
+        in_specs=[vmem] * 4,
+        out_specs=[vmem] * 4,
+        out_shape=[jax.ShapeDtypeStruct((2, width, W), F32)] + [jax.ShapeDtypeStruct((2, width, W), BF16)] * 3,
+        compiler_params=params(4),
+        cost_estimate=pl.CostEstimate(flops=1 << 21, bytes_accessed=4 << 20, transcendentals=0),
+    )(z[0], r[0], z[1], r[1])
+
+
+def fold_kernel(own_ref, a_ref, b_ref, c_ref, out_ref):
+    for g in range(2):
+        total = own_ref[g] + a_ref[g].astype(F32) + b_ref[g].astype(F32) + c_ref[g].astype(F32)
+        out_ref[g] = total.astype(out_ref.dtype)
+
+
+def fold(own, got, dtype):
+    vmem = spec(pltpu.VMEM)
+    return pl.pallas_call(
+        fold_kernel,
+        in_specs=[vmem] * 4,
         out_specs=vmem,
-        scratch_shapes=[pltpu.VMEM((8, rows, W), BF16), pltpu.VMEM((rows, 128), F32)],
-        out_shape=jax.ShapeDtypeStruct((8, width, W), dtype),
-        compiler_params=params(4),
-        cost_estimate=pl.CostEstimate(flops=1 << 29, bytes_accessed=4 << 20, transcendentals=1 << 19),
-    )(total, other, power, shrink, y_own, y_other, tile, received)
-
-
-def pair_kernel(a_ref, b_ref, out_ref):
-    out_ref[0] = a_ref[...]
-    out_ref[1] = b_ref[...]
-
-
-def pair(a, b):
-    vmem = spec(pltpu.VMEM)
-    return pl.pallas_call(
-        pair_kernel,
-        in_specs=[vmem, vmem],
-        out_specs=vmem,
-        out_shape=jax.ShapeDtypeStruct((2,) + a.shape, a.dtype),
-        compiler_params=params(1),
-        cost_estimate=pl.CostEstimate(flops=0, bytes_accessed=1 << 19, transcendentals=0),
-    )(a, b)
-
-
-def last_kernel(factor, a_ref, b_ref, got_ref, z_ref):
-    for g, ref in enumerate((a_ref, b_ref)):
-        z_ref[g * W:(g + 1) * W, :] = jnp.transpose(ref[...] + got_ref[g].astype(F32)) * factor
-
-
-def last(a, b, got, factor):
-    width = a.shape[0]
+        out_shape=jax.ShapeDtypeStruct(own.shape, dtype),
+        compiler_params=params(4),
+        cost_estimate=pl.CostEstimate(flops=1 << 20, bytes_accessed=2 << 20, transcendentals=0),
+    )(own, *got)
+
+
+def last_kernel(factor, own_ref, got_ref, z_ref):
+    for g in range(2):
+        z_ref[g * W:(g + 1) * W, :] = jnp.transpose(own_ref[g] + got_ref[g].astype(F32)) * factor
+
+
+def last(own, got, factor):
+    width = own.shape[1]
     vmem = spec(pltpu.VMEM)
     return pl.pallas_call(
         functools.partial(last_kernel, factor),
-        in_specs=[vmem] * 3,
+        in_specs=[vmem] * 2,
         out_specs=vmem,
         out_shape=jax.ShapeDtypeStruct((2 * W, width), F32),
-        compiler_params=params(2),
+        compiler_params=params(4),
         cost_estimate=pl.CostEstimate(flops=1 << 20, bytes_accessed=2 << 20, transcendentals=0),
-    )(a, b, got)
+    )(own, got)
 
 
 def local(counts, row_marg, ctx_marg, discount, probes):
@@ -265,24 +305,19 @@
     tile, y_part = forward(total, other, inv_row, power, shrink, kept, sent, probes)
     y_chip = (y_part + permute(y_part, CORE_PERM)).astype(BF16)
     y_own = (y_chip.astype(F32) + permute(y_chip, ZL_PERM).astype(F32)).astype(BF16)
-    y_other = lax.optimization_barrier([permute(y_own, u_perm(NEAR[g])) for g in range(2)])
-
-    def run(g, half, dtype):
-        return back(total, other, power, shrink, y_own, y_other[g], tile, received[g], g, half, dtype)
-
-    own, ends = [], []
-    sends = [run(g, 1, BF16) for g in range(2)]
-    for g in range(2):
-        r2 = permute(sends[g], u_perm(FAR[g]))
-        z = run(g, 0, F32)
-        r3 = permute((z[4:8] + r2[4:8].astype(F32)).astype(BF16), v_perm(NEAR[g]))
-        r4 = permute((z[2:4] + r2[2:4].astype(F32) + r3[2:4].astype(F32)).astype(BF16), v_perm(FAR[g]))
-        kept = [z[k] + r2[k].astype(F32) + r3[k].astype(F32) + r4[k].astype(F32) for k in range(2)]
-        own.append(kept[0])
-        ends.append(kept[1].astype(BF16))
-    r5 = permute(pair(*ends), ZH_PERM)
+    y_other = [permute(y_own, u_perm(NEAR[g])) for g in range(2)]
+
+    tiles = [other_tile(g, total, other, power, shrink, received[g]) for g in range(2)]
+    y_other, tiles = lax.optimization_barrier((y_other, tiles))
+    sends = [back(g, 1, y_own, y_other[g], tile, tiles[g], BF16) for g in range(2)]
+    r2 = [[permute(sends[g][c], u_perm(FAR[g])) for g in range(2)] for c in range(2)]
+    z = [back(g, 0, y_own, y_other[g], tile, tiles[g], F32) for g in range(2)]
+    ended = []
+    for c, dtype in enumerate((BF16, F32)):
+        own, *out = pack([z[g][c] for g in range(2)], r2[c])
+        ended.append(fold(own, [permute(out[e - 1], v_perm(e)) for e in (2, 1, 3)], dtype))
     factor = (counts.shape[0] * lax.axis_size("rows")) ** (-0.5)
-    z_proj = last(*own, r5, factor)
+    z_proj = last(ended[1], permute(ended[0], ZH_PERM), factor)
     return (jnp.transpose(y_own), z_proj[None])
 
 

time: 86.3 us -> 74 us (0.86)
  waiting for transfers between devices: 42 us -> 24.4 us
  starting transfers between devices: 18.6 us -> 26 us
  Pallas kernels: 21.6 us -> 20.5 us
    ppermute x15 -> x19, waiting for transfers between devices: 42 us -> 24.4 us  [permute(): return lax.ppermute(a, AXES, perm)]
    ppermute x15 -> x19, starting transfers between devices: 18.6 us -> 26 us  [permute(): return lax.ppermute(a, AXES, perm)]
    pallas_call x6 -> x11, Pallas kernels: 12.5 us -> 11.4 us  [the longest x1 5.71 us: forward(): pl.pallas_call(forward_kernel, in_specs=[vmem] * 9, out_specs=[vmem, vmem...]
  transfers between devices with their start and end apart: 15 -> 19, of which waited for: 11 -> 12; matrix products, arithmetic and copies ran while one was open for 2% -> 1% of each run, Pallas kernels for 20% -> 20%
where the time goes in v3:
time: 74 us; the launch traced here: 73.4 us
  starting transfers between devices  26 us (35%)
  waiting for transfers between devices  24.4 us (33%)
  Pallas kernels  20.5 us (28%)
  other arithmetic  0.98 us (1%)
  between operations  0.79 us (1%)
  local copies, waits for them, and re-layouts  0.77 us (1%)
    ppermute x19, starting transfers between devices, permute(): return lax.ppermute(a, AXES, perm)  26 us
    ppermute x19, waiting for transfers between devices, permute(): return lax.ppermute(a, AXES, perm)  24.4 us
    pallas_call x2, Pallas kernels, prepare(): pl.pallas_call(functools.partial(prepare_kernel, part), in_specs=[spec(pl...  7.9 us
    pallas_call x1, Pallas kernels, forward(): pl.pallas_call(forward_kernel, in_specs=[vmem] * 9, out_specs=[vmem, vmem...  5.71 us
    pallas_call x4, Pallas kernels, back(): pl.pallas_call(functools.partial(back_kernel, group * 16, half), in_specs...  2.84 us
    pallas_call x2, Pallas kernels, other_tile(): pl.pallas_call(functools.partial(other_kernel, group), in_specs=[vmem] *...  2.31 us
  transfers between devices with their start and end apart: 19, of which 12 were waited for; matrix products, arithmetic and copies ran while one was open for 1% of the time, Pallas kernels for 20%

profile of v3, /device:TPU:24, one launch (start us, length us, event | category | flops | bytes accessed | tf_op | source)
XLA Modules:
  0.0 73.4 jit_solution(13146437777808812371)
XLA Ops:
  1.7 3.7 %shard_map.70 = (bf16[4112,256]{1,0:T(8,128)(2,1)S(1)}, bf16[4112,256]{1,0:T(8,128)(2,1)S(1)}) custom-call(bf16[16,256]{1,0:T(8,128)(2,1)S(1)} %get-tuple-element.35.refs_0_, s32[256,16384]{1,0:T(8,128)} %refs_1_.1), custom_call_target="tpu_custom_call" | custom-call | flops 4194304 | bytes 12582912 | tf_op jit(solution)/shard_map/pallas_call | solution.py:118
  5.5 1.6 %collective-permute-start.6 = (bf16[4112,256]{1,0:T(8,128)(2,1)S(1)}, bf16[4112,256]{1,0:T(8,128)(2,1)S(1)}, u32[]{:S(2)}, u32[]{:S(2)}) collective-permute-start(bf16[4112,256]{1,0:T(8,128)(2,1)S(1)} %get-tuple-element.36.sent_a), channel_id=1, source_target_pairs={{0,32},{1,9},{2,34},{3,11},{4,36},{5,13},{6,38},{7,15},{8,40},{9,1... | collective-permute-start | bytes 6316040 | tf_op jit(solution)/shard_map/ppermute | solution.py:41
  7.0 2.1 %collective-permute-start.7 = (bf16[4112,256]{1,0:T(8,128)(2,1)S(1)}, bf16[4112,256]{1,0:T(8,128)(2,1)S(1)}, u32[]{:S(2)}, u32[]{:S(2)}) collective-permute-start(bf16[4112,256]{1,0:T(8,128)(2,1)S(1)} %get-tuple-element.37.sent_b), channel_id=1, source_target_pairs={{0,96},{1,25},{2,98},{3,27},{4,100},{5,29},{6,102},{7,31},{8,104},... | collective-permute-start | bytes 6316040 | tf_op jit(solution)/shard_map/ppermute | solution.py:41
  10.3 2.0 %collective-permute-start.1 = (f32[8,128]{1,0:T(8,128)S(1)}, f32[8,128]{1,0:T(8,128)S(1)}, u32[]{:S(2)}, u32[]{:S(2)}) collective-permute-start(f32[8,128]{1,0:T(8,128)S(1)} %add.9.total_ref), channel_id=1, source_target_pairs={{0,2},{1,3},{2,0},{3,1},{4,6},{5,7},{6,4},{7,5},{8,10},{9,11},{10,... | collective-permute-start | bytes 12296 | tf_op jit(solution)/shard_map/ppermute | solution.py:41
  12.3 4.2 %shard_map.69.kept_ref = bf16[8192,256]{1,0:T(8,128)(2,1)S(1)} custom-call(s32[256,16384]{1,0:T(8,128)} %refs_1_.1), custom_call_target="tpu_custom_call" | custom-call | flops 4194304 | bytes 12582912 | tf_op jit(solution)/shard_map/pallas_call | solution.py:118
  16.5 5.7 %shard_map.71 = (bf16[32,256,256]{2,1,0:T(8,128)(2,1)S(1)}, f32[256,256]{1,0:T(8,128)S(1)}) custom-call(f32[8,128]{1,0:T(8,128)S(1)} %add.9.total_ref, f32[8,128]{1,0:T(8,128)S(1)} %collective-permute-done.1.other_ref, f32[256,128]{1,0:T(8,128)S(1)} %get-tuple-element.32.inv_ref, f32[128,128]{1,0:T(8,128)S(1)} %get-tuple-element.33.power_ref, ...), custom_call_target="tpu_custom_call" | custom-call | flops 2147483648 | bytes 29360128 | tf_op jit(solution)/shard_map/pallas_call | solution.py:176
  22.4 1.4 %collective-permute-done.2 = f32[256,256]{1,0:T(8,128)S(1)} collective-permute-done((f32[256,256]{1,0:T(8,128)S(1)}, f32[256,256]{1,0:T(8,128)S(1)}, u32[]{:S(2)}, u32[]{:S(2)}) %collective-permute-start.2) | collective-permute-done | bytes 262176 | tf_op jit(solution)/shard_map/ppermute | solution.py:41
  23.9 1.8 %collective-permute-start.3 = (bf16[256,256]{1,0:T(8,128)(2,1)S(1)}, bf16[256,256]{1,0:T(8,128)(2,1)S(1)}, u32[]{:S(2)}, u32[]{:S(2)}) collective-permute-start(bf16[256,256]{1,0:T(8,128)(2,1)S(1)} %add_convert_fusion.1), channel_id=1, source_target_pairs={{0,2},{1,3},{2,0},{3,1},{4,6},{5,7},{6,4},{7,5},{8,10},{9,11},{10,... | collective-permute-start | bytes 393224 | tf_op jit(solution)/shard_map/ppermute | solution.py:41
  25.7 3.8 %collective-permute-done.3 = bf16[256,256]{1,0:T(8,128)(2,1)S(1)} collective-permute-done((bf16[256,256]{1,0:T(8,128)(2,1)S(1)}, bf16[256,256]{1,0:T(8,128)(2,1)S(1)}, u32[]{:S(2)}, u32[]{:S(2)}) %collective-permute-start.3) | collective-permute-done | bytes 131104 | tf_op jit(solution)/shard_map/ppermute | solution.py:41
  29.5 1.2 %collective-permute-start.5 = (bf16[256,256]{1,0:T(8,128)(2,1)S(1)}, bf16[256,256]{1,0:T(8,128)(2,1)S(1)}, u32[]{:S(2)}, u32[]{:S(2)}) collective-permute-start(bf16[256,256]{1,0:T(8,128)(2,1)S(1)} %add_convert_fusion.y_own_ref), channel_id=1, source_target_pairs={{0,96},{1,25},{2,98},{3,27},{4,100},{5,29},{6,102},{7,31},{8,104},... | collective-permute-start | bytes 393224 | tf_op jit(solution)/shard_map/ppermute | solution.py:41
  32.8 1.5 %collective-permute-done.7.count_ref = bf16[4112,256]{1,0:T(8,128)(2,1)S(1)} collective-permute-done((bf16[4112,256]{1,0:T(8,128)(2,1)S(1)}, bf16[4112,256]{1,0:T(8,128)(2,1)S(1)}, u32[]{:S(2)}, u32[]{:S(2)}) %collective-permute-start.7) | collective-permute-done | bytes 2105376 | tf_op jit(solution)/shard_map/ppermute | solution.py:41
  36.5 2.1 %collective-permute-start.13 = (bf16[4,256,256]{2,1,0:T(8,128)(2,1)S(1)}, bf16[4,256,256]{2,1,0:T(8,128)(2,1)S(1)}, u32[]{:S(2)}, u32[]{:S(2)}) collective-permute-start(bf16[4,256,256]{2,1,0:T(8,128)(2,1)S(1)} %get-tuple-element.53), channel_id=1, source_target_pairs={{0,96},{1,25},{2,98},{3,27},{4,100},{5,29},{6,102},{7,31},{8,104},... | collective-permute-start | bytes 1572872 | tf_op jit(solution)/shard_map/ppermute | solution.py:41
  39.5 1.2 %collective-permute-start.8 = (bf16[4,256,256]{2,1,0:T(8,128)(2,1)S(1)}, bf16[4,256,256]{2,1,0:T(8,128)(2,1)S(1)}, u32[]{:S(2)}, u32[]{:S(2)}) collective-permute-start(bf16[4,256,256]{2,1,0:T(8,128)(2,1)S(1)} %get-tuple-element.43), channel_id=1, source_target_pairs={{0,96},{1,25},{2,98},{3,27},{4,100},{5,29},{6,102},{7,31},{8,104},... | collective-permute-start | bytes 1572872 | tf_op jit(solution)/shard_map/ppermute | solution.py:41
  40.7 1.3 %collective-permute-start.9 = (bf16[4,256,256]{2,1,0:T(8,128)(2,1)S(1)}, bf16[4,256,256]{2,1,0:T(8,128)(2,1)S(1)}, u32[]{:S(2)}, u32[]{:S(2)}) collective-permute-start(bf16[4,256,256]{2,1,0:T(8,128)(2,1)S(1)} %get-tuple-element.47), channel_id=1, source_target_pairs={{0,32},{1,9},{2,34},{3,11},{4,36},{5,13},{6,38},{7,15},{8,40},{9,1... | collective-permute-start | bytes 1572872 | tf_op jit(solution)/shard_map/ppermute | solution.py:41
  43.5 3.5 %collective-permute-done.13.r_a = bf16[4,256,256]{2,1,0:T(8,128)(2,1)S(1)} collective-permute-done((bf16[4,256,256]{2,1,0:T(8,128)(2,1)S(1)}, bf16[4,256,256]{2,1,0:T(8,128)(2,1)S(1)}, u32[]{:S(2)}, u32[]{:S(2)}) %collective-permute-start.13) | collective-permute-done | bytes 524320 | tf_op jit(solution)/shard_map/ppermute | solution.py:41
  47.0 1.7 %collective-permute-done.14.r_b = bf16[4,256,256]{2,1,0:T(8,128)(2,1)S(1)} collective-permute-done((bf16[4,256,256]{2,1,0:T(8,128)(2,1)S(1)}, bf16[4,256,256]{2,1,0:T(8,128)(2,1)S(1)}, u32[]{:S(2)}, u32[]{:S(2)}) %collective-permute-start.14) | collective-permute-done | bytes 524320 | tf_op jit(solution)/shard_map/ppermute | solution.py:41
  48.8 1.3 %collective-permute-start.15 = (bf16[2,256,256]{2,1,0:T(8,128)(2,1)S(1)}, bf16[2,256,256]{2,1,0:T(8,128)(2,1)S(1)}, u32[]{:S(2)}, u32[]{:S(2)}) collective-permute-start(bf16[2,256,256]{2,1,0:T(8,128)(2,1)S(1)} %get-tuple-element.57), channel_id=1, source_target_pairs={{0,16},{1,65},{2,18},{3,67},{4,20},{5,69},{6,22},{7,71},{8,24},{9,... | collective-permute-start | bytes 786440 | tf_op jit(solution)/shard_map/ppermute | solution.py:41
  50.1 2.9 %collective-permute-start.17 = (bf16[2,256,256]{2,1,0:T(8,128)(2,1)S(1)}, bf16[2,256,256]{2,1,0:T(8,128)(2,1)S(1)}, u32[]{:S(2)}, u32[]{:S(2)}) collective-permute-start(bf16[2,256,256]{2,1,0:T(8,128)(2,1)S(1)} %get-tuple-element.59), channel_id=1, source_target_pairs={{0,24},{1,97},{2,26},{3,99},{4,28},{5,101},{6,30},{7,103},{8,16},{... | collective-permute-start | bytes 786440 | tf_op jit(solution)/shard_map/ppermute | solution.py:41
  53.0 4.2 %collective-permute-done.8.r_a = bf16[4,256,256]{2,1,0:T(8,128)(2,1)S(1)} collective-permute-done((bf16[4,256,256]{2,1,0:T(8,128)(2,1)S(1)}, bf16[4,256,256]{2,1,0:T(8,128)(2,1)S(1)}, u32[]{:S(2)}, u32[]{:S(2)}) %collective-permute-start.8) | collective-permute-done | bytes 524320 | tf_op jit(solution)/shard_map/ppermute | solution.py:41
  57.2 2.4 %collective-permute-done.9.r_b = bf16[4,256,256]{2,1,0:T(8,128)(2,1)S(1)} collective-permute-done((bf16[4,256,256]{2,1,0:T(8,128)(2,1)S(1)}, bf16[4,256,256]{2,1,0:T(8,128)(2,1)S(1)}, u32[]{:S(2)}, u32[]{:S(2)}) %collective-permute-start.9) | collective-permute-done | bytes 524320 | tf_op jit(solution)/shard_map/ppermute | solution.py:41
  61.1 2.8 %collective-permute-start.12 = (bf16[2,256,256]{2,1,0:T(8,128)(2,1)S(1)}, bf16[2,256,256]{2,1,0:T(8,128)(2,1)S(1)}, u32[]{:S(2)}, u32[]{:S(2)}) collective-permute-start(bf16[2,256,256]{2,1,0:T(8,128)(2,1)S(1)} %get-tuple-element.51), channel_id=1, source_target_pairs={{0,24},{1,97},{2,26},{3,99},{4,28},{5,101},{6,30},{7,103},{8,16},{... | collective-permute-start | bytes 786440 | tf_op jit(solution)/shard_map/ppermute | solution.py:41
  64.1 4.0 %collective-permute-start.18 = (bf16[2,256,256]{2,1,0:T(8,128)(2,1)S(1)}, bf16[2,256,256]{2,1,0:T(8,128)(2,1)S(1)}, u32[]{:S(2)}, u32[]{:S(2)}) collective-permute-start(bf16[2,256,256]{2,1,0:T(8,128)(2,1)S(1)} %shard_map.81), channel_id=1, source_target_pairs={{0,4},{1,5},{2,6},{3,7},{4,0},{5,1},{6,2},{7,3},{8,12},{9,13},{10,... | collective-permute-start | bytes 786440 | tf_op jit(solution)/shard_map/ppermute | solution.py:41
  68.8 1.7 %collective-permute-done.12.c_ref = bf16[2,256,256]{2,1,0:T(8,128)(2,1)S(1)} collective-permute-done((bf16[2,256,256]{2,1,0:T(8,128)(2,1)S(1)}, bf16[2,256,256]{2,1,0:T(8,128)(2,1)S(1)}, u32[]{:S(2)}, u32[]{:S(2)}) %collective-permute-start.12) | collective-permute-done | bytes 262176 | tf_op jit(solution)/shard_map/ppermute | solution.py:41
  70.6 1.7 %collective-permute-done.18.got_ref = bf16[2,256,256]{2,1,0:T(8,128)(2,1)S(1)} collective-permute-done((bf16[2,256,256]{2,1,0:T(8,128)(2,1)S(1)}, bf16[2,256,256]{2,1,0:T(8,128)(2,1)S(1)}, u32[]{:S(2)}, u32[]{:S(2)}) %collective-permute-start.18) | collective-permute-done | bytes 262176 | tf_op jit(solution)/shard_map/ppermute | solution.py:41
  (39 shorter events, 12.6 us)
Async XLA Ops:
  5.5 26.2 %collective-permute-start.6 = (bf16[4112,256]{1,0:T(8,128)(2,1)S(1)}, bf16[4112,256]{1,0:T(8,128)(2,1)S(1)}, u32[]{:S(2)}, u32[]{:S(2)}) collective-permute-start(bf16[4112,256]{1,0:T(8,128)(2,1)S(1)} %get-tuple-element.36.sent_a), channel_id=1, source_target_pairs={{0,32},{1,9},{2,34},{3,11},{4,36},{5,13},{6,38},{7,15},{8,40},{9,1... | collective-permute-start | bytes 6316040 | tf_op jit(solution)/shard_map/ppermute | solution.py:41
  7.0 27.3 %collective-permute-start.7 = (bf16[4112,256]{1,0:T(8,128)(2,1)S(1)}, bf16[4112,256]{1,0:T(8,128)(2,1)S(1)}, u32[]{:S(2)}, u32[]{:S(2)}) collective-permute-start(bf16[4112,256]{1,0:T(8,128)(2,1)S(1)} %get-tuple-element.37.sent_b), channel_id=1, source_target_pairs={{0,96},{1,25},{2,98},{3,27},{4,100},{5,29},{6,102},{7,31},{8,104},... | collective-permute-start | bytes 6316040 | tf_op jit(solution)/shard_map/ppermute | solution.py:41
  9.1 1.2 %collective-permute-start = (f32[8,128]{1,0:T(8,128)S(1)}, f32[8,128]{1,0:T(8,128)S(1)}, u32[]{:S(2)}, u32[]{:S(2)}) collective-permute-start(f32[8,128]{1,0:T(8,128)S(1)} %get-tuple-element.31), channel_id=1, source_target_pairs={{0,1},{1,0},{2,3},{3,2},{4,5},{5,4},{6,7},{7,6},{8,9},{9,8},{10,11... | collective-permute-start | bytes 12296 | tf_op jit(solution)/shard_map/ppermute | solution.py:41
  10.3 6.2 %slice-start = ((s8[8388608]{0:T(1024)(128)(4,1)}), s8[4194304]{0:T(1024)(128)(4,1)S(1)}, s32[]{:S(2)}) async-start(s8[8388608]{0:T(1024)(128)(4,1)} %bitcast.4), calls=%async_computation | async-start | bytes 8388608
  10.3 6.2 %slice-start.1 = ((s8[8388608]{0:T(1024)(128)(4,1)}), s8[4194304]{0:T(1024)(128)(4,1)S(1)}, s32[]{:S(2)}) async-start(s8[8388608]{0:T(1024)(128)(4,1)} %bitcast.4), calls=%async_computation.1 | async-start | bytes 8388608
  10.3 6.2 %collective-permute-start.1 = (f32[8,128]{1,0:T(8,128)S(1)}, f32[8,128]{1,0:T(8,128)S(1)}, u32[]{:S(2)}, u32[]{:S(2)}) collective-permute-start(f32[8,128]{1,0:T(8,128)S(1)} %add.9.total_ref), channel_id=1, source_target_pairs={{0,2},{1,3},{2,0},{3,1},{4,6},{5,7},{6,4},{7,5},{8,10},{9,11},{10,... | collective-permute-start | bytes 12296 | tf_op jit(solution)/shard_map/ppermute | solution.py:41
  22.2 1.6 %collective-permute-start.2 = (f32[256,256]{1,0:T(8,128)S(1)}, f32[256,256]{1,0:T(8,128)S(1)}, u32[]{:S(2)}, u32[]{:S(2)}) collective-permute-start(f32[256,256]{1,0:T(8,128)S(1)} %get-tuple-element.38), channel_id=1, source_target_pairs={{0,1},{1,0},{2,3},{3,2},{4,5},{5,4},{6,7},{7,6},{8,9},{9,8},{10,11... | collective-permute-start | bytes 786440 | tf_op jit(solution)/shard_map/ppermute | solution.py:41
  23.9 5.6 %collective-permute-start.3 = (bf16[256,256]{1,0:T(8,128)(2,1)S(1)}, bf16[256,256]{1,0:T(8,128)(2,1)S(1)}, u32[]{:S(2)}, u32[]{:S(2)}) collective-permute-start(bf16[256,256]{1,0:T(8,128)(2,1)S(1)} %add_convert_fusion.1), channel_id=1, source_target_pairs={{0,2},{1,3},{2,0},{3,1},{4,6},{5,7},{6,4},{7,5},{8,10},{9,11},{10,... | collective-permute-start | bytes 393224 | tf_op jit(solution)/shard_map/ppermute | solution.py:41
  29.5 6.3 %collective-permute-start.5 = (bf16[256,256]{1,0:T(8,128)(2,1)S(1)}, bf16[256,256]{1,0:T(8,128)(2,1)S(1)}, u32[]{:S(2)}, u32[]{:S(2)}) collective-permute-start(bf16[256,256]{1,0:T(8,128)(2,1)S(1)} %add_convert_fusion.y_own_ref), channel_id=1, source_target_pairs={{0,96},{1,25},{2,98},{3,27},{4,100},{5,29},{6,102},{7,31},{8,104},... | collective-permute-start | bytes 393224 | tf_op jit(solution)/shard_map/ppermute | solution.py:41
  30.8 5.0 %collective-permute-start.4 = (bf16[256,256]{1,0:T(8,128)(2,1)S(1)}, bf16[256,256]{1,0:T(8,128)(2,1)S(1)}, u32[]{:S(2)}, u32[]{:S(2)}) collective-permute-start(bf16[256,256]{1,0:T(8,128)(2,1)S(1)} %add_convert_fusion.y_own_ref), channel_id=1, source_target_pairs={{0,32},{1,9},{2,34},{3,11},{4,36},{5,13},{6,38},{7,15},{8,40},{9,1... | collective-permute-start | bytes 393224 | tf_op jit(solution)/shard_map/ppermute | solution.py:41
  36.5 10.5 %collective-permute-start.13 = (bf16[4,256,256]{2,1,0:T(8,128)(2,1)S(1)}, bf16[4,256,256]{2,1,0:T(8,128)(2,1)S(1)}, u32[]{:S(2)}, u32[]{:S(2)}) collective-permute-start(bf16[4,256,256]{2,1,0:T(8,128)(2,1)S(1)} %get-tuple-element.53), channel_id=1, source_target_pairs={{0,96},{1,25},{2,98},{3,27},{4,100},{5,29},{6,102},{7,31},{8,104},... | collective-permute-start | bytes 1572872 | tf_op jit(solution)/shard_map/ppermute | solution.py:41
  39.4 9.3 %collective-permute-start.14 = (bf16[4,256,256]{2,1,0:T(8,128)(2,1)S(1)}, bf16[4,256,256]{2,1,0:T(8,128)(2,1)S(1)}, u32[]{:S(2)}, u32[]{:S(2)}) collective-permute-start(bf16[4,256,256]{2,1,0:T(8,128)(2,1)S(1)} %get-tuple-element.55), channel_id=1, source_target_pairs={{0,32},{1,9},{2,34},{3,11},{4,36},{5,13},{6,38},{7,15},{8,40},{9,1... | collective-permute-start | bytes 1572872 | tf_op jit(solution)/shard_map/ppermute | solution.py:41
  39.5 17.7 %collective-permute-start.8 = (bf16[4,256,256]{2,1,0:T(8,128)(2,1)S(1)}, bf16[4,256,256]{2,1,0:T(8,128)(2,1)S(1)}, u32[]{:S(2)}, u32[]{:S(2)}) collective-permute-start(bf16[4,256,256]{2,1,0:T(8,128)(2,1)S(1)} %get-tuple-element.43), channel_id=1, source_target_pairs={{0,96},{1,25},{2,98},{3,27},{4,100},{5,29},{6,102},{7,31},{8,104},... | collective-permute-start | bytes 1572872 | tf_op jit(solution)/shard_map/ppermute | solution.py:41
  40.7 18.9 %collective-permute-start.9 = (bf16[4,256,256]{2,1,0:T(8,128)(2,1)S(1)}, bf16[4,256,256]{2,1,0:T(8,128)(2,1)S(1)}, u32[]{:S(2)}, u32[]{:S(2)}) collective-permute-start(bf16[4,256,256]{2,1,0:T(8,128)(2,1)S(1)} %get-tuple-element.47), channel_id=1, source_target_pairs={{0,32},{1,9},{2,34},{3,11},{4,36},{5,13},{6,38},{7,15},{8,40},{9,1... | collective-permute-start | bytes 1572872 | tf_op jit(solution)/shard_map/ppermute | solution.py:41
  48.8 12.3 %collective-permute-start.15 = (bf16[2,256,256]{2,1,0:T(8,128)(2,1)S(1)}, bf16[2,256,256]{2,1,0:T(8,128)(2,1)S(1)}, u32[]{:S(2)}, u32[]{:S(2)}) collective-permute-start(bf16[2,256,256]{2,1,0:T(8,128)(2,1)S(1)} %get-tuple-element.57), channel_id=1, source_target_pairs={{0,16},{1,65},{2,18},{3,67},{4,20},{5,69},{6,22},{7,71},{8,24},{9,... | collective-permute-start | bytes 786440 | tf_op jit(solution)/shard_map/ppermute | solution.py:41
  50.1 13.8 %collective-permute-start.16 = (bf16[2,256,256]{2,1,0:T(8,128)(2,1)S(1)}, bf16[2,256,256]{2,1,0:T(8,128)(2,1)S(1)}, u32[]{:S(2)}, u32[]{:S(2)}) collective-permute-start(bf16[2,256,256]{2,1,0:T(8,128)(2,1)S(1)} %get-tuple-element.58), channel_id=1, source_target_pairs={{0,8},{1,33},{2,10},{3,35},{4,12},{5,37},{6,14},{7,39},{8,0},{9,41... | collective-permute-start | bytes 786440 | tf_op jit(solution)/shard_map/ppermute | solution.py:41
  50.1 13.8 %collective-permute-start.17 = (bf16[2,256,256]{2,1,0:T(8,128)(2,1)S(1)}, bf16[2,256,256]{2,1,0:T(8,128)(2,1)S(1)}, u32[]{:S(2)}, u32[]{:S(2)}) collective-permute-start(bf16[2,256,256]{2,1,0:T(8,128)(2,1)S(1)} %get-tuple-element.59), channel_id=1, source_target_pairs={{0,24},{1,97},{2,26},{3,99},{4,28},{5,101},{6,30},{7,103},{8,16},{... | collective-permute-start | bytes 786440 | tf_op jit(solution)/shard_map/ppermute | solution.py:41
  59.8 9.0 %collective-permute-start.10 = (bf16[2,256,256]{2,1,0:T(8,128)(2,1)S(1)}, bf16[2,256,256]{2,1,0:T(8,128)(2,1)S(1)}, u32[]{:S(2)}, u32[]{:S(2)}) collective-permute-start(bf16[2,256,256]{2,1,0:T(8,128)(2,1)S(1)} %get-tuple-element.49), channel_id=1, source_target_pairs={{0,16},{1,65},{2,18},{3,67},{4,20},{5,69},{6,22},{7,71},{8,24},{9,... | collective-permute-start | bytes 786440 | tf_op jit(solution)/shard_map/ppermute | solution.py:41
  60.4 8.4 %collective-permute-start.11 = (bf16[2,256,256]{2,1,0:T(8,128)(2,1)S(1)}, bf16[2,256,256]{2,1,0:T(8,128)(2,1)S(1)}, u32[]{:S(2)}, u32[]{:S(2)}) collective-permute-start(bf16[2,256,256]{2,1,0:T(8,128)(2,1)S(1)} %get-tuple-element.50), channel_id=1, source_target_pairs={{0,8},{1,33},{2,10},{3,35},{4,12},{5,37},{6,14},{7,39},{8,0},{9,41... | collective-permute-start | bytes 786440 | tf_op jit(solution)/shard_map/ppermute | solution.py:41
  61.1 9.4 %collective-permute-start.12 = (bf16[2,256,256]{2,1,0:T(8,128)(2,1)S(1)}, bf16[2,256,256]{2,1,0:T(8,128)(2,1)S(1)}, u32[]{:S(2)}, u32[]{:S(2)}) collective-permute-start(bf16[2,256,256]{2,1,0:T(8,128)(2,1)S(1)} %get-tuple-element.51), channel_id=1, source_target_pairs={{0,24},{1,97},{2,26},{3,99},{4,28},{5,101},{6,30},{7,103},{8,16},{... | collective-permute-start | bytes 786440 | tf_op jit(solution)/shard_map/ppermute | solution.py:41
  64.1 8.3 %collective-permute-start.18 = (bf16[2,256,256]{2,1,0:T(8,128)(2,1)S(1)}, bf16[2,256,256]{2,1,0:T(8,128)(2,1)S(1)}, u32[]{:S(2)}, u32[]{:S(2)}) collective-permute-start(bf16[2,256,256]{2,1,0:T(8,128)(2,1)S(1)} %shard_map.81), channel_id=1, source_target_pairs={{0,4},{1,5},{2,6},{3,7},{4,0},{5,1},{6,2},{7,3},{8,12},{9,13},{10,... | collective-permute-start | bytes 786440 | tf_op jit(solution)/shard_map/ppermute | solution.py:41

commit v4 on v3

--- a/solution.py
+++ b/solution.py
@@ -12,7 +12,7 @@
 STEP = 8
 F32, BF16 = jnp.float32, jnp.bfloat16
 
-NEAR, FAR = (1, 3), (3, 1)
+NEAR, FAR = (3, 1), (1, 3)
 
 
 def xor_perm(mask):
@@ -87,42 +87,42 @@
     )(jnp.concatenate([ctx_marg, discount, row_marg]).reshape(258, 128))
 
 
+def fetch_block(counts_ref, in_ref, sem, g, part, s, i=0):
+    r, core = place()
+    d, e, k = slots(g, part)[s]
+    at = pl.multiple_of(block_of(r, core, g, d ^ (FAR[g] * i), e, k) * W, W)
+    return pltpu.make_async_copy(counts_ref.at[:, pl.ds(at, W)], in_ref.at[s + 8 * i], sem.at[s + 8 * i])
+
+
 def prepare_kernel(part, *refs):
     if part == 1:
-        tail_ref, counts_ref, *outs, in_ref, sem = refs
+        tail_ref, counts_ref, *outs, in_a, in_b, sem_a, sem_b = refs
+        bufs = ((in_a, sem_a), (in_b, sem_b))
+    else:
+        counts_ref, *outs, in_a, sem_a = refs
+        bufs = ((in_a, sem_a),)
+    copies = [(g, s) for g in range(len(outs)) for s in range(16)]
+    for g, s in copies:
+        fetch_block(counts_ref, *bufs[g], g, part, s).start()
+    if part == 1:
         for out_ref in outs:
             out_ref[16 * W:16 * W + 16, :] = tail_ref[...]
-    else:
-        counts_ref, kept_ref, in_ref, sem = refs
-    r, core = place()
-
-    def fetch(s):
-        d, e, k = slots(s // 16, part)[s % 16]
-        at = pl.multiple_of(block_of(r, core, s // 16, d, e, k) * W, W)
-        return pltpu.make_async_copy(counts_ref.at[:, pl.ds(at, W)], in_ref.at[s], sem.at[s])
-
-    for s in range(32):
-        fetch(s).start()
-    for s in range(32):
-        fetch(s).wait()
-        block = in_ref[s].astype(F32).astype(BF16)
-        if part == 1:
-            outs[s // 16][s % 16 * W:(s % 16 + 1) * W, :] = block
-        else:
-            kept_ref[s * W:(s + 1) * W, :] = block
+    for g, s in copies:
+        fetch_block(counts_ref, *bufs[g], g, part, s).wait()
+        outs[g][s * W:(s + 1) * W, :] = bufs[g][0][s].astype(F32).astype(BF16)
 
 
 def prepare(part, counts, *tail):
     rows = counts.shape[0]
-    lengths = [16 * W + 16] * 2 if part else [32 * W]
+    n = 1 + part
     return pl.pallas_call(
         functools.partial(prepare_kernel, part),
         in_specs=[spec(pltpu.VMEM)] * part + [spec(pl.ANY)],
-        out_specs=[spec(pltpu.VMEM)] * len(lengths),
-        out_shape=[jax.ShapeDtypeStruct((n, W), BF16) for n in lengths],
-        scratch_shapes=[pltpu.VMEM((32, rows, W), jnp.int32), pltpu.SemaphoreType.DMA((32,))],
-        compiler_params=params(42),
-        cost_estimate=pl.CostEstimate(flops=1 << 22, bytes_accessed=12 << 20, transcendentals=0),
+        out_specs=[spec(pltpu.VMEM)] * n,
+        out_shape=[jax.ShapeDtypeStruct((16 * W + 16 * part, W), BF16)] * n,
+        scratch_shapes=[pltpu.VMEM((16, rows, W), jnp.int32)] * n + [pltpu.SemaphoreType.DMA((16,))] * n,
+        compiler_params=params(38),
+        cost_estimate=pl.CostEstimate(flops=1 << 22, bytes_accessed=n * (6 << 20), transcendentals=0),
     )(*tail, counts)
 
 
@@ -141,47 +141,56 @@
     return jnp.concatenate([both, both], axis=1)
 
 
-def forward_kernel(total_ref, other_ref, inv_ref, power_ref, shrink_ref, kept_ref, sent_a, sent_b, probes_ref,
-                   tile_ref, y_ref, acc_ref, work_ref):
+def forward_kernel(total_ref, other_ref, inv_ref, power_ref, shrink_ref, sent_a, sent_b, kept_a, probes_ref, counts_ref,
+                   tile_ref, y_ref, acc_ref, work_ref, in_ref, sem):
     r, core = place()
     total = whole_total(total_ref, other_ref)
     rows = inv_ref.shape[0]
+    for s in range(16):
+        fetch_block(counts_ref, in_ref, sem, 1, 0, s).start()
     acc_ref[...] = jnp.zeros_like(acc_ref)
-    for g, sent_ref in enumerate((sent_a, sent_b)):
-        for part in range(2):
-            @pl.loop(0, 2)
-            def _(i):
-                sums = None
-                for n, (d, e, k) in enumerate(slots(g, part)[:8]):
-                    block = block_of(r, core, g, d ^ (FAR[g] * i), e, k)
-                    at = pl.multiple_of(block * W, W)
-                    shrink = column_terms(shrink_ref, block)
-                    scale = column_terms(power_ref, block) * total
-                    if part == 0:
-                        source, base, out = kept_ref, (16 * g + 8 * i + n) * rows, tile_ref.at[16 * g + 8 * i + n]
-                    else:
-                        source, base, out = sent_ref, (8 * i + n) * rows, work_ref.at[n]
-                    base = pl.multiple_of(base, rows)
-                    for q in range(0, rows, 32):
-                        out[q:q + 32, :] = tile_rows(source[pl.ds(base + q, 32), :], shrink, scale, inv_ref[q:q + 32, :])
-                    term = jnp.dot(out[...], probes_ref[pl.ds(at, W), :], preferred_element_type=F32)
-                    sums = term if sums is None else sums + term
-                acc_ref[...] += sums
+    for part, g, blocks in ((1, 0, sent_a), (1, 1, sent_b), (0, 0, kept_a), (0, 1, None)):
+        @pl.loop(0, 2)
+        def _(i):
+            sums = None
+            if blocks is None:
+                for n in range(8):
+                    fetch_block(counts_ref, in_ref, sem, g, part, n, i).wait()
+            for n, (d, e, k) in enumerate(slots(g, part)[:8]):
+                block = block_of(r, core, g, d ^ (FAR[g] * i), e, k)
+                at = pl.multiple_of(block * W, W)
+                shrink = column_terms(shrink_ref, block)
+                scale = column_terms(power_ref, block) * total
+                if blocks is None:
+                    source = in_ref.at[8 * i + n]
+                else:
+                    source = blocks.at[pl.ds(pl.multiple_of((8 * i + n) * rows, rows), rows)]
+                out = work_ref.at[n] if part else tile_ref.at[16 * g + 8 * i + n]
+                for q in range(0, rows, 32):
+                    out[q:q + 32, :] = tile_rows(source[q:q + 32, :], shrink, scale, inv_ref[q:q + 32, :])
+                term = jnp.dot(out[...], probes_ref[pl.ds(at, W), :], preferred_element_type=F32)
+                sums = term if sums is None else sums + term
+            acc_ref[...] += sums
     y_ref[...] = jnp.transpose(acc_ref[...])
 
 
-def forward(total, other, inv_row, power, shrink, kept, sent, probes):
+def forward(total, other, inv_row, power, shrink, sent, kept, probes, counts):
     rows, width = inv_row.shape[0], probes.shape[1]
     vmem = spec(pltpu.VMEM)
     return pl.pallas_call(
         forward_kernel,
-        in_specs=[vmem] * 9,
+        in_specs=[vmem] * 9 + [spec(pl.ANY)],
         out_specs=[vmem, vmem],
-        scratch_shapes=[pltpu.VMEM((rows, width), F32), pltpu.VMEM((STEP, rows, W), BF16)],
+        scratch_shapes=[
+            pltpu.VMEM((rows, width), F32),
+            pltpu.VMEM((STEP, rows, W), BF16),
+            pltpu.VMEM((16, rows, W), jnp.int32),
+            pltpu.SemaphoreType.DMA((16,)),
+        ],
         out_shape=(jax.ShapeDtypeStruct((32, rows, W), BF16), jax.ShapeDtypeStruct((width, rows), F32)),
-        compiler_params=params(6),
+        compiler_params=params(30),
         cost_estimate=pl.CostEstimate(flops=1 << 31, bytes_accessed=28 << 20, transcendentals=1 << 22),
-    )(total, other, inv_row, power, shrink, kept, *sent, probes)
+    )(total, other, inv_row, power, shrink, *sent, kept, probes, counts)
 
 
 def other_kernel(group, total_ref, other_ref, power_ref, shrink_ref, count_ref, tile_ref, inv_ref):
@@ -298,24 +307,25 @@
 def local(counts, row_marg, ctx_marg, discount, probes):
     power, shrink, total, inv_row, tail = context(ctx_marg, discount, row_marg)
     sent = prepare(1, counts, tail)
+    total = total + permute(total, CORE_PERM)
+    sent, total = lax.optimization_barrier((sent, total))
     received = [permute(sent[g], u_perm(NEAR[g])) for g in range(2)]
-    total = total + permute(total, CORE_PERM)
     other = permute(total, ZL_PERM)
     kept, = prepare(0, counts)
-    tile, y_part = forward(total, other, inv_row, power, shrink, kept, sent, probes)
+    tile, y_part = forward(total, other, inv_row, power, shrink, sent, kept, probes, counts)
     y_chip = (y_part + permute(y_part, CORE_PERM)).astype(BF16)
     y_own = (y_chip.astype(F32) + permute(y_chip, ZL_PERM).astype(F32)).astype(BF16)
     y_other = [permute(y_own, u_perm(NEAR[g])) for g in range(2)]
 
     tiles = [other_tile(g, total, other, power, shrink, received[g]) for g in range(2)]
-    y_other, tiles = lax.optimization_barrier((y_other, tiles))
+    y_other, tiles = zip(*[lax.optimization_barrier((y_other[g], tiles[g])) for g in range(2)])
     sends = [back(g, 1, y_own, y_other[g], tile, tiles[g], BF16) for g in range(2)]
     r2 = [[permute(sends[g][c], u_perm(FAR[g])) for g in range(2)] for c in range(2)]
     z = [back(g, 0, y_own, y_other[g], tile, tiles[g], F32) for g in range(2)]
     ended = []
     for c, dtype in enumerate((BF16, F32)):
         own, *out = pack([z[g][c] for g in range(2)], r2[c])
-        ended.append(fold(own, [permute(out[e - 1], v_perm(e)) for e in (2, 1, 3)], dtype))
+        ended.append(fold(own, [permute(out[e - 1], v_perm(e)) for e in (3, 1, 2)], dtype))
     factor = (counts.shape[0] * lax.axis_size("rows")) ** (-0.5)
     z_proj = last(ended[1], permute(ended[0], ZH_PERM), factor)
     return (jnp.transpose(y_own), z_proj[None])

time: 74 us -> 72.6 us (0.981)
  Pallas kernels: 20.5 us -> 19.2 us
  starting transfers between devices: 26 us -> 26.9 us
    pallas_call x2, Pallas kernels: 7.9 us -> 6.37 us  [prepare(): pl.pallas_call(functools.partial(prepare_kernel, part), in_specs=[spec(pl...]
    ppermute x19, starting transfers between devices: 26 us -> 26.9 us  [permute(): return lax.ppermute(a, AXES, perm)]
  transfers between devices with their start and end apart: 19 -> 19, of which waited for: 12 -> 9; matrix products, arithmetic and copies ran while one was open for 1% -> 1% of each run, Pallas kernels for 20% -> 25%
where the time goes in v4:
time: 72.6 us; the launch traced here: 72.4 us
  starting transfers between devices  26.9 us (37%)
  waiting for transfers between devices  23.7 us (33%)
  Pallas kernels  19.2 us (26%)
  other arithmetic  0.97 us (1%)
  between operations  0.84 us (1%)
  local copies, waits for them, and re-layouts  0.77 us (1%)
    ppermute x19, starting transfers between devices, permute(): return lax.ppermute(a, AXES, perm)  26.9 us
    ppermute x19, waiting for transfers between devices, permute(): return lax.ppermute(a, AXES, perm)  23.7 us
    pallas_call x2, Pallas kernels, prepare(): pl.pallas_call(functools.partial(prepare_kernel, part), in_specs=[spec(pl...  6.37 us
    pallas_call x1, Pallas kernels, forward(): pl.pallas_call(forward_kernel, in_specs=[vmem] * 9 + [spec(pl.ANY)], out_...  5.91 us
    pallas_call x4, Pallas kernels, back(): pl.pallas_call(functools.partial(back_kernel, group * 16, half), in_specs...  2.85 us
    pallas_call x2, Pallas kernels, other_tile(): pl.pallas_call(functools.partial(other_kernel, group), in_specs=[vmem] *...  2.34 us
  transfers between devices with their start and end apart: 19, of which 9 were waited for; matrix products, arithmetic and copies ran while one was open for 1% of the time, Pallas kernels for 25%

profile of v4, /device:TPU:24, one launch (start us, length us, event | category | flops | bytes accessed | tf_op | source)
XLA Modules:
  0.0 72.4 jit_solution(2582050394622860237)
XLA Ops:
  1.8 4.1 %shard_map.69 = (bf16[4112,256]{1,0:T(8,128)(2,1)S(1)}, bf16[4112,256]{1,0:T(8,128)(2,1)S(1)}) custom-call(bf16[16,256]{1,0:T(8,128)(2,1)S(1)} %get-tuple-element.34.refs_0_, s32[256,16384]{1,0:T(8,128)} %counts_ref.1), custom_call_target="tpu_custom_call" | custom-call | flops 4194304 | bytes 12582912 | tf_op jit(solution)/shard_map/pallas_call | solution.py:118
  5.9 1.6 %collective-permute-start.8 = (bf16[4112,256]{1,0:T(8,128)(2,1)S(1)}, bf16[4112,256]{1,0:T(8,128)(2,1)S(1)}, u32[]{:S(2)}, u32[]{:S(2)}) collective-permute-start(bf16[4112,256]{1,0:T(8,128)(2,1)S(1)} %get-tuple-element.43.sent_b), channel_id=1, source_target_pairs={{0,32},{1,9},{2,34},{3,11},{4,36},{5,13},{6,38},{7,15},{8,40},{9,1... | collective-permute-start | bytes 6316040 | tf_op jit(solution)/shard_map/ppermute | solution.py:41
  7.5 2.1 %collective-permute-start.5 = (bf16[4112,256]{1,0:T(8,128)(2,1)S(1)}, bf16[4112,256]{1,0:T(8,128)(2,1)S(1)}, u32[]{:S(2)}, u32[]{:S(2)}) collective-permute-start(bf16[4112,256]{1,0:T(8,128)(2,1)S(1)} %get-tuple-element.42.sent_a), channel_id=1, source_target_pairs={{0,96},{1,25},{2,98},{3,27},{4,100},{5,29},{6,102},{7,31},{8,104},... | collective-permute-start | bytes 6316040 | tf_op jit(solution)/shard_map/ppermute | solution.py:41
  9.6 1.9 %collective-permute-start.1 = (f32[8,128]{1,0:T(8,128)S(1)}, f32[8,128]{1,0:T(8,128)S(1)}, u32[]{:S(2)}, u32[]{:S(2)}) collective-permute-start(f32[8,128]{1,0:T(8,128)S(1)} %add.9.total_ref), channel_id=1, source_target_pairs={{0,2},{1,3},{2,0},{3,1},{4,6},{5,7},{6,4},{7,5},{8,10},{9,11},{10,... | collective-permute-start | bytes 12296 | tf_op jit(solution)/shard_map/ppermute | solution.py:41
  11.5 2.3 %shard_map.70.kept_a = bf16[4096,256]{1,0:T(8,128)(2,1)S(1)} custom-call(s32[256,16384]{1,0:T(8,128)} %counts_ref.1), custom_call_target="tpu_custom_call" | custom-call | flops 4194304 | bytes 6291456 | tf_op jit(solution)/shard_map/pallas_call | solution.py:118
  13.9 5.9 %shard_map.71 = (bf16[32,256,256]{2,1,0:T(8,128)(2,1)S(1)}, f32[256,256]{1,0:T(8,128)S(1)}) custom-call(f32[8,128]{1,0:T(8,128)S(1)} %add.9.total_ref, f32[8,128]{1,0:T(8,128)S(1)} %collective-permute-done.1.other_ref, f32[256,128]{1,0:T(8,128)S(1)} %get-tuple-element.39.inv_ref, f32[128,128]{1,0:T(8,128)S(1)} %get-tuple-element.40.power_ref, ...), custom_call_target="tpu_custom_call" | custom-call | flops 2147483648 | bytes 29360128 | tf_op jit(solution)/shard_map/pallas_call | solution.py:180
  19.9 1.5 %collective-permute-done.2 = f32[256,256]{1,0:T(8,128)S(1)} collective-permute-done((f32[256,256]{1,0:T(8,128)S(1)}, f32[256,256]{1,0:T(8,128)S(1)}, u32[]{:S(2)}, u32[]{:S(2)}) %collective-permute-start.2) | collective-permute-done | bytes 262176 | tf_op jit(solution)/shard_map/ppermute | solution.py:41
  21.4 1.3 %collective-permute-start.3 = (bf16[256,256]{1,0:T(8,128)(2,1)S(1)}, bf16[256,256]{1,0:T(8,128)(2,1)S(1)}, u32[]{:S(2)}, u32[]{:S(2)}) collective-permute-start(bf16[256,256]{1,0:T(8,128)(2,1)S(1)} %add_convert_fusion.1), channel_id=1, source_target_pairs={{0,2},{1,3},{2,0},{3,1},{4,6},{5,7},{6,4},{7,5},{8,10},{9,11},{10,... | collective-permute-start | bytes 393224 | tf_op jit(solution)/shard_map/ppermute | solution.py:41
  22.7 4.3 %collective-permute-done.3 = bf16[256,256]{1,0:T(8,128)(2,1)S(1)} collective-permute-done((bf16[256,256]{1,0:T(8,128)(2,1)S(1)}, bf16[256,256]{1,0:T(8,128)(2,1)S(1)}, u32[]{:S(2)}, u32[]{:S(2)}) %collective-permute-start.3) | collective-permute-done | bytes 131104 | tf_op jit(solution)/shard_map/ppermute | solution.py:41
  28.5 3.6 %collective-permute-done.8.count_ref = bf16[4112,256]{1,0:T(8,128)(2,1)S(1)} collective-permute-done((bf16[4112,256]{1,0:T(8,128)(2,1)S(1)}, bf16[4112,256]{1,0:T(8,128)(2,1)S(1)}, u32[]{:S(2)}, u32[]{:S(2)}) %collective-permute-start.8) | collective-permute-done | bytes 2105376 | tf_op jit(solution)/shard_map/ppermute | solution.py:41
  32.1 1.2 %shard_map.75.other_ref = bf16[16,256,256]{2,1,0:T(8,128)(2,1)S(1)} custom-call(f32[8,128]{1,0:T(8,128)S(1)} %add.9.total_ref, f32[8,128]{1,0:T(8,128)S(1)} %collective-permute-done.1.other_ref, f32[128,128]{1,0:T(8,128)S(1)} %get-tuple-element.40.power_ref, f32[128,128]{1,0:T(8,128)S(1)} %get-tuple-element.41.shrink_ref, ...), custom_call_target="tpu_custom_call" | custom-call | flops 16777216 | bytes 4194304 | tf_op jit(solution)/shard_map/pallas_call | solution.py:218
  34.2 2.8 %collective-permute-start.14 = (bf16[4,256,256]{2,1,0:T(8,128)(2,1)S(1)}, bf16[4,256,256]{2,1,0:T(8,128)(2,1)S(1)}, u32[]{:S(2)}, u32[]{:S(2)}) collective-permute-start(bf16[4,256,256]{2,1,0:T(8,128)(2,1)S(1)} %get-tuple-element.61), channel_id=1, source_target_pairs={{0,96},{1,25},{2,98},{3,27},{4,100},{5,29},{6,102},{7,31},{8,104},... | collective-permute-start | bytes 1572872 | tf_op jit(solution)/shard_map/ppermute | solution.py:41
  37.1 1.2 %shard_map.72.other_ref = bf16[16,256,256]{2,1,0:T(8,128)(2,1)S(1)} custom-call(f32[8,128]{1,0:T(8,128)S(1)} %add.9.total_ref, f32[8,128]{1,0:T(8,128)S(1)} %collective-permute-done.1.other_ref, f32[128,128]{1,0:T(8,128)S(1)} %get-tuple-element.40.power_ref, f32[128,128]{1,0:T(8,128)S(1)} %get-tuple-element.41.shrink_ref, ...), custom_call_target="tpu_custom_call" | custom-call | flops 16777216 | bytes 4194304 | tf_op jit(solution)/shard_map/pallas_call | solution.py:218
  39.3 1.1 %collective-permute-start.9 = (bf16[4,256,256]{2,1,0:T(8,128)(2,1)S(1)}, bf16[4,256,256]{2,1,0:T(8,128)(2,1)S(1)}, u32[]{:S(2)}, u32[]{:S(2)}) collective-permute-start(bf16[4,256,256]{2,1,0:T(8,128)(2,1)S(1)} %get-tuple-element.53), channel_id=1, source_target_pairs={{0,96},{1,25},{2,98},{3,27},{4,100},{5,29},{6,102},{7,31},{8,104},... | collective-permute-start | bytes 1572872 | tf_op jit(solution)/shard_map/ppermute | solution.py:41
  42.6 2.2 %collective-permute-done.14.r_b = bf16[4,256,256]{2,1,0:T(8,128)(2,1)S(1)} collective-permute-done((bf16[4,256,256]{2,1,0:T(8,128)(2,1)S(1)}, bf16[4,256,256]{2,1,0:T(8,128)(2,1)S(1)}, u32[]{:S(2)}, u32[]{:S(2)}) %collective-permute-start.14) | collective-permute-done | bytes 524320 | tf_op jit(solution)/shard_map/ppermute | solution.py:41
  44.7 3.6 %collective-permute-done.13.r_a = bf16[4,256,256]{2,1,0:T(8,128)(2,1)S(1)} collective-permute-done((bf16[4,256,256]{2,1,0:T(8,128)(2,1)S(1)}, bf16[4,256,256]{2,1,0:T(8,128)(2,1)S(1)}, u32[]{:S(2)}, u32[]{:S(2)}) %collective-permute-start.13) | collective-permute-done | bytes 524320 | tf_op jit(solution)/shard_map/ppermute | solution.py:41
  48.8 1.0 %collective-permute-start.16 = (bf16[2,256,256]{2,1,0:T(8,128)(2,1)S(1)}, bf16[2,256,256]{2,1,0:T(8,128)(2,1)S(1)}, u32[]{:S(2)}, u32[]{:S(2)}) collective-permute-start(bf16[2,256,256]{2,1,0:T(8,128)(2,1)S(1)} %get-tuple-element.64), channel_id=1, source_target_pairs={{0,8},{1,33},{2,10},{3,35},{4,12},{5,37},{6,14},{7,39},{8,0},{9,41... | collective-permute-start | bytes 786440 | tf_op jit(solution)/shard_map/ppermute | solution.py:41
  49.8 3.5 %collective-permute-start.17 = (bf16[2,256,256]{2,1,0:T(8,128)(2,1)S(1)}, bf16[2,256,256]{2,1,0:T(8,128)(2,1)S(1)}, u32[]{:S(2)}, u32[]{:S(2)}) collective-permute-start(bf16[2,256,256]{2,1,0:T(8,128)(2,1)S(1)} %get-tuple-element.65), channel_id=1, source_target_pairs={{0,16},{1,65},{2,18},{3,67},{4,20},{5,69},{6,22},{7,71},{8,24},{9,... | collective-permute-start | bytes 786440 | tf_op jit(solution)/shard_map/ppermute | solution.py:41
  53.3 4.8 %collective-permute-done.6.r_a = bf16[4,256,256]{2,1,0:T(8,128)(2,1)S(1)} collective-permute-done((bf16[4,256,256]{2,1,0:T(8,128)(2,1)S(1)}, bf16[4,256,256]{2,1,0:T(8,128)(2,1)S(1)}, u32[]{:S(2)}, u32[]{:S(2)}) %collective-permute-start.6) | collective-permute-done | bytes 524320 | tf_op jit(solution)/shard_map/ppermute | solution.py:41
  59.0 4.0 %collective-permute-start.12 = (bf16[2,256,256]{2,1,0:T(8,128)(2,1)S(1)}, bf16[2,256,256]{2,1,0:T(8,128)(2,1)S(1)}, u32[]{:S(2)}, u32[]{:S(2)}) collective-permute-start(bf16[2,256,256]{2,1,0:T(8,128)(2,1)S(1)} %get-tuple-element.57), channel_id=1, source_target_pairs={{0,16},{1,65},{2,18},{3,67},{4,20},{5,69},{6,22},{7,71},{8,24},{9,... | collective-permute-start | bytes 786440 | tf_op jit(solution)/shard_map/ppermute | solution.py:41
  63.1 4.0 %collective-permute-start.18 = (bf16[2,256,256]{2,1,0:T(8,128)(2,1)S(1)}, bf16[2,256,256]{2,1,0:T(8,128)(2,1)S(1)}, u32[]{:S(2)}, u32[]{:S(2)}) collective-permute-start(bf16[2,256,256]{2,1,0:T(8,128)(2,1)S(1)} %shard_map.81), channel_id=1, source_target_pairs={{0,4},{1,5},{2,6},{3,7},{4,0},{5,1},{6,2},{7,3},{8,12},{9,13},{10,... | collective-permute-start | bytes 786440 | tf_op jit(solution)/shard_map/ppermute | solution.py:41
  67.9 2.3 %collective-permute-done.12.c_ref = bf16[2,256,256]{2,1,0:T(8,128)(2,1)S(1)} collective-permute-done((bf16[2,256,256]{2,1,0:T(8,128)(2,1)S(1)}, bf16[2,256,256]{2,1,0:T(8,128)(2,1)S(1)}, u32[]{:S(2)}, u32[]{:S(2)}) %collective-permute-start.12) | collective-permute-done | bytes 262176 | tf_op jit(solution)/shard_map/ppermute | solution.py:41
  70.3 1.2 %collective-permute-done.18.got_ref = bf16[2,256,256]{2,1,0:T(8,128)(2,1)S(1)} collective-permute-done((bf16[2,256,256]{2,1,0:T(8,128)(2,1)S(1)}, bf16[2,256,256]{2,1,0:T(8,128)(2,1)S(1)}, u32[]{:S(2)}, u32[]{:S(2)}) %collective-permute-start.18) | collective-permute-done | bytes 262176 | tf_op jit(solution)/shard_map/ppermute | solution.py:41
  71.4 1.0 %shard_map.82 = f32[512,256]{1,0:T(8,128)} custom-call(f32[2,256,256]{2,1,0:T(8,128)S(1)} %shard_map.79.own_ref, bf16[2,256,256]{2,1,0:T(8,128)(2,1)S(1)} %collective-permute-done.18.got_ref), custom_call_target="tpu_custom_call" | custom-call | flops 1048576 | bytes 2097152 | tf_op jit(solution)/shard_map/pallas_call | solution.py:297
  (39 shorter events, 9.2 us)
Async XLA Ops:
  1.7 4.2 %collective-permute-start = (f32[8,128]{1,0:T(8,128)S(1)}, f32[8,128]{1,0:T(8,128)S(1)}, u32[]{:S(2)}, u32[]{:S(2)}) collective-permute-start(f32[8,128]{1,0:T(8,128)S(1)} %get-tuple-element.37), channel_id=1, source_target_pairs={{0,1},{1,0},{2,3},{3,2},{4,5},{5,4},{6,7},{7,6},{8,9},{9,8},{10,11... | collective-permute-start | bytes 12296 | tf_op jit(solution)/shard_map/ppermute | solution.py:41
  1.8 12.0 %slice-start = ((s8[8388608]{0:T(1024)(128)(4,1)}), s8[4194304]{0:T(1024)(128)(4,1)S(1)}, s32[]{:S(2)}) async-start(s8[8388608]{0:T(1024)(128)(4,1)} %bitcast.4), calls=%async_computation | async-start | bytes 8388608
  5.9 7.9 %slice-start.1 = ((s8[8388608]{0:T(1024)(128)(4,1)}), s8[4194304]{0:T(1024)(128)(4,1)S(1)}, s32[]{:S(2)}) async-start(s8[8388608]{0:T(1024)(128)(4,1)} %bitcast.4), calls=%async_computation.1 | async-start | bytes 8388608
  5.9 26.2 %collective-permute-start.8 = (bf16[4112,256]{1,0:T(8,128)(2,1)S(1)}, bf16[4112,256]{1,0:T(8,128)(2,1)S(1)}, u32[]{:S(2)}, u32[]{:S(2)}) collective-permute-start(bf16[4112,256]{1,0:T(8,128)(2,1)S(1)} %get-tuple-element.43.sent_b), channel_id=1, source_target_pairs={{0,32},{1,9},{2,34},{3,11},{4,36},{5,13},{6,38},{7,15},{8,40},{9,1... | collective-permute-start | bytes 6316040 | tf_op jit(solution)/shard_map/ppermute | solution.py:41
  7.5 29.6 %collective-permute-start.5 = (bf16[4112,256]{1,0:T(8,128)(2,1)S(1)}, bf16[4112,256]{1,0:T(8,128)(2,1)S(1)}, u32[]{:S(2)}, u32[]{:S(2)}) collective-permute-start(bf16[4112,256]{1,0:T(8,128)(2,1)S(1)} %get-tuple-element.42.sent_a), channel_id=1, source_target_pairs={{0,96},{1,25},{2,98},{3,27},{4,100},{5,29},{6,102},{7,31},{8,104},... | collective-permute-start | bytes 6316040 | tf_op jit(solution)/shard_map/ppermute | solution.py:41
  9.6 4.2 %collective-permute-start.1 = (f32[8,128]{1,0:T(8,128)S(1)}, f32[8,128]{1,0:T(8,128)S(1)}, u32[]{:S(2)}, u32[]{:S(2)}) collective-permute-start(f32[8,128]{1,0:T(8,128)S(1)} %add.9.total_ref), channel_id=1, source_target_pairs={{0,2},{1,3},{2,0},{3,1},{4,6},{5,7},{6,4},{7,5},{8,10},{9,11},{10,... | collective-permute-start | bytes 12296 | tf_op jit(solution)/shard_map/ppermute | solution.py:41
  19.8 1.6 %collective-permute-start.2 = (f32[256,256]{1,0:T(8,128)S(1)}, f32[256,256]{1,0:T(8,128)S(1)}, u32[]{:S(2)}, u32[]{:S(2)}) collective-permute-start(f32[256,256]{1,0:T(8,128)S(1)} %get-tuple-element.44), channel_id=1, source_target_pairs={{0,1},{1,0},{2,3},{3,2},{4,5},{5,4},{6,7},{7,6},{8,9},{9,8},{10,11... | collective-permute-start | bytes 786440 | tf_op jit(solution)/shard_map/ppermute | solution.py:41
  21.4 5.6 %collective-permute-start.3 = (bf16[256,256]{1,0:T(8,128)(2,1)S(1)}, bf16[256,256]{1,0:T(8,128)(2,1)S(1)}, u32[]{:S(2)}, u32[]{:S(2)}) collective-permute-start(bf16[256,256]{1,0:T(8,128)(2,1)S(1)} %add_convert_fusion.1), channel_id=1, source_target_pairs={{0,2},{1,3},{2,0},{3,1},{4,6},{5,7},{6,4},{7,5},{8,10},{9,11},{10,... | collective-permute-start | bytes 393224 | tf_op jit(solution)/shard_map/ppermute | solution.py:41
  27.1 6.4 %collective-permute-start.7 = (bf16[256,256]{1,0:T(8,128)(2,1)S(1)}, bf16[256,256]{1,0:T(8,128)(2,1)S(1)}, u32[]{:S(2)}, u32[]{:S(2)}) collective-permute-start(bf16[256,256]{1,0:T(8,128)(2,1)S(1)} %add_convert_fusion.y_own_ref), channel_id=1, source_target_pairs={{0,32},{1,9},{2,34},{3,11},{4,36},{5,13},{6,38},{7,15},{8,40},{9,1... | collective-permute-start | bytes 393224 | tf_op jit(solution)/shard_map/ppermute | solution.py:41
  27.8 10.5 %collective-permute-start.4 = (bf16[256,256]{1,0:T(8,128)(2,1)S(1)}, bf16[256,256]{1,0:T(8,128)(2,1)S(1)}, u32[]{:S(2)}, u32[]{:S(2)}) collective-permute-start(bf16[256,256]{1,0:T(8,128)(2,1)S(1)} %add_convert_fusion.y_own_ref), channel_id=1, source_target_pairs={{0,96},{1,25},{2,98},{3,27},{4,100},{5,29},{6,102},{7,31},{8,104},... | collective-permute-start | bytes 393224 | tf_op jit(solution)/shard_map/ppermute | solution.py:41
  34.2 10.5 %collective-permute-start.14 = (bf16[4,256,256]{2,1,0:T(8,128)(2,1)S(1)}, bf16[4,256,256]{2,1,0:T(8,128)(2,1)S(1)}, u32[]{:S(2)}, u32[]{:S(2)}) collective-permute-start(bf16[4,256,256]{2,1,0:T(8,128)(2,1)S(1)} %get-tuple-element.61), channel_id=1, source_target_pairs={{0,96},{1,25},{2,98},{3,27},{4,100},{5,29},{6,102},{7,31},{8,104},... | collective-permute-start | bytes 1572872 | tf_op jit(solution)/shard_map/ppermute | solution.py:41
  39.0 9.3 %collective-permute-start.13 = (bf16[4,256,256]{2,1,0:T(8,128)(2,1)S(1)}, bf16[4,256,256]{2,1,0:T(8,128)(2,1)S(1)}, u32[]{:S(2)}, u32[]{:S(2)}) collective-permute-start(bf16[4,256,256]{2,1,0:T(8,128)(2,1)S(1)} %get-tuple-element.59), channel_id=1, source_target_pairs={{0,32},{1,9},{2,34},{3,11},{4,36},{5,13},{6,38},{7,15},{8,40},{9,1... | collective-permute-start | bytes 1572872 | tf_op jit(solution)/shard_map/ppermute | solution.py:41
  39.3 13.9 %collective-permute-start.9 = (bf16[4,256,256]{2,1,0:T(8,128)(2,1)S(1)}, bf16[4,256,256]{2,1,0:T(8,128)(2,1)S(1)}, u32[]{:S(2)}, u32[]{:S(2)}) collective-permute-start(bf16[4,256,256]{2,1,0:T(8,128)(2,1)S(1)} %get-tuple-element.53), channel_id=1, source_target_pairs={{0,96},{1,25},{2,98},{3,27},{4,100},{5,29},{6,102},{7,31},{8,104},... | collective-permute-start | bytes 1572872 | tf_op jit(solution)/shard_map/ppermute | solution.py:41
  40.5 17.6 %collective-permute-start.6 = (bf16[4,256,256]{2,1,0:T(8,128)(2,1)S(1)}, bf16[4,256,256]{2,1,0:T(8,128)(2,1)S(1)}, u32[]{:S(2)}, u32[]{:S(2)}) collective-permute-start(bf16[4,256,256]{2,1,0:T(8,128)(2,1)S(1)} %get-tuple-element.49), channel_id=1, source_target_pairs={{0,32},{1,9},{2,34},{3,11},{4,36},{5,13},{6,38},{7,15},{8,40},{9,1... | collective-permute-start | bytes 1572872 | tf_op jit(solution)/shard_map/ppermute | solution.py:41
  48.5 10.5 %collective-permute-start.15 = (bf16[2,256,256]{2,1,0:T(8,128)(2,1)S(1)}, bf16[2,256,256]{2,1,0:T(8,128)(2,1)S(1)}, u32[]{:S(2)}, u32[]{:S(2)}) collective-permute-start(bf16[2,256,256]{2,1,0:T(8,128)(2,1)S(1)} %get-tuple-element.63), channel_id=1, source_target_pairs={{0,24},{1,97},{2,26},{3,99},{4,28},{5,101},{6,30},{7,103},{8,16},{... | collective-permute-start | bytes 786440 | tf_op jit(solution)/shard_map/ppermute | solution.py:41
  48.8 14.2 %collective-permute-start.16 = (bf16[2,256,256]{2,1,0:T(8,128)(2,1)S(1)}, bf16[2,256,256]{2,1,0:T(8,128)(2,1)S(1)}, u32[]{:S(2)}, u32[]{:S(2)}) collective-permute-start(bf16[2,256,256]{2,1,0:T(8,128)(2,1)S(1)} %get-tuple-element.64), channel_id=1, source_target_pairs={{0,8},{1,33},{2,10},{3,35},{4,12},{5,37},{6,14},{7,39},{8,0},{9,41... | collective-permute-start | bytes 786440 | tf_op jit(solution)/shard_map/ppermute | solution.py:41
  49.8 13.3 %collective-permute-start.17 = (bf16[2,256,256]{2,1,0:T(8,128)(2,1)S(1)}, bf16[2,256,256]{2,1,0:T(8,128)(2,1)S(1)}, u32[]{:S(2)}, u32[]{:S(2)}) collective-permute-start(bf16[2,256,256]{2,1,0:T(8,128)(2,1)S(1)} %get-tuple-element.65), channel_id=1, source_target_pairs={{0,16},{1,65},{2,18},{3,67},{4,20},{5,69},{6,22},{7,71},{8,24},{9,... | collective-permute-start | bytes 786440 | tf_op jit(solution)/shard_map/ppermute | solution.py:41
  58.2 9.6 %collective-permute-start.10 = (bf16[2,256,256]{2,1,0:T(8,128)(2,1)S(1)}, bf16[2,256,256]{2,1,0:T(8,128)(2,1)S(1)}, u32[]{:S(2)}, u32[]{:S(2)}) collective-permute-start(bf16[2,256,256]{2,1,0:T(8,128)(2,1)S(1)} %get-tuple-element.55), channel_id=1, source_target_pairs={{0,24},{1,97},{2,26},{3,99},{4,28},{5,101},{6,30},{7,103},{8,16},{... | collective-permute-start | bytes 786440 | tf_op jit(solution)/shard_map/ppermute | solution.py:41
  58.3 9.5 %collective-permute-start.11 = (bf16[2,256,256]{2,1,0:T(8,128)(2,1)S(1)}, bf16[2,256,256]{2,1,0:T(8,128)(2,1)S(1)}, u32[]{:S(2)}, u32[]{:S(2)}) collective-permute-start(bf16[2,256,256]{2,1,0:T(8,128)(2,1)S(1)} %get-tuple-element.56), channel_id=1, source_target_pairs={{0,8},{1,33},{2,10},{3,35},{4,12},{5,37},{6,14},{7,39},{8,0},{9,41... | collective-permute-start | bytes 786440 | tf_op jit(solution)/shard_map/ppermute | solution.py:41
  59.0 11.2 %collective-permute-start.12 = (bf16[2,256,256]{2,1,0:T(8,128)(2,1)S(1)}, bf16[2,256,256]{2,1,0:T(8,128)(2,1)S(1)}, u32[]{:S(2)}, u32[]{:S(2)}) collective-permute-start(bf16[2,256,256]{2,1,0:T(8,128)(2,1)S(1)} %get-tuple-element.57), channel_id=1, source_target_pairs={{0,16},{1,65},{2,18},{3,67},{4,20},{5,69},{6,22},{7,71},{8,24},{9,... | collective-permute-start | bytes 786440 | tf_op jit(solution)/shard_map/ppermute | solution.py:41
  63.1 8.3 %collective-permute-start.18 = (bf16[2,256,256]{2,1,0:T(8,128)(2,1)S(1)}, bf16[2,256,256]{2,1,0:T(8,128)(2,1)S(1)}, u32[]{:S(2)}, u32[]{:S(2)}) collective-permute-start(bf16[2,256,256]{2,1,0:T(8,128)(2,1)S(1)} %shard_map.81), channel_id=1, source_target_pairs={{0,4},{1,5},{2,6},{3,7},{4,0},{5,1},{6,2},{7,3},{8,12},{9,13},{10,... | collective-permute-start | bytes 786440 | tf_op jit(solution)/shard_map/ppermute | solution.py:41

commit v5 on v4

--- a/solution.py
+++ b/solution.py
@@ -271,7 +271,7 @@
 def fold_kernel(own_ref, a_ref, b_ref, c_ref, out_ref):
     for g in range(2):
         total = own_ref[g] + a_ref[g].astype(F32) + b_ref[g].astype(F32) + c_ref[g].astype(F32)
-        out_ref[g] = total.astype(out_ref.dtype)
+        out_ref[g] = (jnp.transpose(total) if out_ref.dtype == F32 else total).astype(out_ref.dtype)
 
 
 def fold(own, got, dtype):
@@ -288,7 +288,7 @@
 
 def last_kernel(factor, own_ref, got_ref, z_ref):
     for g in range(2):
-        z_ref[g * W:(g + 1) * W, :] = jnp.transpose(own_ref[g] + got_ref[g].astype(F32)) * factor
+        z_ref[g * W:(g + 1) * W, :] = (own_ref[g] + jnp.transpose(got_ref[g].astype(F32))) * factor
 
 
 def last(own, got, factor):
@@ -325,7 +325,7 @@
     ended = []
     for c, dtype in enumerate((BF16, F32)):
         own, *out = pack([z[g][c] for g in range(2)], r2[c])
-        ended.append(fold(own, [permute(out[e - 1], v_perm(e)) for e in (3, 1, 2)], dtype))
+        ended.append(fold(own, [permute(out[e - 1], v_perm(e)) for e in ((3, 1, 2), (2, 1, 3))[c]], dtype))
     factor = (counts.shape[0] * lax.axis_size("rows")) ** (-0.5)
     z_proj = last(ended[1], permute(ended[0], ZH_PERM), factor)
     return (jnp.transpose(y_own), z_proj[None])

time: 72.6 us -> 71.9 us (level)
  no operation moved by 1% of the time
where the time goes in v5:
time: 71.9 us; the launch traced here: 71.8 us
  starting transfers between devices  26.3 us (37%)
  waiting for transfers between devices  23.6 us (33%)
  Pallas kernels  19.3 us (27%)
  other arithmetic  0.97 us (1%)
  between operations  0.84 us (1%)
  local copies, waits for them, and re-layouts  0.77 us (1%)
    ppermute x19, starting transfers between devices, permute(): return lax.ppermute(a, AXES, perm)  26.3 us
    ppermute x19, waiting for transfers between devices, permute(): return lax.ppermute(a, AXES, perm)  23.6 us
    pallas_call x2, Pallas kernels, prepare(): pl.pallas_call(functools.partial(prepare_kernel, part), in_specs=[spec(pl...  6.37 us
    pallas_call x1, Pallas kernels, forward(): pl.pallas_call(forward_kernel, in_specs=[vmem] * 9 + [spec(pl.ANY)], out_...  5.91 us
    pallas_call x4, Pallas kernels, back(): pl.pallas_call(functools.partial(back_kernel, group * 16, half), in_specs...  2.85 us
    pallas_call x2, Pallas kernels, other_tile(): pl.pallas_call(functools.partial(other_kernel, group), in_specs=[vmem] *...  2.34 us
  transfers between devices with their start and end apart: 19, of which 9 were waited for; matrix products, arithmetic and copies ran while one was open for 1% of the time, Pallas kernels for 25%

profile of v5, /device:TPU:24, one launch (start us, length us, event | category | flops | bytes accessed | tf_op | source)
XLA Modules:
  0.0 71.8 jit_solution(10919497433954292332)
XLA Ops:
  1.8 4.1 %shard_map.69 = (bf16[4112,256]{1,0:T(8,128)(2,1)S(1)}, bf16[4112,256]{1,0:T(8,128)(2,1)S(1)}) custom-call(bf16[16,256]{1,0:T(8,128)(2,1)S(1)} %get-tuple-element.34.refs_0_, s32[256,16384]{1,0:T(8,128)} %counts_ref.1), custom_call_target="tpu_custom_call" | custom-call | flops 4194304 | bytes 12582912 | tf_op jit(solution)/shard_map/pallas_call | solution.py:118
  5.9 1.6 %collective-permute-start.8 = (bf16[4112,256]{1,0:T(8,128)(2,1)S(1)}, bf16[4112,256]{1,0:T(8,128)(2,1)S(1)}, u32[]{:S(2)}, u32[]{:S(2)}) collective-permute-start(bf16[4112,256]{1,0:T(8,128)(2,1)S(1)} %get-tuple-element.43.sent_b), channel_id=1, source_target_pairs={{0,32},{1,9},{2,34},{3,11},{4,36},{5,13},{6,38},{7,15},{8,40},{9,1... | collective-permute-start | bytes 6316040 | tf_op jit(solution)/shard_map/ppermute | solution.py:41
  7.5 2.1 %collective-permute-start.5 = (bf16[4112,256]{1,0:T(8,128)(2,1)S(1)}, bf16[4112,256]{1,0:T(8,128)(2,1)S(1)}, u32[]{:S(2)}, u32[]{:S(2)}) collective-permute-start(bf16[4112,256]{1,0:T(8,128)(2,1)S(1)} %get-tuple-element.42.sent_a), channel_id=1, source_target_pairs={{0,96},{1,25},{2,98},{3,27},{4,100},{5,29},{6,102},{7,31},{8,104},... | collective-permute-start | bytes 6316040 | tf_op jit(solution)/shard_map/ppermute | solution.py:41
  9.6 1.9 %collective-permute-start.1 = (f32[8,128]{1,0:T(8,128)S(1)}, f32[8,128]{1,0:T(8,128)S(1)}, u32[]{:S(2)}, u32[]{:S(2)}) collective-permute-start(f32[8,128]{1,0:T(8,128)S(1)} %add.9.total_ref), channel_id=1, source_target_pairs={{0,2},{1,3},{2,0},{3,1},{4,6},{5,7},{6,4},{7,5},{8,10},{9,11},{10,... | collective-permute-start | bytes 12296 | tf_op jit(solution)/shard_map/ppermute | solution.py:41
  11.5 2.3 %shard_map.70.kept_a = bf16[4096,256]{1,0:T(8,128)(2,1)S(1)} custom-call(s32[256,16384]{1,0:T(8,128)} %counts_ref.1), custom_call_target="tpu_custom_call" | custom-call | flops 4194304 | bytes 6291456 | tf_op jit(solution)/shard_map/pallas_call | solution.py:118
  13.9 5.9 %shard_map.71 = (bf16[32,256,256]{2,1,0:T(8,128)(2,1)S(1)}, f32[256,256]{1,0:T(8,128)S(1)}) custom-call(f32[8,128]{1,0:T(8,128)S(1)} %add.9.total_ref, f32[8,128]{1,0:T(8,128)S(1)} %collective-permute-done.1.other_ref, f32[256,128]{1,0:T(8,128)S(1)} %get-tuple-element.39.inv_ref, f32[128,128]{1,0:T(8,128)S(1)} %get-tuple-element.40.power_ref, ...), custom_call_target="tpu_custom_call" | custom-call | flops 2147483648 | bytes 29360128 | tf_op jit(solution)/shard_map/pallas_call | solution.py:180
  19.9 1.5 %collective-permute-done.2 = f32[256,256]{1,0:T(8,128)S(1)} collective-permute-done((f32[256,256]{1,0:T(8,128)S(1)}, f32[256,256]{1,0:T(8,128)S(1)}, u32[]{:S(2)}, u32[]{:S(2)}) %collective-permute-start.2) | collective-permute-done | bytes 262176 | tf_op jit(solution)/shard_map/ppermute | solution.py:41
  21.4 1.3 %collective-permute-start.3 = (bf16[256,256]{1,0:T(8,128)(2,1)S(1)}, bf16[256,256]{1,0:T(8,128)(2,1)S(1)}, u32[]{:S(2)}, u32[]{:S(2)}) collective-permute-start(bf16[256,256]{1,0:T(8,128)(2,1)S(1)} %add_convert_fusion.1), channel_id=1, source_target_pairs={{0,2},{1,3},{2,0},{3,1},{4,6},{5,7},{6,4},{7,5},{8,10},{9,11},{10,... | collective-permute-start | bytes 393224 | tf_op jit(solution)/shard_map/ppermute | solution.py:41
  22.7 4.3 %collective-permute-done.3 = bf16[256,256]{1,0:T(8,128)(2,1)S(1)} collective-permute-done((bf16[256,256]{1,0:T(8,128)(2,1)S(1)}, bf16[256,256]{1,0:T(8,128)(2,1)S(1)}, u32[]{:S(2)}, u32[]{:S(2)}) %collective-permute-start.3) | collective-permute-done | bytes 131104 | tf_op jit(solution)/shard_map/ppermute | solution.py:41
  28.5 3.6 %collective-permute-done.8.count_ref = bf16[4112,256]{1,0:T(8,128)(2,1)S(1)} collective-permute-done((bf16[4112,256]{1,0:T(8,128)(2,1)S(1)}, bf16[4112,256]{1,0:T(8,128)(2,1)S(1)}, u32[]{:S(2)}, u32[]{:S(2)}) %collective-permute-start.8) | collective-permute-done | bytes 2105376 | tf_op jit(solution)/shard_map/ppermute | solution.py:41
  32.1 1.2 %shard_map.75.other_ref = bf16[16,256,256]{2,1,0:T(8,128)(2,1)S(1)} custom-call(f32[8,128]{1,0:T(8,128)S(1)} %add.9.total_ref, f32[8,128]{1,0:T(8,128)S(1)} %collective-permute-done.1.other_ref, f32[128,128]{1,0:T(8,128)S(1)} %get-tuple-element.40.power_ref, f32[128,128]{1,0:T(8,128)S(1)} %get-tuple-element.41.shrink_ref, ...), custom_call_target="tpu_custom_call" | custom-call | flops 16777216 | bytes 4194304 | tf_op jit(solution)/shard_map/pallas_call | solution.py:218
  34.2 2.8 %collective-permute-start.14 = (bf16[4,256,256]{2,1,0:T(8,128)(2,1)S(1)}, bf16[4,256,256]{2,1,0:T(8,128)(2,1)S(1)}, u32[]{:S(2)}, u32[]{:S(2)}) collective-permute-start(bf16[4,256,256]{2,1,0:T(8,128)(2,1)S(1)} %get-tuple-element.61), channel_id=1, source_target_pairs={{0,96},{1,25},{2,98},{3,27},{4,100},{5,29},{6,102},{7,31},{8,104},... | collective-permute-start | bytes 1572872 | tf_op jit(solution)/shard_map/ppermute | solution.py:41
  37.1 1.2 %shard_map.72.other_ref = bf16[16,256,256]{2,1,0:T(8,128)(2,1)S(1)} custom-call(f32[8,128]{1,0:T(8,128)S(1)} %add.9.total_ref, f32[8,128]{1,0:T(8,128)S(1)} %collective-permute-done.1.other_ref, f32[128,128]{1,0:T(8,128)S(1)} %get-tuple-element.40.power_ref, f32[128,128]{1,0:T(8,128)S(1)} %get-tuple-element.41.shrink_ref, ...), custom_call_target="tpu_custom_call" | custom-call | flops 16777216 | bytes 4194304 | tf_op jit(solution)/shard_map/pallas_call | solution.py:218
  39.3 1.1 %collective-permute-start.9 = (bf16[4,256,256]{2,1,0:T(8,128)(2,1)S(1)}, bf16[4,256,256]{2,1,0:T(8,128)(2,1)S(1)}, u32[]{:S(2)}, u32[]{:S(2)}) collective-permute-start(bf16[4,256,256]{2,1,0:T(8,128)(2,1)S(1)} %get-tuple-element.53), channel_id=1, source_target_pairs={{0,96},{1,25},{2,98},{3,27},{4,100},{5,29},{6,102},{7,31},{8,104},... | collective-permute-start | bytes 1572872 | tf_op jit(solution)/shard_map/ppermute | solution.py:41
  42.6 2.2 %collective-permute-done.14.r_b = bf16[4,256,256]{2,1,0:T(8,128)(2,1)S(1)} collective-permute-done((bf16[4,256,256]{2,1,0:T(8,128)(2,1)S(1)}, bf16[4,256,256]{2,1,0:T(8,128)(2,1)S(1)}, u32[]{:S(2)}, u32[]{:S(2)}) %collective-permute-start.14) | collective-permute-done | bytes 524320 | tf_op jit(solution)/shard_map/ppermute | solution.py:41
  44.7 3.6 %collective-permute-done.13.r_a = bf16[4,256,256]{2,1,0:T(8,128)(2,1)S(1)} collective-permute-done((bf16[4,256,256]{2,1,0:T(8,128)(2,1)S(1)}, bf16[4,256,256]{2,1,0:T(8,128)(2,1)S(1)}, u32[]{:S(2)}, u32[]{:S(2)}) %collective-permute-start.13) | collective-permute-done | bytes 524320 | tf_op jit(solution)/shard_map/ppermute | solution.py:41
  48.8 1.0 %collective-permute-start.16 = (bf16[2,256,256]{2,1,0:T(8,128)(2,1)S(1)}, bf16[2,256,256]{2,1,0:T(8,128)(2,1)S(1)}, u32[]{:S(2)}, u32[]{:S(2)}) collective-permute-start(bf16[2,256,256]{2,1,0:T(8,128)(2,1)S(1)} %get-tuple-element.64), channel_id=1, source_target_pairs={{0,8},{1,33},{2,10},{3,35},{4,12},{5,37},{6,14},{7,39},{8,0},{9,41... | collective-permute-start | bytes 786440 | tf_op jit(solution)/shard_map/ppermute | solution.py:41
  49.8 3.5 %collective-permute-start.17 = (bf16[2,256,256]{2,1,0:T(8,128)(2,1)S(1)}, bf16[2,256,256]{2,1,0:T(8,128)(2,1)S(1)}, u32[]{:S(2)}, u32[]{:S(2)}) collective-permute-start(bf16[2,256,256]{2,1,0:T(8,128)(2,1)S(1)} %get-tuple-element.65), channel_id=1, source_target_pairs={{0,16},{1,65},{2,18},{3,67},{4,20},{5,69},{6,22},{7,71},{8,24},{9,... | collective-permute-start | bytes 786440 | tf_op jit(solution)/shard_map/ppermute | solution.py:41
  53.3 4.8 %collective-permute-done.6.r_a = bf16[4,256,256]{2,1,0:T(8,128)(2,1)S(1)} collective-permute-done((bf16[4,256,256]{2,1,0:T(8,128)(2,1)S(1)}, bf16[4,256,256]{2,1,0:T(8,128)(2,1)S(1)}, u32[]{:S(2)}, u32[]{:S(2)}) %collective-permute-start.6) | collective-permute-done | bytes 524320 | tf_op jit(solution)/shard_map/ppermute | solution.py:41
  59.0 3.4 %collective-permute-start.12 = (bf16[2,256,256]{2,1,0:T(8,128)(2,1)S(1)}, bf16[2,256,256]{2,1,0:T(8,128)(2,1)S(1)}, u32[]{:S(2)}, u32[]{:S(2)}) collective-permute-start(bf16[2,256,256]{2,1,0:T(8,128)(2,1)S(1)} %get-tuple-element.57), channel_id=1, source_target_pairs={{0,24},{1,97},{2,26},{3,99},{4,28},{5,101},{6,30},{7,103},{8,16},{... | collective-permute-start | bytes 786440 | tf_op jit(solution)/shard_map/ppermute | solution.py:41
  62.5 4.0 %collective-permute-start.18 = (bf16[2,256,256]{2,1,0:T(8,128)(2,1)S(1)}, bf16[2,256,256]{2,1,0:T(8,128)(2,1)S(1)}, u32[]{:S(2)}, u32[]{:S(2)}) collective-permute-start(bf16[2,256,256]{2,1,0:T(8,128)(2,1)S(1)} %shard_map.81), channel_id=1, source_target_pairs={{0,4},{1,5},{2,6},{3,7},{4,0},{5,1},{6,2},{7,3},{8,12},{9,13},{10,... | collective-permute-start | bytes 786440 | tf_op jit(solution)/shard_map/ppermute | solution.py:41
  67.3 1.7 %collective-permute-done.12.c_ref = bf16[2,256,256]{2,1,0:T(8,128)(2,1)S(1)} collective-permute-done((bf16[2,256,256]{2,1,0:T(8,128)(2,1)S(1)}, bf16[2,256,256]{2,1,0:T(8,128)(2,1)S(1)}, u32[]{:S(2)}, u32[]{:S(2)}) %collective-permute-start.12) | collective-permute-done | bytes 262176 | tf_op jit(solution)/shard_map/ppermute | solution.py:41
  69.2 1.6 %collective-permute-done.18.got_ref = bf16[2,256,256]{2,1,0:T(8,128)(2,1)S(1)} collective-permute-done((bf16[2,256,256]{2,1,0:T(8,128)(2,1)S(1)}, bf16[2,256,256]{2,1,0:T(8,128)(2,1)S(1)}, u32[]{:S(2)}, u32[]{:S(2)}) %collective-permute-start.18) | collective-permute-done | bytes 262176 | tf_op jit(solution)/shard_map/ppermute | solution.py:41
  70.8 0.9 %shard_map.82 = f32[512,256]{1,0:T(8,128)} custom-call(f32[2,256,256]{2,1,0:T(8,128)S(1)} %shard_map.79.own_ref, bf16[2,256,256]{2,1,0:T(8,128)(2,1)S(1)} %collective-permute-done.18.got_ref), custom_call_target="tpu_custom_call" | custom-call | flops 1048576 | bytes 2097152 | tf_op jit(solution)/shard_map/pallas_call | solution.py:297
  (39 shorter events, 9.3 us)
Async XLA Ops:
  1.7 4.2 %collective-permute-start = (f32[8,128]{1,0:T(8,128)S(1)}, f32[8,128]{1,0:T(8,128)S(1)}, u32[]{:S(2)}, u32[]{:S(2)}) collective-permute-start(f32[8,128]{1,0:T(8,128)S(1)} %get-tuple-element.37), channel_id=1, source_target_pairs={{0,1},{1,0},{2,3},{3,2},{4,5},{5,4},{6,7},{7,6},{8,9},{9,8},{10,11... | collective-permute-start | bytes 12296 | tf_op jit(solution)/shard_map/ppermute | solution.py:41
  1.8 12.0 %slice-start = ((s8[8388608]{0:T(1024)(128)(4,1)}), s8[4194304]{0:T(1024)(128)(4,1)S(1)}, s32[]{:S(2)}) async-start(s8[8388608]{0:T(1024)(128)(4,1)} %bitcast.4), calls=%async_computation | async-start | bytes 8388608
  5.9 7.9 %slice-start.1 = ((s8[8388608]{0:T(1024)(128)(4,1)}), s8[4194304]{0:T(1024)(128)(4,1)S(1)}, s32[]{:S(2)}) async-start(s8[8388608]{0:T(1024)(128)(4,1)} %bitcast.4), calls=%async_computation.1 | async-start | bytes 8388608
  5.9 26.2 %collective-permute-start.8 = (bf16[4112,256]{1,0:T(8,128)(2,1)S(1)}, bf16[4112,256]{1,0:T(8,128)(2,1)S(1)}, u32[]{:S(2)}, u32[]{:S(2)}) collective-permute-start(bf16[4112,256]{1,0:T(8,128)(2,1)S(1)} %get-tuple-element.43.sent_b), channel_id=1, source_target_pairs={{0,32},{1,9},{2,34},{3,11},{4,36},{5,13},{6,38},{7,15},{8,40},{9,1... | collective-permute-start | bytes 6316040 | tf_op jit(solution)/shard_map/ppermute | solution.py:41
  7.5 29.6 %collective-permute-start.5 = (bf16[4112,256]{1,0:T(8,128)(2,1)S(1)}, bf16[4112,256]{1,0:T(8,128)(2,1)S(1)}, u32[]{:S(2)}, u32[]{:S(2)}) collective-permute-start(bf16[4112,256]{1,0:T(8,128)(2,1)S(1)} %get-tuple-element.42.sent_a), channel_id=1, source_target_pairs={{0,96},{1,25},{2,98},{3,27},{4,100},{5,29},{6,102},{7,31},{8,104},... | collective-permute-start | bytes 6316040 | tf_op jit(solution)/shard_map/ppermute | solution.py:41
  9.6 4.2 %collective-permute-start.1 = (f32[8,128]{1,0:T(8,128)S(1)}, f32[8,128]{1,0:T(8,128)S(1)}, u32[]{:S(2)}, u32[]{:S(2)}) collective-permute-start(f32[8,128]{1,0:T(8,128)S(1)} %add.9.total_ref), channel_id=1, source_target_pairs={{0,2},{1,3},{2,0},{3,1},{4,6},{5,7},{6,4},{7,5},{8,10},{9,11},{10,... | collective-permute-start | bytes 12296 | tf_op jit(solution)/shard_map/ppermute | solution.py:41
  19.8 1.6 %collective-permute-start.2 = (f32[256,256]{1,0:T(8,128)S(1)}, f32[256,256]{1,0:T(8,128)S(1)}, u32[]{:S(2)}, u32[]{:S(2)}) collective-permute-start(f32[256,256]{1,0:T(8,128)S(1)} %get-tuple-element.44), channel_id=1, source_target_pairs={{0,1},{1,0},{2,3},{3,2},{4,5},{5,4},{6,7},{7,6},{8,9},{9,8},{10,11... | collective-permute-start | bytes 786440 | tf_op jit(solution)/shard_map/ppermute | solution.py:41
  21.4 5.6 %collective-permute-start.3 = (bf16[256,256]{1,0:T(8,128)(2,1)S(1)}, bf16[256,256]{1,0:T(8,128)(2,1)S(1)}, u32[]{:S(2)}, u32[]{:S(2)}) collective-permute-start(bf16[256,256]{1,0:T(8,128)(2,1)S(1)} %add_convert_fusion.1), channel_id=1, source_target_pairs={{0,2},{1,3},{2,0},{3,1},{4,6},{5,7},{6,4},{7,5},{8,10},{9,11},{10,... | collective-permute-start | bytes 393224 | tf_op jit(solution)/shard_map/ppermute | solution.py:41
  27.1 6.4 %collective-permute-start.7 = (bf16[256,256]{1,0:T(8,128)(2,1)S(1)}, bf16[256,256]{1,0:T(8,128)(2,1)S(1)}, u32[]{:S(2)}, u32[]{:S(2)}) collective-permute-start(bf16[256,256]{1,0:T(8,128)(2,1)S(1)} %add_convert_fusion.y_own_ref), channel_id=1, source_target_pairs={{0,32},{1,9},{2,34},{3,11},{4,36},{5,13},{6,38},{7,15},{8,40},{9,1... | collective-permute-start | bytes 393224 | tf_op jit(solution)/shard_map/ppermute | solution.py:41
  27.8 10.5 %collective-permute-start.4 = (bf16[256,256]{1,0:T(8,128)(2,1)S(1)}, bf16[256,256]{1,0:T(8,128)(2,1)S(1)}, u32[]{:S(2)}, u32[]{:S(2)}) collective-permute-start(bf16[256,256]{1,0:T(8,128)(2,1)S(1)} %add_convert_fusion.y_own_ref), channel_id=1, source_target_pairs={{0,96},{1,25},{2,98},{3,27},{4,100},{5,29},{6,102},{7,31},{8,104},... | collective-permute-start | bytes 393224 | tf_op jit(solution)/shard_map/ppermute | solution.py:41
  34.2 10.5 %collective-permute-start.14 = (bf16[4,256,256]{2,1,0:T(8,128)(2,1)S(1)}, bf16[4,256,256]{2,1,0:T(8,128)(2,1)S(1)}, u32[]{:S(2)}, u32[]{:S(2)}) collective-permute-start(bf16[4,256,256]{2,1,0:T(8,128)(2,1)S(1)} %get-tuple-element.61), channel_id=1, source_target_pairs={{0,96},{1,25},{2,98},{3,27},{4,100},{5,29},{6,102},{7,31},{8,104},... | collective-permute-start | bytes 1572872 | tf_op jit(solution)/shard_map/ppermute | solution.py:41
  39.0 9.3 %collective-permute-start.13 = (bf16[4,256,256]{2,1,0:T(8,128)(2,1)S(1)}, bf16[4,256,256]{2,1,0:T(8,128)(2,1)S(1)}, u32[]{:S(2)}, u32[]{:S(2)}) collective-permute-start(bf16[4,256,256]{2,1,0:T(8,128)(2,1)S(1)} %get-tuple-element.59), channel_id=1, source_target_pairs={{0,32},{1,9},{2,34},{3,11},{4,36},{5,13},{6,38},{7,15},{8,40},{9,1... | collective-permute-start | bytes 1572872 | tf_op jit(solution)/shard_map/ppermute | solution.py:41
  39.3 13.9 %collective-permute-start.9 = (bf16[4,256,256]{2,1,0:T(8,128)(2,1)S(1)}, bf16[4,256,256]{2,1,0:T(8,128)(2,1)S(1)}, u32[]{:S(2)}, u32[]{:S(2)}) collective-permute-start(bf16[4,256,256]{2,1,0:T(8,128)(2,1)S(1)} %get-tuple-element.53), channel_id=1, source_target_pairs={{0,96},{1,25},{2,98},{3,27},{4,100},{5,29},{6,102},{7,31},{8,104},... | collective-permute-start | bytes 1572872 | tf_op jit(solution)/shard_map/ppermute | solution.py:41
  40.5 17.6 %collective-permute-start.6 = (bf16[4,256,256]{2,1,0:T(8,128)(2,1)S(1)}, bf16[4,256,256]{2,1,0:T(8,128)(2,1)S(1)}, u32[]{:S(2)}, u32[]{:S(2)}) collective-permute-start(bf16[4,256,256]{2,1,0:T(8,128)(2,1)S(1)} %get-tuple-element.49), channel_id=1, source_target_pairs={{0,32},{1,9},{2,34},{3,11},{4,36},{5,13},{6,38},{7,15},{8,40},{9,1... | collective-permute-start | bytes 1572872 | tf_op jit(solution)/shard_map/ppermute | solution.py:41
  48.5 10.5 %collective-permute-start.15 = (bf16[2,256,256]{2,1,0:T(8,128)(2,1)S(1)}, bf16[2,256,256]{2,1,0:T(8,128)(2,1)S(1)}, u32[]{:S(2)}, u32[]{:S(2)}) collective-permute-start(bf16[2,256,256]{2,1,0:T(8,128)(2,1)S(1)} %get-tuple-element.63), channel_id=1, source_target_pairs={{0,24},{1,97},{2,26},{3,99},{4,28},{5,101},{6,30},{7,103},{8,16},{... | collective-permute-start | bytes 786440 | tf_op jit(solution)/shard_map/ppermute | solution.py:41
  48.8 13.6 %collective-permute-start.16 = (bf16[2,256,256]{2,1,0:T(8,128)(2,1)S(1)}, bf16[2,256,256]{2,1,0:T(8,128)(2,1)S(1)}, u32[]{:S(2)}, u32[]{:S(2)}) collective-permute-start(bf16[2,256,256]{2,1,0:T(8,128)(2,1)S(1)} %get-tuple-element.64), channel_id=1, source_target_pairs={{0,8},{1,33},{2,10},{3,35},{4,12},{5,37},{6,14},{7,39},{8,0},{9,41... | collective-permute-start | bytes 786440 | tf_op jit(solution)/shard_map/ppermute | solution.py:41
  49.8 12.7 %collective-permute-start.17 = (bf16[2,256,256]{2,1,0:T(8,128)(2,1)S(1)}, bf16[2,256,256]{2,1,0:T(8,128)(2,1)S(1)}, u32[]{:S(2)}, u32[]{:S(2)}) collective-permute-start(bf16[2,256,256]{2,1,0:T(8,128)(2,1)S(1)} %get-tuple-element.65), channel_id=1, source_target_pairs={{0,16},{1,65},{2,18},{3,67},{4,20},{5,69},{6,22},{7,71},{8,24},{9,... | collective-permute-start | bytes 786440 | tf_op jit(solution)/shard_map/ppermute | solution.py:41
  58.2 9.0 %collective-permute-start.10 = (bf16[2,256,256]{2,1,0:T(8,128)(2,1)S(1)}, bf16[2,256,256]{2,1,0:T(8,128)(2,1)S(1)}, u32[]{:S(2)}, u32[]{:S(2)}) collective-permute-start(bf16[2,256,256]{2,1,0:T(8,128)(2,1)S(1)} %get-tuple-element.55), channel_id=1, source_target_pairs={{0,16},{1,65},{2,18},{3,67},{4,20},{5,69},{6,22},{7,71},{8,24},{9,... | collective-permute-start | bytes 786440 | tf_op jit(solution)/shard_map/ppermute | solution.py:41
  58.3 8.9 %collective-permute-start.11 = (bf16[2,256,256]{2,1,0:T(8,128)(2,1)S(1)}, bf16[2,256,256]{2,1,0:T(8,128)(2,1)S(1)}, u32[]{:S(2)}, u32[]{:S(2)}) collective-permute-start(bf16[2,256,256]{2,1,0:T(8,128)(2,1)S(1)} %get-tuple-element.56), channel_id=1, source_target_pairs={{0,8},{1,33},{2,10},{3,35},{4,12},{5,37},{6,14},{7,39},{8,0},{9,41... | collective-permute-start | bytes 786440 | tf_op jit(solution)/shard_map/ppermute | solution.py:41
  59.0 10.0 %collective-permute-start.12 = (bf16[2,256,256]{2,1,0:T(8,128)(2,1)S(1)}, bf16[2,256,256]{2,1,0:T(8,128)(2,1)S(1)}, u32[]{:S(2)}, u32[]{:S(2)}) collective-permute-start(bf16[2,256,256]{2,1,0:T(8,128)(2,1)S(1)} %get-tuple-element.57), channel_id=1, source_target_pairs={{0,24},{1,97},{2,26},{3,99},{4,28},{5,101},{6,30},{7,103},{8,16},{... | collective-permute-start | bytes 786440 | tf_op jit(solution)/shard_map/ppermute | solution.py:41
  62.5 8.3 %collective-permute-start.18 = (bf16[2,256,256]{2,1,0:T(8,128)(2,1)S(1)}, bf16[2,256,256]{2,1,0:T(8,128)(2,1)S(1)}, u32[]{:S(2)}, u32[]{:S(2)}) collective-permute-start(bf16[2,256,256]{2,1,0:T(8,128)(2,1)S(1)} %shard_map.81), channel_id=1, source_target_pairs={{0,4},{1,5},{2,6},{3,7},{4,0},{5,1},{6,2},{7,3},{8,12},{9,13},{10,... | collective-permute-start | bytes 786440 | tf_op jit(solution)/shard_map/ppermute | solution.py:41

commit v6 on v5

--- a/solution.py
+++ b/solution.py
@@ -193,7 +193,7 @@
     )(total, other, inv_row, power, shrink, *sent, kept, probes, counts)
 
 
-def other_kernel(group, total_ref, other_ref, power_ref, shrink_ref, count_ref, tile_ref, inv_ref):
+def other_kernel(group, half, total_ref, other_ref, power_ref, shrink_ref, count_ref, tile_ref, inv_ref):
     r, core = place()
     total = whole_total(total_ref, other_ref)
     rows = tile_ref.shape[1]
@@ -201,26 +201,23 @@
     marg = tail[0:1, :] + tail[1:2, :] * 64.0 + tail[2:3, :] * 4096.0
     inv_ref[...] = 1.0 / jnp.transpose(jnp.broadcast_to(marg, (128, rows)))
 
-    @pl.loop(0, 2)
-    def _(i):
-        for n, (d, e, k) in enumerate(slots(group, 0)[:8]):
-            block = block_of(r, core, group, d ^ (FAR[group] * i), e, k)
-            shrink = column_terms(shrink_ref, block)
-            scale = column_terms(power_ref, block) * total
-            s = 8 * i + n
-            base = pl.multiple_of(s * rows, rows)
-            for q in range(0, rows, 32):
-                tile_ref[s, q:q + 32, :] = tile_rows(count_ref[pl.ds(base + q, 32), :], shrink, scale, inv_ref[q:q + 32, :])
-
-
-def other_tile(group, total, other, power, shrink, received):
-    vmem = spec(pltpu.VMEM)
-    return pl.pallas_call(
-        functools.partial(other_kernel, group),
+    for n, (d, e, k) in enumerate(slots(group, 0)[8 * half:8 * half + 8]):
+        block = block_of(r, core, group, d, e, k)
+        shrink = column_terms(shrink_ref, block)
+        scale = column_terms(power_ref, block) * total
+        base = (8 * half + n) * rows
+        for q in range(0, rows, 32):
+            tile_ref[n, q:q + 32, :] = tile_rows(count_ref[base + q:base + q + 32, :], shrink, scale, inv_ref[q:q + 32, :])
+
+
+def other_tile(group, half, total, other, power, shrink, received):
+    vmem = spec(pltpu.VMEM)
+    return pl.pallas_call(
+        functools.partial(other_kernel, group, half),
         in_specs=[vmem] * 5,
         out_specs=vmem,
         scratch_shapes=[pltpu.VMEM((W, 128), F32)],
-        out_shape=jax.ShapeDtypeStruct((16, W, W), BF16),
+        out_shape=jax.ShapeDtypeStruct((8, W, W), BF16),
         compiler_params=params(4),
         cost_estimate=pl.CostEstimate(flops=1 << 24, bytes_accessed=4 << 20, transcendentals=1 << 20),
     )(total, other, power, shrink, received)
@@ -229,7 +226,7 @@
 def back_kernel(base, half, y_own_ref, y_other_ref, own_ref, other_ref, *outs):
     for n in range(8):
         out = jnp.dot(y_own_ref[...], own_ref[base + half * 8 + n], preferred_element_type=F32)
-        out = out + jnp.dot(y_other_ref[...], other_ref[half * 8 + n], preferred_element_type=F32)
+        out = out + jnp.dot(y_other_ref[...], other_ref[n], preferred_element_type=F32)
         outs[n // 4][n % 4] = out.astype(outs[0].dtype)
 
 
@@ -317,11 +314,12 @@
     y_own = (y_chip.astype(F32) + permute(y_chip, ZL_PERM).astype(F32)).astype(BF16)
     y_other = [permute(y_own, u_perm(NEAR[g])) for g in range(2)]
 
-    tiles = [other_tile(g, total, other, power, shrink, received[g]) for g in range(2)]
+    tiles = [other_tile(g, 1, total, other, power, shrink, received[g]) for g in range(2)]
     y_other, tiles = zip(*[lax.optimization_barrier((y_other[g], tiles[g])) for g in range(2)])
     sends = [back(g, 1, y_own, y_other[g], tile, tiles[g], BF16) for g in range(2)]
     r2 = [[permute(sends[g][c], u_perm(FAR[g])) for g in range(2)] for c in range(2)]
-    z = [back(g, 0, y_own, y_other[g], tile, tiles[g], F32) for g in range(2)]
+    later = [other_tile(g, 0, total, other, power, shrink, received[g]) for g in range(2)]
+    z = [back(g, 0, y_own, y_other[g], tile, later[g], F32) for g in range(2)]
     ended = []
     for c, dtype in enumerate((BF16, F32)):
         own, *out = pack([z[g][c] for g in range(2)], r2[c])

time: 71.9 us -> 71.2 us (level)
  waiting for transfers between devices: 23.6 us -> 22.7 us
    ppermute x19, waiting for transfers between devices: 23.6 us -> 22.7 us  [permute(): return lax.ppermute(a, AXES, perm)]
    pallas_call x2 -> x4, Pallas kernels: 2.34 us -> 2.26 us  [other_tile(): pl.pallas_call(functools.partial(other_kernel, group, half), in_specs=[vm...]
  transfers between devices with their start and end apart: 19 -> 19, of which waited for: 9 -> 9; matrix products, arithmetic and copies ran while one was open for 1% -> 1% of each run, Pallas kernels for 25% -> 26%
where the time goes in v6:
time: 71.2 us; the launch traced here: 70.9 us
  starting transfers between devices  26.4 us (37%)
  waiting for transfers between devices  22.7 us (32%)
  Pallas kernels  19.2 us (27%)
  other arithmetic  0.97 us (1%)
  between operations  0.85 us (1%)
  local copies, waits for them, and re-layouts  0.77 us (1%)
    ppermute x19, starting transfers between devices, permute(): return lax.ppermute(a, AXES, perm)  26.4 us
    ppermute x19, waiting for transfers between devices, permute(): return lax.ppermute(a, AXES, perm)  22.7 us
    pallas_call x2, Pallas kernels, prepare(): pl.pallas_call(functools.partial(prepare_kernel, part), in_specs=[spec(pl...  6.37 us
    pallas_call x1, Pallas kernels, forward(): pl.pallas_call(forward_kernel, in_specs=[vmem] * 9 + [spec(pl.ANY)], out_...  5.91 us
    pallas_call x4, Pallas kernels, back(): pl.pallas_call(functools.partial(back_kernel, group * 16, half), in_specs...  2.84 us
    pallas_call x4, Pallas kernels, other_tile(): pl.pallas_call(functools.partial(other_kernel, group, half), in_specs=[vm...  2.26 us
  transfers between devices with their start and end apart: 19, of which 9 were waited for; matrix products, arithmetic and copies ran while one was open for 1% of the time, Pallas kernels for 26%

profile of v6, /device:TPU:24, one launch (start us, length us, event | category | flops | bytes accessed | tf_op | source)
XLA Modules:
  0.0 70.9 jit_solution(13022790313303687744)
XLA Ops:
  0.6 0.9 %add_bitcast_fusion.all_ref = s32[258,128]{1,0:T(8,128)S(1)} fusion(s32[256]{0:T(256)} %param.6, s32[16384]{0:T(1024)} %param.8, s32[16384]{0:T(1024)} %param.7), kind=kLoop, calls=%fused_computation.2 | loop fusion | flops 66048 | bytes 264192 | tf_op jit(solution)/shard_map/reshape | solution.py:87
  1.8 4.1 %shard_map.69 = (bf16[4112,256]{1,0:T(8,128)(2,1)S(1)}, bf16[4112,256]{1,0:T(8,128)(2,1)S(1)}) custom-call(bf16[16,256]{1,0:T(8,128)(2,1)S(1)} %get-tuple-element.34.refs_0_, s32[256,16384]{1,0:T(8,128)} %counts_ref.1), custom_call_target="tpu_custom_call" | custom-call | flops 4194304 | bytes 12582912 | tf_op jit(solution)/shard_map/pallas_call | solution.py:118
  5.9 1.6 %collective-permute-start.8 = (bf16[4112,256]{1,0:T(8,128)(2,1)S(1)}, bf16[4112,256]{1,0:T(8,128)(2,1)S(1)}, u32[]{:S(2)}, u32[]{:S(2)}) collective-permute-start(bf16[4112,256]{1,0:T(8,128)(2,1)S(1)} %get-tuple-element.43.sent_b), channel_id=1, source_target_pairs={{0,32},{1,9},{2,34},{3,11},{4,36},{5,13},{6,38},{7,15},{8,40},{9,1... | collective-permute-start | bytes 6316040 | tf_op jit(solution)/shard_map/ppermute | solution.py:41
  7.5 2.1 %collective-permute-start.5 = (bf16[4112,256]{1,0:T(8,128)(2,1)S(1)}, bf16[4112,256]{1,0:T(8,128)(2,1)S(1)}, u32[]{:S(2)}, u32[]{:S(2)}) collective-permute-start(bf16[4112,256]{1,0:T(8,128)(2,1)S(1)} %get-tuple-element.42.sent_a), channel_id=1, source_target_pairs={{0,96},{1,25},{2,98},{3,27},{4,100},{5,29},{6,102},{7,31},{8,104},... | collective-permute-start | bytes 6316040 | tf_op jit(solution)/shard_map/ppermute | solution.py:41
  9.6 1.9 %collective-permute-start.1 = (f32[8,128]{1,0:T(8,128)S(1)}, f32[8,128]{1,0:T(8,128)S(1)}, u32[]{:S(2)}, u32[]{:S(2)}) collective-permute-start(f32[8,128]{1,0:T(8,128)S(1)} %add.9.total_ref), channel_id=1, source_target_pairs={{0,2},{1,3},{2,0},{3,1},{4,6},{5,7},{6,4},{7,5},{8,10},{9,11},{10,... | collective-permute-start | bytes 12296 | tf_op jit(solution)/shard_map/ppermute | solution.py:41
  11.5 2.3 %shard_map.70.kept_a = bf16[4096,256]{1,0:T(8,128)(2,1)S(1)} custom-call(s32[256,16384]{1,0:T(8,128)} %counts_ref.1), custom_call_target="tpu_custom_call" | custom-call | flops 4194304 | bytes 6291456 | tf_op jit(solution)/shard_map/pallas_call | solution.py:118
  13.9 5.9 %shard_map.71 = (bf16[32,256,256]{2,1,0:T(8,128)(2,1)S(1)}, f32[256,256]{1,0:T(8,128)S(1)}) custom-call(f32[8,128]{1,0:T(8,128)S(1)} %add.9.total_ref, f32[8,128]{1,0:T(8,128)S(1)} %collective-permute-done.1.other_ref, f32[256,128]{1,0:T(8,128)S(1)} %get-tuple-element.39.inv_ref, f32[128,128]{1,0:T(8,128)S(1)} %get-tuple-element.40.power_ref, ...), custom_call_target="tpu_custom_call" | custom-call | flops 2147483648 | bytes 29360128 | tf_op jit(solution)/shard_map/pallas_call | solution.py:180
  19.9 1.5 %collective-permute-done.2 = f32[256,256]{1,0:T(8,128)S(1)} collective-permute-done((f32[256,256]{1,0:T(8,128)S(1)}, f32[256,256]{1,0:T(8,128)S(1)}, u32[]{:S(2)}, u32[]{:S(2)}) %collective-permute-start.2) | collective-permute-done | bytes 262176 | tf_op jit(solution)/shard_map/ppermute | solution.py:41
  21.4 1.3 %collective-permute-start.3 = (bf16[256,256]{1,0:T(8,128)(2,1)S(1)}, bf16[256,256]{1,0:T(8,128)(2,1)S(1)}, u32[]{:S(2)}, u32[]{:S(2)}) collective-permute-start(bf16[256,256]{1,0:T(8,128)(2,1)S(1)} %add_convert_fusion.1), channel_id=1, source_target_pairs={{0,2},{1,3},{2,0},{3,1},{4,6},{5,7},{6,4},{7,5},{8,10},{9,11},{10,... | collective-permute-start | bytes 393224 | tf_op jit(solution)/shard_map/ppermute | solution.py:41
  22.8 4.3 %collective-permute-done.3 = bf16[256,256]{1,0:T(8,128)(2,1)S(1)} collective-permute-done((bf16[256,256]{1,0:T(8,128)(2,1)S(1)}, bf16[256,256]{1,0:T(8,128)(2,1)S(1)}, u32[]{:S(2)}, u32[]{:S(2)}) %collective-permute-start.3) | collective-permute-done | bytes 131104 | tf_op jit(solution)/shard_map/ppermute | solution.py:41
  28.5 3.6 %collective-permute-done.8.count_ref = bf16[4112,256]{1,0:T(8,128)(2,1)S(1)} collective-permute-done((bf16[4112,256]{1,0:T(8,128)(2,1)S(1)}, bf16[4112,256]{1,0:T(8,128)(2,1)S(1)}, u32[]{:S(2)}, u32[]{:S(2)}) %collective-permute-start.8) | collective-permute-done | bytes 2105376 | tf_op jit(solution)/shard_map/ppermute | solution.py:41
  34.2 2.8 %collective-permute-start.14 = (bf16[4,256,256]{2,1,0:T(8,128)(2,1)S(1)}, bf16[4,256,256]{2,1,0:T(8,128)(2,1)S(1)}, u32[]{:S(2)}, u32[]{:S(2)}) collective-permute-start(bf16[4,256,256]{2,1,0:T(8,128)(2,1)S(1)} %get-tuple-element.61), channel_id=1, source_target_pairs={{0,96},{1,25},{2,98},{3,27},{4,100},{5,29},{6,102},{7,31},{8,104},... | collective-permute-start | bytes 1572872 | tf_op jit(solution)/shard_map/ppermute | solution.py:41
  38.7 1.1 %collective-permute-start.9 = (bf16[4,256,256]{2,1,0:T(8,128)(2,1)S(1)}, bf16[4,256,256]{2,1,0:T(8,128)(2,1)S(1)}, u32[]{:S(2)}, u32[]{:S(2)}) collective-permute-start(bf16[4,256,256]{2,1,0:T(8,128)(2,1)S(1)} %get-tuple-element.53), channel_id=1, source_target_pairs={{0,96},{1,25},{2,98},{3,27},{4,100},{5,29},{6,102},{7,31},{8,104},... | collective-permute-start | bytes 1572872 | tf_op jit(solution)/shard_map/ppermute | solution.py:41
  43.1 1.6 %collective-permute-done.14.r_b = bf16[4,256,256]{2,1,0:T(8,128)(2,1)S(1)} collective-permute-done((bf16[4,256,256]{2,1,0:T(8,128)(2,1)S(1)}, bf16[4,256,256]{2,1,0:T(8,128)(2,1)S(1)}, u32[]{:S(2)}, u32[]{:S(2)}) %collective-permute-start.14) | collective-permute-done | bytes 524320 | tf_op jit(solution)/shard_map/ppermute | solution.py:41
  44.7 2.9 %collective-permute-done.13.r_a = bf16[4,256,256]{2,1,0:T(8,128)(2,1)S(1)} collective-permute-done((bf16[4,256,256]{2,1,0:T(8,128)(2,1)S(1)}, bf16[4,256,256]{2,1,0:T(8,128)(2,1)S(1)}, u32[]{:S(2)}, u32[]{:S(2)}) %collective-permute-start.13) | collective-permute-done | bytes 524320 | tf_op jit(solution)/shard_map/ppermute | solution.py:41
  48.2 1.0 %collective-permute-start.16 = (bf16[2,256,256]{2,1,0:T(8,128)(2,1)S(1)}, bf16[2,256,256]{2,1,0:T(8,128)(2,1)S(1)}, u32[]{:S(2)}, u32[]{:S(2)}) collective-permute-start(bf16[2,256,256]{2,1,0:T(8,128)(2,1)S(1)} %get-tuple-element.64), channel_id=1, source_target_pairs={{0,8},{1,33},{2,10},{3,35},{4,12},{5,37},{6,14},{7,39},{8,0},{9,41... | collective-permute-start | bytes 786440 | tf_op jit(solution)/shard_map/ppermute | solution.py:41
  49.1 3.5 %collective-permute-start.17 = (bf16[2,256,256]{2,1,0:T(8,128)(2,1)S(1)}, bf16[2,256,256]{2,1,0:T(8,128)(2,1)S(1)}, u32[]{:S(2)}, u32[]{:S(2)}) collective-permute-start(bf16[2,256,256]{2,1,0:T(8,128)(2,1)S(1)} %get-tuple-element.65), channel_id=1, source_target_pairs={{0,16},{1,65},{2,18},{3,67},{4,20},{5,69},{6,22},{7,71},{8,24},{9,... | collective-permute-start | bytes 786440 | tf_op jit(solution)/shard_map/ppermute | solution.py:41
  52.6 4.5 %collective-permute-done.6.r_a = bf16[4,256,256]{2,1,0:T(8,128)(2,1)S(1)} collective-permute-done((bf16[4,256,256]{2,1,0:T(8,128)(2,1)S(1)}, bf16[4,256,256]{2,1,0:T(8,128)(2,1)S(1)}, u32[]{:S(2)}, u32[]{:S(2)}) %collective-permute-start.6) | collective-permute-done | bytes 524320 | tf_op jit(solution)/shard_map/ppermute | solution.py:41
  57.5 0.9 %collective-permute-start.11 = (bf16[2,256,256]{2,1,0:T(8,128)(2,1)S(1)}, bf16[2,256,256]{2,1,0:T(8,128)(2,1)S(1)}, u32[]{:S(2)}, u32[]{:S(2)}) collective-permute-start(bf16[2,256,256]{2,1,0:T(8,128)(2,1)S(1)} %get-tuple-element.56), channel_id=1, source_target_pairs={{0,8},{1,33},{2,10},{3,35},{4,12},{5,37},{6,14},{7,39},{8,0},{9,41... | collective-permute-start | bytes 786440 | tf_op jit(solution)/shard_map/ppermute | solution.py:41
  58.4 3.1 %collective-permute-start.12 = (bf16[2,256,256]{2,1,0:T(8,128)(2,1)S(1)}, bf16[2,256,256]{2,1,0:T(8,128)(2,1)S(1)}, u32[]{:S(2)}, u32[]{:S(2)}) collective-permute-start(bf16[2,256,256]{2,1,0:T(8,128)(2,1)S(1)} %get-tuple-element.57), channel_id=1, source_target_pairs={{0,24},{1,97},{2,26},{3,99},{4,28},{5,101},{6,30},{7,103},{8,16},{... | collective-permute-start | bytes 786440 | tf_op jit(solution)/shard_map/ppermute | solution.py:41
  61.7 4.0 %collective-permute-start.18 = (bf16[2,256,256]{2,1,0:T(8,128)(2,1)S(1)}, bf16[2,256,256]{2,1,0:T(8,128)(2,1)S(1)}, u32[]{:S(2)}, u32[]{:S(2)}) collective-permute-start(bf16[2,256,256]{2,1,0:T(8,128)(2,1)S(1)} %shard_map.83), channel_id=1, source_target_pairs={{0,4},{1,5},{2,6},{3,7},{4,0},{5,1},{6,2},{7,3},{8,12},{9,13},{10,... | collective-permute-start | bytes 786440 | tf_op jit(solution)/shard_map/ppermute | solution.py:41
  66.4 1.7 %collective-permute-done.12.c_ref = bf16[2,256,256]{2,1,0:T(8,128)(2,1)S(1)} collective-permute-done((bf16[2,256,256]{2,1,0:T(8,128)(2,1)S(1)}, bf16[2,256,256]{2,1,0:T(8,128)(2,1)S(1)}, u32[]{:S(2)}, u32[]{:S(2)}) %collective-permute-start.12) | collective-permute-done | bytes 262176 | tf_op jit(solution)/shard_map/ppermute | solution.py:41
  68.3 1.6 %collective-permute-done.18.got_ref = bf16[2,256,256]{2,1,0:T(8,128)(2,1)S(1)} collective-permute-done((bf16[2,256,256]{2,1,0:T(8,128)(2,1)S(1)}, bf16[2,256,256]{2,1,0:T(8,128)(2,1)S(1)}, u32[]{:S(2)}, u32[]{:S(2)}) %collective-permute-start.18) | collective-permute-done | bytes 262176 | tf_op jit(solution)/shard_map/ppermute | solution.py:41
  70.0 0.9 %shard_map.84 = f32[512,256]{1,0:T(8,128)} custom-call(f32[2,256,256]{2,1,0:T(8,128)S(1)} %shard_map.81.own_ref, bf16[2,256,256]{2,1,0:T(8,128)(2,1)S(1)} %collective-permute-done.18.got_ref), custom_call_target="tpu_custom_call" | custom-call | flops 1048576 | bytes 2097152 | tf_op jit(solution)/shard_map/pallas_call | solution.py:294
  (41 shorter events, 10.7 us)
Async XLA Ops:
  1.7 4.2 %collective-permute-start = (f32[8,128]{1,0:T(8,128)S(1)}, f32[8,128]{1,0:T(8,128)S(1)}, u32[]{:S(2)}, u32[]{:S(2)}) collective-permute-start(f32[8,128]{1,0:T(8,128)S(1)} %get-tuple-element.37), channel_id=1, source_target_pairs={{0,1},{1,0},{2,3},{3,2},{4,5},{5,4},{6,7},{7,6},{8,9},{9,8},{10,11... | collective-permute-start | bytes 12296 | tf_op jit(solution)/shard_map/ppermute | solution.py:41
  1.8 12.0 %slice-start = ((s8[8388608]{0:T(1024)(128)(4,1)}), s8[4194304]{0:T(1024)(128)(4,1)S(1)}, s32[]{:S(2)}) async-start(s8[8388608]{0:T(1024)(128)(4,1)} %bitcast.4), calls=%async_computation | async-start | bytes 8388608
  5.9 7.9 %slice-start.1 = ((s8[8388608]{0:T(1024)(128)(4,1)}), s8[4194304]{0:T(1024)(128)(4,1)S(1)}, s32[]{:S(2)}) async-start(s8[8388608]{0:T(1024)(128)(4,1)} %bitcast.4), calls=%async_computation.1 | async-start | bytes 8388608
  5.9 26.2 %collective-permute-start.8 = (bf16[4112,256]{1,0:T(8,128)(2,1)S(1)}, bf16[4112,256]{1,0:T(8,128)(2,1)S(1)}, u32[]{:S(2)}, u32[]{:S(2)}) collective-permute-start(bf16[4112,256]{1,0:T(8,128)(2,1)S(1)} %get-tuple-element.43.sent_b), channel_id=1, source_target_pairs={{0,32},{1,9},{2,34},{3,11},{4,36},{5,13},{6,38},{7,15},{8,40},{9,1... | collective-permute-start | bytes 6316040 | tf_op jit(solution)/shard_map/ppermute | solution.py:41
  7.5 29.6 %collective-permute-start.5 = (bf16[4112,256]{1,0:T(8,128)(2,1)S(1)}, bf16[4112,256]{1,0:T(8,128)(2,1)S(1)}, u32[]{:S(2)}, u32[]{:S(2)}) collective-permute-start(bf16[4112,256]{1,0:T(8,128)(2,1)S(1)} %get-tuple-element.42.sent_a), channel_id=1, source_target_pairs={{0,96},{1,25},{2,98},{3,27},{4,100},{5,29},{6,102},{7,31},{8,104},... | collective-permute-start | bytes 6316040 | tf_op jit(solution)/shard_map/ppermute | solution.py:41
  9.6 4.2 %collective-permute-start.1 = (f32[8,128]{1,0:T(8,128)S(1)}, f32[8,128]{1,0:T(8,128)S(1)}, u32[]{:S(2)}, u32[]{:S(2)}) collective-permute-start(f32[8,128]{1,0:T(8,128)S(1)} %add.9.total_ref), channel_id=1, source_target_pairs={{0,2},{1,3},{2,0},{3,1},{4,6},{5,7},{6,4},{7,5},{8,10},{9,11},{10,... | collective-permute-start | bytes 12296 | tf_op jit(solution)/shard_map/ppermute | solution.py:41
  19.8 1.6 %collective-permute-start.2 = (f32[256,256]{1,0:T(8,128)S(1)}, f32[256,256]{1,0:T(8,128)S(1)}, u32[]{:S(2)}, u32[]{:S(2)}) collective-permute-start(f32[256,256]{1,0:T(8,128)S(1)} %get-tuple-element.44), channel_id=1, source_target_pairs={{0,1},{1,0},{2,3},{3,2},{4,5},{5,4},{6,7},{7,6},{8,9},{9,8},{10,11... | collective-permute-start | bytes 786440 | tf_op jit(solution)/shard_map/ppermute | solution.py:41
  21.4 5.6 %collective-permute-start.3 = (bf16[256,256]{1,0:T(8,128)(2,1)S(1)}, bf16[256,256]{1,0:T(8,128)(2,1)S(1)}, u32[]{:S(2)}, u32[]{:S(2)}) collective-permute-start(bf16[256,256]{1,0:T(8,128)(2,1)S(1)} %add_convert_fusion.1), channel_id=1, source_target_pairs={{0,2},{1,3},{2,0},{3,1},{4,6},{5,7},{6,4},{7,5},{8,10},{9,11},{10,... | collective-permute-start | bytes 393224 | tf_op jit(solution)/shard_map/ppermute | solution.py:41
  27.1 6.4 %collective-permute-start.7 = (bf16[256,256]{1,0:T(8,128)(2,1)S(1)}, bf16[256,256]{1,0:T(8,128)(2,1)S(1)}, u32[]{:S(2)}, u32[]{:S(2)}) collective-permute-start(bf16[256,256]{1,0:T(8,128)(2,1)S(1)} %add_convert_fusion.y_own_ref), channel_id=1, source_target_pairs={{0,32},{1,9},{2,34},{3,11},{4,36},{5,13},{6,38},{7,15},{8,40},{9,1... | collective-permute-start | bytes 393224 | tf_op jit(solution)/shard_map/ppermute | solution.py:41
  27.8 9.9 %collective-permute-start.4 = (bf16[256,256]{1,0:T(8,128)(2,1)S(1)}, bf16[256,256]{1,0:T(8,128)(2,1)S(1)}, u32[]{:S(2)}, u32[]{:S(2)}) collective-permute-start(bf16[256,256]{1,0:T(8,128)(2,1)S(1)} %add_convert_fusion.y_own_ref), channel_id=1, source_target_pairs={{0,96},{1,25},{2,98},{3,27},{4,100},{5,29},{6,102},{7,31},{8,104},... | collective-permute-start | bytes 393224 | tf_op jit(solution)/shard_map/ppermute | solution.py:41
  34.2 10.5 %collective-permute-start.14 = (bf16[4,256,256]{2,1,0:T(8,128)(2,1)S(1)}, bf16[4,256,256]{2,1,0:T(8,128)(2,1)S(1)}, u32[]{:S(2)}, u32[]{:S(2)}) collective-permute-start(bf16[4,256,256]{2,1,0:T(8,128)(2,1)S(1)} %get-tuple-element.61), channel_id=1, source_target_pairs={{0,96},{1,25},{2,98},{3,27},{4,100},{5,29},{6,102},{7,31},{8,104},... | collective-permute-start | bytes 1572872 | tf_op jit(solution)/shard_map/ppermute | solution.py:41
  38.4 9.3 %collective-permute-start.13 = (bf16[4,256,256]{2,1,0:T(8,128)(2,1)S(1)}, bf16[4,256,256]{2,1,0:T(8,128)(2,1)S(1)}, u32[]{:S(2)}, u32[]{:S(2)}) collective-permute-start(bf16[4,256,256]{2,1,0:T(8,128)(2,1)S(1)} %get-tuple-element.59), channel_id=1, source_target_pairs={{0,32},{1,9},{2,34},{3,11},{4,36},{5,13},{6,38},{7,15},{8,40},{9,1... | collective-permute-start | bytes 1572872 | tf_op jit(solution)/shard_map/ppermute | solution.py:41
  38.7 13.9 %collective-permute-start.9 = (bf16[4,256,256]{2,1,0:T(8,128)(2,1)S(1)}, bf16[4,256,256]{2,1,0:T(8,128)(2,1)S(1)}, u32[]{:S(2)}, u32[]{:S(2)}) collective-permute-start(bf16[4,256,256]{2,1,0:T(8,128)(2,1)S(1)} %get-tuple-element.53), channel_id=1, source_target_pairs={{0,96},{1,25},{2,98},{3,27},{4,100},{5,29},{6,102},{7,31},{8,104},... | collective-permute-start | bytes 1572872 | tf_op jit(solution)/shard_map/ppermute | solution.py:41
  39.8 17.3 %collective-permute-start.6 = (bf16[4,256,256]{2,1,0:T(8,128)(2,1)S(1)}, bf16[4,256,256]{2,1,0:T(8,128)(2,1)S(1)}, u32[]{:S(2)}, u32[]{:S(2)}) collective-permute-start(bf16[4,256,256]{2,1,0:T(8,128)(2,1)S(1)} %get-tuple-element.49), channel_id=1, source_target_pairs={{0,32},{1,9},{2,34},{3,11},{4,36},{5,13},{6,38},{7,15},{8,40},{9,1... | collective-permute-start | bytes 1572872 | tf_op jit(solution)/shard_map/ppermute | solution.py:41
  47.8 10.6 %collective-permute-start.15 = (bf16[2,256,256]{2,1,0:T(8,128)(2,1)S(1)}, bf16[2,256,256]{2,1,0:T(8,128)(2,1)S(1)}, u32[]{:S(2)}, u32[]{:S(2)}) collective-permute-start(bf16[2,256,256]{2,1,0:T(8,128)(2,1)S(1)} %get-tuple-element.63), channel_id=1, source_target_pairs={{0,24},{1,97},{2,26},{3,99},{4,28},{5,101},{6,30},{7,103},{8,16},{... | collective-permute-start | bytes 786440 | tf_op jit(solution)/shard_map/ppermute | solution.py:41
  48.2 13.4 %collective-permute-start.16 = (bf16[2,256,256]{2,1,0:T(8,128)(2,1)S(1)}, bf16[2,256,256]{2,1,0:T(8,128)(2,1)S(1)}, u32[]{:S(2)}, u32[]{:S(2)}) collective-permute-start(bf16[2,256,256]{2,1,0:T(8,128)(2,1)S(1)} %get-tuple-element.64), channel_id=1, source_target_pairs={{0,8},{1,33},{2,10},{3,35},{4,12},{5,37},{6,14},{7,39},{8,0},{9,41... | collective-permute-start | bytes 786440 | tf_op jit(solution)/shard_map/ppermute | solution.py:41
  49.1 12.4 %collective-permute-start.17 = (bf16[2,256,256]{2,1,0:T(8,128)(2,1)S(1)}, bf16[2,256,256]{2,1,0:T(8,128)(2,1)S(1)}, u32[]{:S(2)}, u32[]{:S(2)}) collective-permute-start(bf16[2,256,256]{2,1,0:T(8,128)(2,1)S(1)} %get-tuple-element.65), channel_id=1, source_target_pairs={{0,16},{1,65},{2,18},{3,67},{4,20},{5,69},{6,22},{7,71},{8,24},{9,... | collective-permute-start | bytes 786440 | tf_op jit(solution)/shard_map/ppermute | solution.py:41
  57.4 9.0 %collective-permute-start.10 = (bf16[2,256,256]{2,1,0:T(8,128)(2,1)S(1)}, bf16[2,256,256]{2,1,0:T(8,128)(2,1)S(1)}, u32[]{:S(2)}, u32[]{:S(2)}) collective-permute-start(bf16[2,256,256]{2,1,0:T(8,128)(2,1)S(1)} %get-tuple-element.55), channel_id=1, source_target_pairs={{0,16},{1,65},{2,18},{3,67},{4,20},{5,69},{6,22},{7,71},{8,24},{9,... | collective-permute-start | bytes 786440 | tf_op jit(solution)/shard_map/ppermute | solution.py:41
  57.5 8.9 %collective-permute-start.11 = (bf16[2,256,256]{2,1,0:T(8,128)(2,1)S(1)}, bf16[2,256,256]{2,1,0:T(8,128)(2,1)S(1)}, u32[]{:S(2)}, u32[]{:S(2)}) collective-permute-start(bf16[2,256,256]{2,1,0:T(8,128)(2,1)S(1)} %get-tuple-element.56), channel_id=1, source_target_pairs={{0,8},{1,33},{2,10},{3,35},{4,12},{5,37},{6,14},{7,39},{8,0},{9,41... | collective-permute-start | bytes 786440 | tf_op jit(solution)/shard_map/ppermute | solution.py:41
  58.4 9.7 %collective-permute-start.12 = (bf16[2,256,256]{2,1,0:T(8,128)(2,1)S(1)}, bf16[2,256,256]{2,1,0:T(8,128)(2,1)S(1)}, u32[]{:S(2)}, u32[]{:S(2)}) collective-permute-start(bf16[2,256,256]{2,1,0:T(8,128)(2,1)S(1)} %get-tuple-element.57), channel_id=1, source_target_pairs={{0,24},{1,97},{2,26},{3,99},{4,28},{5,101},{6,30},{7,103},{8,16},{... | collective-permute-start | bytes 786440 | tf_op jit(solution)/shard_map/ppermute | solution.py:41
  61.7 8.3 %collective-permute-start.18 = (bf16[2,256,256]{2,1,0:T(8,128)(2,1)S(1)}, bf16[2,256,256]{2,1,0:T(8,128)(2,1)S(1)}, u32[]{:S(2)}, u32[]{:S(2)}) collective-permute-start(bf16[2,256,256]{2,1,0:T(8,128)(2,1)S(1)} %shard_map.83), channel_id=1, source_target_pairs={{0,4},{1,5},{2,6},{3,7},{4,0},{5,1},{6,2},{7,3},{8,12},{9,13},{10,... | collective-permute-start | bytes 786440 | tf_op jit(solution)/shard_map/ppermute | solution.py:41
